TPU v7x, 32 devices: a whole 2x2x4 slice. The times are simulated.
32 devices in a mesh: member: 2 (over x), horiz: 4 (over y, core), vert: 4 (over z).
Axes of the slice: x: 2, y: 2, z: 4, core: 2. Of those that a mesh axis runs over, the one named last changes fastest.
Arguments:
- velocity: float32 [6, 64, 288, 128], P('member', 'horiz', 'vert'), parts along dimension 0, may hold values from -6 to 6
- stress: float32 [12, 64, 288, 128], P('member', 'horiz', 'vert'), parts along dimension 0, may hold values from -6 to 6
- material_index: int32 [288], P('vert'), may hold values from 0 to 7
- material_table: float32 [8, 4], replicated, may hold values from 0.5 to 1.5
- split_level: int32 [1], replicated, may hold values from 72 to 143
- source_x: int32 [16], replicated, may hold values from 0 to 63
- source_z: int32 [16], replicated, may hold values from 0 to 287
- source_y: int32 [16], replicated, may hold values from 0 to 127
- amplitude: float32 [32], P('member'), parts along dimension 0, may hold values from 1 to 10
Outputs:
- velocity_out: float32 [6, 64, 288, 128], P('member', 'horiz', 'vert'), parts along dimension 0
- stress_out: float32 [12, 64, 288, 128], P('member', 'horiz', 'vert'), parts along dimension 0
There are 2 independent parts, one for each index of `member`. A program takes and returns all parts, laid end to end along the dimension named above; an argument that names none is the same for every part. Nothing has to cross between parts.
All inputs are finite; a program needn't handle non-finite values.
Results may differ from a plain program's by a relative error of at most 0.000082.
Values sent between devices are 32-bit elements; how exact they have to be, the bound alone decides.
No kernel may reach another device: no remote copies, remote signals or barrier semaphores. Data moves between devices by JAX's collectives and lax.ppermute only.
A program may use at most 64 MiB of HBM per device.

v0:
```python
import jax
import jax.numpy as jnp
from jax import lax
from jax.sharding import PartitionSpec as P

courant = 0.2
wavelet = (1.0, -0.5)
pair_table = ((0, 3, 4), (3, 1, 5), (4, 5, 2))


def from_behind(block, axis, distance):
    devices = range(lax.axis_size(axis))
    route = [(i - distance, i) for i in devices if i - distance in devices]
    return lax.ppermute(block, axis, route)


def zero_rim(field, axis):
    return jnp.zeros_like(lax.slice_in_dim(field, 0, 1, axis=axis))


def backward(field, axis, edge):
    if edge is None:
        edge = zero_rim(field, axis)
    count = field.shape[axis]
    before = jnp.concatenate([edge, lax.slice_in_dim(field, 0, count - 1, axis=axis)], axis)
    return field - before


def forward(field, axis, edge):
    if edge is None:
        edge = zero_rim(field, axis)
    count = field.shape[axis]
    after = jnp.concatenate([lax.slice_in_dim(field, 1, count, axis=axis), edge], axis)
    return after - field


def velocity_update(speeds, forces, coeff, chooser):
    result = []
    for k in range(3):
        total = backward(forces[pair_table[k][0]], 0, chooser(k, 0))
        total = total + backward(forces[pair_table[k][1]], 1, chooser(k, 1))
        total = total + backward(forces[pair_table[k][2]], 2, chooser(k, 2))
        result.append((1.0 - courant * coeff[3]) * speeds[k] + courant * coeff[0] * total)
    return result


def stress_update(speeds, forces, coeff, chooser, source, wave):
    grads = [[forward(speeds[i], j, chooser(i, j)) for j in range(3)] for i in range(3)]
    spread = grads[0][0] + grads[1][1] + grads[2][2]
    result = []
    for c in range(3):
        result.append(
            forces[c]
            + courant * (coeff[1] * spread + 2.0 * coeff[2] * grads[c][c])
            + courant * wave * source
        )
    for i, j in ((0, 1), (0, 2), (1, 2)):
        result.append(forces[pair_table[i][j]] + courant * coeff[2] * (grads[i][j] + grads[j][i]))
    return result


def edge_chooser(x_plane, z_plane):

    def chooser(k, axis):
        if axis == 0:
            return x_plane[k][None]
        if axis == 1:
            return z_plane[k][:, None]
        return None

    return chooser


def point_field(
    amplitude, source_x, source_z, source_y, start_x, count_x, start_z, count_z, count_y
):
    onehot_x = (
        source_x[:, None] == start_x + jnp.arange(count_x, dtype=jnp.int32)[None, :]
    ).astype(jnp.float32)
    onehot_z = (
        source_z[:, None] == start_z + jnp.arange(count_z, dtype=jnp.int32)[None, :]
    ).astype(jnp.float32)
    onehot_y = (source_y[:, None] == jnp.arange(count_y, dtype=jnp.int32)[None, :]).astype(
        jnp.float32
    )
    return jnp.einsum(
        "s,sx,sz,sy->xzy", amplitude, onehot_x, onehot_z, onehot_y, precision=lax.Precision.HIGHEST
    )


def local(
    velocity,
    stress,
    material_index,
    material_table,
    split_level,
    source_x,
    source_z,
    source_y,
    amplitude,
):
    cells_x, cells_z, cells_y = (velocity.shape[1], velocity.shape[2], velocity.shape[3])
    offset_x = lax.axis_index("horiz") * cells_x
    offset_z = lax.axis_index("vert") * cells_z
    kinds = material_table.shape[0]
    picks = (material_index[:, None] == jnp.arange(kinds, dtype=jnp.int32)[None, :]).astype(
        jnp.float32
    )
    table = jnp.dot(picks, material_table, precision=lax.Precision.HIGHEST)
    levels = offset_z + jnp.arange(cells_z, dtype=jnp.int32)
    solid = (levels >= split_level[0]).astype(jnp.float32)
    coeffs = jnp.stack([table[:, 0], table[:, 1], table[:, 2] * solid, table[:, 3]])
    coeff = [coeffs[c][None, :, None] for c in range(4)]
    source = point_field(
        amplitude, source_x, source_z, source_y, offset_x, cells_x, offset_z, cells_z, cells_y
    )
    speeds = [velocity[k] for k in range(3)]
    forces = [stress[c] for c in range(6)]
    for step in range(2):
        left_plane = from_behind(
            jnp.stack([forces[0][-1], forces[3][-1], forces[4][-1]]), "horiz", 1
        )
        lower_plane = from_behind(
            jnp.stack([forces[3][:, -1], forces[1][:, -1], forces[5][:, -1]]), "vert", 1
        )
        speeds = velocity_update(speeds, forces, coeff, edge_chooser(left_plane, lower_plane))
        stacked = jnp.stack(speeds)
        right_plane = from_behind(stacked[:, 0], "horiz", -1)
        upper_plane = from_behind(stacked[:, :, 0], "vert", -1)
        forces = stress_update(
            speeds, forces, coeff, edge_chooser(right_plane, upper_plane), source, wavelet[step]
        )
    return (jnp.stack(speeds), jnp.stack(forces))


def solution(mesh):
    return jax.shard_map(
        local,
        mesh=mesh,
        in_specs=(
            P("member", "horiz", "vert", None),
            P("member", "horiz", "vert", None),
            P("vert"),
            P(),
            P(),
            P(),
            P(),
            P(),
            P("member"),
        ),
        out_specs=(P("member", "horiz", "vert", None), P("member", "horiz", "vert", None)),
        check_vma=False,
    )
```

profile of v0, /device:TPU:9, one launch (start us, length us, event | category | flops | bytes accessed | tf_op | source)
XLA Modules:
  0.0 74.7 jit_solution(17161098606194053571)
XLA Ops:
  0.7 3.4 %fusion.74 = (f32[1,16,72,128]{3,2,1,0:T(8,128)}, f32[1,16,72,128]{3,2,1,0:T(8,128)S(1)}, f32[16,72,128]{2,1,0:T(8,128)}, f32[16,72,128]{2,1,0:T(8,128)S(1)}, f3...) fusion(f32[6,16,72,128]{3,2,1,0:T(8,128)} %param.10), kind=kLoop, calls=%fused_computation.171 | loop fusion | bytes 7077888 | tf_op jit(solution)/shard_map/slice | solution.py:118
  5.0 0.9 %copy.313 = f32[1,16,72,128]{3,1,2,0:T(8,128)} copy(f32[1,16,72,128]{3,2,1,0:T(8,128)S(1)} %get-tuple-element.21) | data formatting | bytes 1179648
  7.3 3.2 %collective-permute-start.1 = (f32[3,16,128]{2,1,0:T(8,128)}, f32[3,16,128]{2,1,0:T(8,128)}, u32[]{:S(2)}, u32[]{:S(2)}) collective-permute-start(f32[3,16,128]{2,1,0:T(8,128)} %pad_maximum_fusion.6), channel_id=1, source_target_pairs={{0,1},{1,2},{2,3},{4,5},{5,6},{6,7},{8,9},{9,10},{10,11},{12,13},{... | collective-permute-start | bytes 73736 | tf_op jit(solution)/shard_map/ppermute | solution.py:14
  11.3 4.0 %collective-permute-start = (f32[3,72,128]{2,0,1:T(4,128)}, f32[3,72,128]{2,0,1:T(4,128)}, u32[]{:S(2)}, u32[]{:S(2)}) collective-permute-start(f32[3,72,128]{2,0,1:T(4,128)} %pad_maximum_fusion.2), channel_id=1, source_target_pairs={{0,4},{4,8},{8,12},{1,5},{5,9},{9,13},{2,6},{6,10},{10,14},{3,7},{... | collective-permute-start | bytes 331784 | tf_op jit(solution)/shard_map/ppermute | solution.py:14
  15.3 1.3 %fusion.75 = (f32[1,15,72,128]{3,2,1,0:T(8,128)}, f32[1,15,72,128]{3,2,1,0:T(8,128)}, f32[15,72,128]{2,1,0:T(8,128)}) fusion(f32[6,16,72,128]{3,2,1,0:T(8,128)S(1)} %copy-done.1), kind=kLoop, calls=%fused_computation.172 | loop fusion | bytes 3317760 | tf_op jit(solution)/shard_map/slice | solution.py:25
  17.4 1.1 %fusion.77 = (f32[1,16,72,128]{3,2,1,0:T(8,128)}, f32[1,16,72,128]{3,2,1,0:T(8,128)}) fusion(f32[3,16,72,128]{3,2,1,0:T(8,128)S(1)} %copy-done.15), kind=kLoop, calls=%fused_computation.174 | loop fusion | bytes 2359296 | tf_op jit(solution)/shard_map/slice | solution.py:117
  19.6 1.2 %broadcast_multiply_fusion.5 = (f32[72]{0:T(128)S(1)}, f32[72]{0:T(128)}) fusion(f32[72,4]{0,1:T(4,128)} %copy-done.18, s32[]{:T(128)} %bitcast.172, s32[]{:T(128)S(6)} %mul.133), kind=kLoop, calls=%fused_computation.170 | loop fusion | flops 288 | bytes 872 | tf_op jit(solution)/shard_map/mul | solution.py:54
  22.5 1.4 %broadcast_multiply_fusion.1 = (f32[16,72,128]{2,1,0:T(8,128)S(1)}, f32[16,72,128]{2,1,0:T(8,128)S(1)}) fusion(s32[16]{0:T(128)} %param.16, f32[16,72]{1,0:T(8,128)S(1)} %compare_convert_fusion, f32[16,16]{0,1:T(8,128)S(1)} %compare_select_fusion), kind=kOutput, calls=%fused_computation.126 | convolution fusion | flops 28479488 | bytes 1185344 | tf_op jit(solution)/shard_map/s,sx,sz,sy->xzy/dot_general | solution.py:86
  24.5 1.1 %slice.391 = f32[16,71,128]{2,0,1:T(8,128)S(1)} slice(f32[16,72,128]{2,0,1:T(8,128)} %bitcast.158), slice={[0:16], [0:71], [0:128]} | slice | bytes 1163264 | tf_op jit(solution)/shard_map/slice | solution.py:25
  25.7 1.2 %copy.312 = f32[1,15,72,128]{3,1,2,0:T(8,128)S(1)} copy(f32[1,15,72,128]{3,2,1,0:T(8,128)} %get-tuple-element.27) | data formatting | bytes 1105920
  28.0 1.2 %fusion.81 = (f32[1,72,128]{2,0,1:T(1,128)S(1)}, f32[1,72,128]{2,0,1:T(1,128)S(1)}, f32[1,72,128]{2,0,1:T(1,128)S(1)}) fusion(f32[3,72,128]{2,0,1:T(4,128)} %collective-permute-done), kind=kLoop, calls=%fused_computation.178 | loop fusion | bytes 221184 | tf_op jit(solution)/shard_map/slice | solution.py:66
  29.7 2.1 %broadcast_multiply_fusion = (f32[16,72,128]{2,1,0:T(8,128)S(1)}, f32[16,72,128]{2,1,0:T(8,128)S(1)}, f32[16,72,128]{2,1,0:T(8,128)S(1)}, f32[16,72,128]{2,1,0:T(8,128)S(1)}) fusion(f32[72]{0:T(128)S(1)} %get-tuple-element.77, f32[16,72,127]{2,1,0:T(8,128)S(1)} %bitcast.188, f32[6,16,72,128]{3,2,1,0:T(8,128)S(1)} %copy-done.1, ...), kind=kLoop, calls=%fused_computation.125 | loop fusion | flops 2506752 | bytes 8838720 | tf_op jit(solution)/shard_map/mul | solution.py:43
  34.2 2.6 %collective-permute-start.3 = (f32[3,16,128]{2,0,1:T(4,128)S(1)}, f32[3,16,128]{2,0,1:T(4,128)S(1)}, u32[]{:S(2)}, u32[]{:S(2)}) collective-permute-start(f32[3,16,128]{2,0,1:T(4,128)S(1)} %fusion.65), channel_id=1, source_target_pairs={{1,0},{2,1},{3,2},{5,4},{6,5},{7,6},{9,8},{10,9},{11,10},{13,12},{... | collective-permute-start | bytes 73736 | tf_op jit(solution)/shard_map/ppermute | solution.py:14
  37.9 1.9 %collective-permute-start.2 = (f32[3,72,128]{2,0,1:T(4,128)S(1)}, f32[3,72,128]{2,0,1:T(4,128)S(1)}, u32[]{:S(2)}, u32[]{:S(2)}) collective-permute-start(f32[3,72,128]{2,0,1:T(4,128)S(1)} %maximum_bitcast_fusion), channel_id=1, source_target_pairs={{4,0},{8,4},{12,8},{5,1},{9,5},{13,9},{6,2},{10,6},{14,10},{7,3},{... | collective-permute-start | bytes 331784 | tf_op jit(solution)/shard_map/ppermute | solution.py:14
  40.2 4.1 %collective-permute-done.2 = f32[3,72,128]{2,0,1:T(4,128)S(1)} collective-permute-done((f32[3,72,128]{2,0,1:T(4,128)S(1)}, f32[3,72,128]{2,0,1:T(4,128)S(1)}, u32[]{:S(2)}, u32[]{:S(2)}) %collective-permute-start.2) | collective-permute-done | bytes 110624 | tf_op jit(solution)/shard_map/ppermute | solution.py:14
  45.1 1.4 %fusion.16 = (f32[16,72,128]{2,0,1:T(8,128)S(1)}, f32[16,72,128]{2,0,1:T(8,128)S(1)}, f32[16,72,128]{2,0,1:T(8,128)S(1)}, f32[16,72,128]{2,0,1:T(8,128)S(1)}) fusion(f32[16,72,128]{2,0,1:T(8,128)S(1)} %get-tuple-element.11, f32[16,1,128]{2,0,1:T(8,128)S(1)} %bitcast.206, f32[16,71,128]{2,0,1:T(8,128)S(1)} %slice.421, ...), kind=kLoop, calls=%fused_computation.30 | loop fusion | flops 2949120 | bytes 11202624 | tf_op jit(solution)/shard_map/add | solution.py:58
  47.4 2.6 %collective-permute-start.5 = (f32[3,16,128]{2,1,0:T(8,128)S(1)}, f32[3,16,128]{2,1,0:T(8,128)S(1)}, u32[]{:S(2)}, u32[]{:S(2)}) collective-permute-start(f32[3,16,128]{2,1,0:T(8,128)S(1)} %pad_maximum_fusion.7), channel_id=1, source_target_pairs={{0,1},{1,2},{2,3},{4,5},{5,6},{6,7},{8,9},{9,10},{10,11},{12,13},{... | collective-permute-start | bytes 73736 | tf_op jit(solution)/shard_map/ppermute | solution.py:14
  50.4 2.2 %collective-permute-start.4 = (f32[3,72,128]{2,0,1:T(4,128)S(1)}, f32[3,72,128]{2,0,1:T(4,128)S(1)}, u32[]{:S(2)}, u32[]{:S(2)}) collective-permute-start(f32[3,72,128]{2,0,1:T(4,128)S(1)} %pad_maximum_fusion.3), channel_id=1, source_target_pairs={{0,4},{4,8},{8,12},{1,5},{5,9},{9,13},{2,6},{6,10},{10,14},{3,7},{... | collective-permute-start | bytes 331784 | tf_op jit(solution)/shard_map/ppermute | solution.py:14
  52.6 1.9 %collective-permute-done.4 = f32[3,72,128]{2,0,1:T(4,128)S(1)} collective-permute-done((f32[3,72,128]{2,0,1:T(4,128)S(1)}, f32[3,72,128]{2,0,1:T(4,128)S(1)}, u32[]{:S(2)}, u32[]{:S(2)}) %collective-permute-start.4) | collective-permute-done | bytes 110624 | tf_op jit(solution)/shard_map/ppermute | solution.py:14
  56.6 2.6 %collective-permute-start.7 = (f32[3,16,128]{2,1,0:T(8,128)S(1)}, f32[3,16,128]{2,1,0:T(8,128)S(1)}, u32[]{:S(2)}, u32[]{:S(2)}) collective-permute-start(f32[3,16,128]{2,1,0:T(8,128)S(1)} %slice_bitcast_fusion.4), channel_id=1, source_target_pairs={{1,0},{2,1},{3,2},{5,4},{6,5},{7,6},{9,8},{10,9},{11,10},{13,12},{... | collective-permute-start | bytes 73736 | tf_op jit(solution)/shard_map/ppermute | solution.py:14
  60.3 1.7 %copy.157 = f32[3,16,72,128]{3,2,1,0:T(8,128)} copy(f32[3,16,72,128]{3,1,0,2:T(8,128)S(1)} %pad_maximum_fusion) | data formatting | bytes 3538944
  62.1 1.9 %collective-permute-start.6 = (f32[3,72,128]{2,0,1:T(4,128)S(1)}, f32[3,72,128]{2,0,1:T(4,128)S(1)}, u32[]{:S(2)}, u32[]{:S(2)}) collective-permute-start(f32[3,72,128]{2,0,1:T(4,128)S(1)} %copy.136), channel_id=1, source_target_pairs={{4,0},{8,4},{12,8},{5,1},{9,5},{13,9},{6,2},{10,6},{14,10},{7,3},{... | collective-permute-start | bytes 331784 | tf_op jit(solution)/shard_map/ppermute | solution.py:14
  64.3 5.2 %collective-permute-done.6 = f32[3,72,128]{2,0,1:T(4,128)S(1)} collective-permute-done((f32[3,72,128]{2,0,1:T(4,128)S(1)}, f32[3,72,128]{2,0,1:T(4,128)S(1)}, u32[]{:S(2)}, u32[]{:S(2)}) %collective-permute-start.6) | collective-permute-done | bytes 110624 | tf_op jit(solution)/shard_map/ppermute | solution.py:14
  72.9 1.8 %copy-done.16 = f32[6,16,72,128]{3,2,1,0:T(8,128)} copy-done((f32[6,16,72,128]{3,2,1,0:T(8,128)}, f32[6,16,72,128]{3,2,1,0:T(8,128)S(1)}, u32[]{:S(2)}) %copy-start.16) | copy-done | bytes 3538968
  (133 shorter events, 20.5 us)
Async XLA Ops:
  0.6 15.9 %copy-start = (f32[8,4]{0,1:T(4,128)S(1)}, f32[8,4]{0,1:T(4,128)}, u32[]{:S(2)}) copy-start(f32[8,4]{0,1:T(4,128)} %param.12) | copy-start | bytes 388
  0.6 9.8 %copy-start.1 = (f32[6,16,72,128]{3,2,1,0:T(8,128)S(1)}, f32[6,16,72,128]{3,2,1,0:T(8,128)}, u32[]{:S(2)}) copy-start(f32[6,16,72,128]{3,2,1,0:T(8,128)} %param.10) | copy-start | bytes 10616836
  4.0 2.6 %copy-start.9 = (f32[16,72,128]{2,1,0:T(8,128)}, f32[16,72,128]{2,1,0:T(8,128)S(1)}, u32[]{:S(2)}) copy-start(f32[16,72,128]{2,1,0:T(8,128)S(1)} %get-tuple-element.25) | copy-start | bytes 1769476
  4.0 12.5 %copy-start.19 = (s32[72]{0:T(128)S(1)}, s32[72]{0:T(128)}, u32[]{:S(2)}) copy-start(s32[72]{0:T(128)} %param.11) | copy-start | bytes 868
  4.0 13.3 %copy-start.15 = (f32[3,16,72,128]{3,2,1,0:T(8,128)S(1)}, f32[3,16,72,128]{3,2,1,0:T(8,128)}, u32[]{:S(2)}) copy-start(f32[3,16,72,128]{3,2,1,0:T(8,128)} %param.9) | copy-start | bytes 5308420
  7.3 19.9 %collective-permute-start.1 = (f32[3,16,128]{2,1,0:T(8,128)}, f32[3,16,128]{2,1,0:T(8,128)}, u32[]{:S(2)}, u32[]{:S(2)}) collective-permute-start(f32[3,16,128]{2,1,0:T(8,128)} %pad_maximum_fusion.6), channel_id=1, source_target_pairs={{0,1},{1,2},{2,3},{4,5},{5,6},{6,7},{8,9},{9,10},{10,11},{12,13},{... | collective-permute-start | bytes 73736 | tf_op jit(solution)/shard_map/ppermute | solution.py:14
  11.3 16.8 %collective-permute-start = (f32[3,72,128]{2,0,1:T(4,128)}, f32[3,72,128]{2,0,1:T(4,128)}, u32[]{:S(2)}, u32[]{:S(2)}) collective-permute-start(f32[3,72,128]{2,0,1:T(4,128)} %pad_maximum_fusion.2), channel_id=1, source_target_pairs={{0,4},{4,8},{8,12},{1,5},{5,9},{9,13},{2,6},{6,10},{10,14},{3,7},{... | collective-permute-start | bytes 331784 | tf_op jit(solution)/shard_map/ppermute | solution.py:14
  16.7 2.9 %copy-start.18 = (f32[72,4]{0,1:T(4,128)}, f32[72,4]{0,1:T(4,128)S(1)}, u32[]{:S(2)}) copy-start(f32[72,4]{0,1:T(4,128)S(1)} %fusion.64) | copy-start | bytes 3460
  20.9 6.0 %copy-start.14 = (f32[1,15,72,128]{3,2,1,0:T(8,128)S(1)}, f32[1,15,72,128]{3,2,1,0:T(8,128)}, u32[]{:S(2)}) copy-start(f32[1,15,72,128]{3,2,1,0:T(8,128)} %get-tuple-element.26) | copy-start | bytes 1658884
  20.9 6.1 %copy-start.6 = (f32[1,16,72,128]{3,2,1,0:T(8,128)S(1)}, f32[1,16,72,128]{3,2,1,0:T(8,128)}, u32[]{:S(2)}) copy-start(f32[1,16,72,128]{3,2,1,0:T(8,128)} %get-tuple-element.24) | copy-start | bytes 1769476
  20.9 8.4 %copy-start.5 = (f32[1,16,72,128]{3,2,1,0:T(8,128)S(1)}, f32[1,16,72,128]{3,2,1,0:T(8,128)}, u32[]{:S(2)}) copy-start(f32[1,16,72,128]{3,2,1,0:T(8,128)} %copy-done.4) | copy-start | bytes 1769476
  20.9 8.4 %copy-start.7 = (f32[1,16,72,128]{3,2,1,0:T(8,128)S(1)}, f32[1,16,72,128]{3,2,1,0:T(8,128)}, u32[]{:S(2)}) copy-start(f32[1,16,72,128]{3,2,1,0:T(8,128)} %get-tuple-element.20) | copy-start | bytes 1769476
  26.8 2.8 %copy-start.3 = (f32[16,72,128]{2,1,0:T(8,128)S(1)}, f32[16,72,128]{2,1,0:T(8,128)}, u32[]{:S(2)}) copy-start(f32[16,72,128]{2,1,0:T(8,128)} %copy-done.2) | copy-start | bytes 1769476
  26.8 2.8 %copy-start.8 = (f32[16,72,128]{2,1,0:T(8,128)S(1)}, f32[16,72,128]{2,1,0:T(8,128)}, u32[]{:S(2)}) copy-start(f32[16,72,128]{2,1,0:T(8,128)} %get-tuple-element.22) | copy-start | bytes 1769476
  26.8 2.8 %copy-start.10 = (f32[16,72,128]{2,1,0:T(8,128)S(1)}, f32[16,72,128]{2,1,0:T(8,128)}, u32[]{:S(2)}) copy-start(f32[16,72,128]{2,1,0:T(8,128)} %copy-done.9) | copy-start | bytes 1769476
  26.9 2.8 %copy-start.13 = (f32[15,72,128]{2,1,0:T(8,128)S(1)}, f32[15,72,128]{2,1,0:T(8,128)}, u32[]{:S(2)}) copy-start(f32[15,72,128]{2,1,0:T(8,128)} %get-tuple-element.28) | copy-start | bytes 1658884
  29.7 2.1 %copy-start.11 = (f32[1,16,72,128]{3,2,1,0:T(8,128)S(1)}, f32[1,16,72,128]{3,2,1,0:T(8,128)}, u32[]{:S(2)}) copy-start(f32[1,16,72,128]{3,2,1,0:T(8,128)} %get-tuple-element.32) | copy-start | bytes 1769476
  29.7 2.1 %copy-start.12 = (f32[1,16,72,128]{3,2,1,0:T(8,128)S(1)}, f32[1,16,72,128]{3,2,1,0:T(8,128)}, u32[]{:S(2)}) copy-start(f32[1,16,72,128]{3,2,1,0:T(8,128)} %get-tuple-element.33) | copy-start | bytes 1769476
  34.2 6.1 %collective-permute-start.3 = (f32[3,16,128]{2,0,1:T(4,128)S(1)}, f32[3,16,128]{2,0,1:T(4,128)S(1)}, u32[]{:S(2)}, u32[]{:S(2)}) collective-permute-start(f32[3,16,128]{2,0,1:T(4,128)S(1)} %fusion.65), channel_id=1, source_target_pairs={{1,0},{2,1},{3,2},{5,4},{6,5},{7,6},{9,8},{10,9},{11,10},{13,12},{... | collective-permute-start | bytes 73736 | tf_op jit(solution)/shard_map/ppermute | solution.py:14
  37.9 6.5 %collective-permute-start.2 = (f32[3,72,128]{2,0,1:T(4,128)S(1)}, f32[3,72,128]{2,0,1:T(4,128)S(1)}, u32[]{:S(2)}, u32[]{:S(2)}) collective-permute-start(f32[3,72,128]{2,0,1:T(4,128)S(1)} %maximum_bitcast_fusion), channel_id=1, source_target_pairs={{4,0},{8,4},{12,8},{5,1},{9,5},{13,9},{6,2},{10,6},{14,10},{7,3},{... | collective-permute-start | bytes 331784 | tf_op jit(solution)/shard_map/ppermute | solution.py:14
  47.4 5.2 %collective-permute-start.5 = (f32[3,16,128]{2,1,0:T(8,128)S(1)}, f32[3,16,128]{2,1,0:T(8,128)S(1)}, u32[]{:S(2)}, u32[]{:S(2)}) collective-permute-start(f32[3,16,128]{2,1,0:T(8,128)S(1)} %pad_maximum_fusion.7), channel_id=1, source_target_pairs={{0,1},{1,2},{2,3},{4,5},{5,6},{6,7},{8,9},{9,10},{10,11},{12,13},{... | collective-permute-start | bytes 73736 | tf_op jit(solution)/shard_map/ppermute | solution.py:14
  50.4 4.1 %collective-permute-start.4 = (f32[3,72,128]{2,0,1:T(4,128)S(1)}, f32[3,72,128]{2,0,1:T(4,128)S(1)}, u32[]{:S(2)}, u32[]{:S(2)}) collective-permute-start(f32[3,72,128]{2,0,1:T(4,128)S(1)} %pad_maximum_fusion.3), channel_id=1, source_target_pairs={{0,4},{4,8},{8,12},{1,5},{5,9},{9,13},{2,6},{6,10},{10,14},{3,7},{... | collective-permute-start | bytes 331784 | tf_op jit(solution)/shard_map/ppermute | solution.py:14
  56.6 7.7 %collective-permute-start.7 = (f32[3,16,128]{2,1,0:T(8,128)S(1)}, f32[3,16,128]{2,1,0:T(8,128)S(1)}, u32[]{:S(2)}, u32[]{:S(2)}) collective-permute-start(f32[3,16,128]{2,1,0:T(8,128)S(1)} %slice_bitcast_fusion.4), channel_id=1, source_target_pairs={{1,0},{2,1},{3,2},{5,4},{6,5},{7,6},{9,8},{10,9},{11,10},{13,12},{... | collective-permute-start | bytes 73736 | tf_op jit(solution)/shard_map/ppermute | solution.py:14
  62.1 7.5 %collective-permute-start.6 = (f32[3,72,128]{2,0,1:T(4,128)S(1)}, f32[3,72,128]{2,0,1:T(4,128)S(1)}, u32[]{:S(2)}, u32[]{:S(2)}) collective-permute-start(f32[3,72,128]{2,0,1:T(4,128)S(1)} %copy.136), channel_id=1, source_target_pairs={{4,0},{8,4},{12,8},{5,1},{9,5},{13,9},{6,2},{10,6},{14,10},{7,3},{... | collective-permute-start | bytes 331784 | tf_op jit(solution)/shard_map/ppermute | solution.py:14
  (4 other events, 4.3 us)
where the time goes:
time: 75.3 us; the launch traced here: 74.7 us
  local copies, waits for them, and re-layouts  21.9 us (29%)
  starting transfers between devices  21.2 us (28%)
  other arithmetic  16.8 us (22%)
  waiting for transfers between devices  11.2 us (15%)
  between operations  2.1 us (3%)
  matrix products  1.58 us (2%)
    ppermute x8, starting transfers between devices, from_behind(): return lax.ppermute(block, axis, route)  21.2 us
    ppermute x8, waiting for transfers between devices, from_behind(): return lax.ppermute(block, axis, route)  11.2 us
    unnamed x54, local copies, waits for them, and re-layouts  8.39 us
    slice x1, local copies, waits for them, and re-layouts, local(): forces = [stress[c] for c in range(6)]  3.36 us
    mul x2, other arithmetic, velocity_update(): (1.0 - courant * coeff[3]) * speeds[k] + courant * coeff[0] * total  2.74 us
    slice x5, local copies, waits for them, and re-layouts, backward(): lax.slice_in_dim(field, 0, count - 1, axis=axis)  2.49 us
    slice x18, local copies, waits for them, and re-layouts, forward(): lax.slice_in_dim(field, 1, count, axis=axis)  1.81 us
    add x3, other arithmetic, velocity_update(): (1.0 - courant * coeff[3]) * speeds[k] + courant * coeff[0] * total  1.71 us
  transfers between devices with their start and end apart: 8, of which 3 were waited for; matrix products, arithmetic and copies ran while one was open for 23% of the time, Pallas kernels for 0%

commit v1 on v0

v1 whole, which is shorter than its diff:
```python
import functools

import jax
import jax.numpy as jnp
from jax import lax
from jax.experimental import pallas as pl
from jax.experimental.pallas import tpu as pltpu
from jax.sharding import PartitionSpec as P

courant = 0.2
wavelet = (1.0, -0.5)
pair_table = ((0, 3, 4), (3, 1, 5), (4, 5, 2))
front = (0, 3, 4)
top = (3, 1, 5)
PAD = 8
ANY = pl.BlockSpec(memory_space=pl.ANY)
VMEM = pl.BlockSpec(memory_space=pltpu.VMEM)
SMEM = pl.BlockSpec(memory_space=pltpu.SMEM)


def swap_pairs(rows, cols, along, odd):
    out = []
    for i in range(rows):
        for j in range(cols):
            at, size = (i, rows) if along == 0 else (j, cols)
            if not odd:
                to = at ^ 1
            elif at in (0, size - 1):
                to = None
            else:
                to = at + 1 if at % 2 else at - 1
            if along == 0:
                target = (i, j ^ 1) if to is None else (to, j)
            else:
                target = (i ^ 1, j) if to is None else (i, to)
            out.append((i * cols + j, target[0] * cols + target[1]))
    return out


def swap(block, along, odd):
    rows, cols = lax.axis_size("horiz"), lax.axis_size("vert")
    return lax.ppermute(block, ("horiz", "vert"), swap_pairs(rows, cols, along, odd))


def lane_of(shape):
    return lax.broadcasted_iota(jnp.int32, shape, len(shape) - 1)


def back_lane(a):
    moved = pltpu.roll(a, 1, 1)
    return a - jnp.where(lane_of(a.shape) == 0, 0.0, moved)


def fore_lane(a):
    last = a.shape[-1] - 1
    moved = pltpu.roll(a, last, 1)
    return jnp.where(lane_of(a.shape) == last, 0.0, moved) - a


def velocity_tile(s_at, v_at, rb, dq):
    out = []
    for k in range(3):
        a, b, c = pair_table[k]
        total = (s_at(a, 0, 0) - s_at(a, -1, 0)) + (s_at(b, 0, 0) - s_at(b, 0, -1))
        total = total + back_lane(s_at(c, 0, 0))
        out.append(dq * v_at(k) + rb * total)
    return out


def strain(v_at):
    grads = []
    for i in range(3):
        here = v_at(i, 0, 0)
        grads.append([v_at(i, 1, 0) - here, v_at(i, 0, 1) - here, fore_lane(here)])
    return grads


def stress_terms(g, rl, rm, wanted=range(6)):
    out = {}
    if any(c < 3 for c in wanted):
        spread = rl * (g[0][0] + g[1][1] + g[2][2])
    for c in wanted:
        if c < 3:
            out[c] = spread + 2.0 * rm * g[c][c]
        else:
            i, j = ((0, 1), (0, 2), (1, 2))[c - 3]
            out[c] = rm * (g[i][j] + g[j][i])
    return out


def memo(fn):
    seen = {}

    def call(*key):
        if key not in seen:
            seen[key] = fn(*key)
        return seen[key]

    return call


MSG = 200


def level_scalars(index_ref, table_ref, split_ref, z, offset):
    kind = index_ref[z]
    solid = jnp.where(offset + z >= split_ref[0], 1.0, 0.0)
    return (
        courant * table_ref[kind, 0],
        1.0 - courant * table_ref[kind, 3],
        courant * table_ref[kind, 1],
        courant * (table_ref[kind, 2] * solid),
    )


def edge_kernel(n, m, y, v_ref, s_ref, index_ref, table_ref, split_ref, out_a, out_b, low, high, sems):
    vert = lax.axis_index("vert")
    odd = vert % 2 == 1
    copies = []
    for at, (buf, start) in enumerate(((low, 0), (high, m - 8))):
        copies.append(
            pltpu.make_async_copy(s_ref.at[:, :, pl.ds(start, 8), :], buf.at[pl.ds(0, 6), pl.ds(1, n)], sems.at[2 * at])
        )
        copies.append(
            pltpu.make_async_copy(
                v_ref.at[:, :, pl.ds(start, 8), :], buf.at[pl.ds(6, 3), pl.ds(1, n)], sems.at[2 * at + 1]
            )
        )
    for copy in copies:
        copy.start()
    for buf in (low, high):
        for f in front:
            buf[f, 0] = jnp.zeros((8, y), jnp.float32)
    offset = vert * m
    at_first = level_scalars(index_ref, table_ref, split_ref, 0, offset)
    at_second = level_scalars(index_ref, table_ref, split_ref, 1, offset)
    at_last = level_scalars(index_ref, table_ref, split_ref, m - 1, offset)
    for copy in copies:
        copy.wait()
    low2 = low.reshape(9 * (n + 1) * 8, y)
    high2 = high.reshape(9 * (n + 1) * 8, y)

    def row(buf, f, z, dx=0):
        return buf[pl.Slice((f * (n + 1) + 1 + dx) * 8 + z, n, 8), :]

    def moved(buf, z, scal):
        return velocity_tile(
            memo(lambda f, dx, dz: row(buf, f, z + dz, dx)), lambda k: row(buf, 6 + k, z), scal[0], scal[1]
        )

    up = [row(high2, f, 7) for f in range(6)] + moved(high2, 7, at_last)
    down = [row(low2, f, 0) for f in range(9)] + moved(low2, 1, at_second)

    def put(at, rows, up_value, down_value):
        out_a[pl.ds(at, rows), :] = jnp.where(odd, down_value, up_value)
        out_b[pl.ds(at, rows), :] = jnp.where(odd, up_value, down_value)

    for f in range(12):
        put(f * n, n, up[f] if f < 9 else down[f], down[f])
    base = 12 * n
    for c in range(4):
        splat = [jnp.full((1, y), a[c], jnp.float32) for a in (at_last, at_first)]
        put(base + c, 1, *splat)
    ahead = jnp.full((1, y), at_second[0], jnp.float32)
    put(base + 4, 1, ahead, ahead)
    for c, f in enumerate(front):
        corner = low[f, n, pl.ds(1, 1), :]
        put(base + 5 + c, 1, corner, corner)


def level_kernel(m, index_ref, table_ref, split_ref, out_ref):
    offset = lax.axis_index("vert") * m
    y = out_ref.shape[-1]

    def body(z, carry):
        for c, value in enumerate(level_scalars(index_ref, table_ref, split_ref, z, offset)):
            out_ref[c, pl.ds(z, 1), :] = jnp.full((1, y), value, jnp.float32)
        return carry

    lax.fori_loop(0, m, body, 0, unroll=8)


def sort_levels(a_ref, b_ref, below, above):
    vert = lax.axis_index("vert")
    odd = vert % 2 == 1
    has_below = jnp.where(vert > 0, 1.0, 0.0)
    has_above = jnp.where(vert < lax.axis_size("vert") - 1, 1.0, 0.0)
    for t in range(MSG // 8):
        at = pl.ds(8 * t, 8)
        a, b = a_ref[at, :], b_ref[at, :]
        below[at, :] = has_below * jnp.where(odd, a, b)
        above[at, :] = has_above * jnp.where(odd, b, a)


def add_sources(add_row, plane_x, z_low, z_high, scale, x_at, z_at, src):
    sx, sz, sy, amp = src

    def body(i, carry):
        z = sz[i] - z_at

        @pl.when((sx[i] - x_at == plane_x) & (z >= z_low) & (z < z_high))
        def _():
            lane = lane_of((1, 128))
            add_row(z, jnp.where(lane == sy[i], scale * amp[i], 0.0))

        return carry

    lax.fori_loop(0, sx.shape[0], body, 0)


def plane_kernel(
    n, m, y, v_ref, s_ref, a_ref, b_ref, level_ref, sx, sz, sy, amp,
    out_a, out_b, coef, below, above, sl, vl, sr, vr, msg, sems,
):
    horiz, vert = lax.axis_index("horiz"), lax.axis_index("vert")
    body = pl.ds(PAD, m)
    copies = [
        pltpu.make_async_copy(s_ref.at[:, pl.ds(0, 2)], sl.at[:, pl.ds(1, 2), body], sems.at[0]),
        pltpu.make_async_copy(v_ref.at[:, pl.ds(0, 2)], vl.at[:, :, body], sems.at[1]),
        pltpu.make_async_copy(s_ref.at[:, pl.ds(n - 2, 2)], sr.at[:, :, body], sems.at[2]),
        pltpu.make_async_copy(v_ref.at[:, pl.ds(n - 1, 1)], vr.at[:, pl.ds(0, 1), body], sems.at[3]),
    ]
    for copy in copies:
        copy.start()
    sort_levels(a_ref, b_ref, below, above)
    lowest, first, second = PAD - 1, PAD + m, PAD + m + 1
    base = 12 * n
    for c in range(4):
        coef[c, body, :] = level_ref[c]
        coef[c, pl.ds(lowest, 1), :] = below[pl.ds(base + c, 1), :]
        coef[c, pl.ds(first, 1), :] = above[pl.ds(base + c, 1), :]
    coef[0, pl.ds(second, 1), :] = above[pl.ds(base + 4, 1), :]
    for f in front:
        sl[f, 0] = jnp.zeros((m + 16, y), jnp.float32)
    for k in range(3):
        vr[k, 1] = jnp.zeros((m + 16, y), jnp.float32)

    for x, buf, at in ((0, sl, 1), (1, sl, 2), (n - 2, sr, 0), (n - 1, sr, 1)):
        for f in range(6):
            buf[f, at, pl.ds(lowest, 1), :] = below[pl.ds(f * n + x, 1), :]
            buf[f, at, pl.ds(first, 1), :] = above[pl.ds(f * n + x, 1), :]
    for x, buf, at in ((0, vl, 0), (1, vl, 1), (n - 1, vr, 0)):
        for k in range(3):
            buf[k, at, pl.ds(lowest, 1), :] = below[pl.ds((6 + k) * n + x, 1), :]
            buf[k, at, pl.ds(first, 1), :] = above[pl.ds((6 + k) * n + x, 1), :]
            buf[k, at, pl.ds(second, 1), :] = above[pl.ds((9 + k) * n + x, 1), :]

    tiles = [(PAD + 8 * t, 8) for t in range(m // 8)]
    right, left = horiz % 2, 1 - horiz % 2
    tail = 6 * m

    def cs(c, r, size):
        return coef[c, pl.ds(r, size), :]

    def move(s_buf, v_buf, s_at, v_at, r, size):
        new = velocity_tile(
            memo(lambda f, dx, dz: s_buf[f, s_at + dx, pl.ds(r + dz, size), :]),
            lambda k: v_buf[k, v_at, pl.ds(r, size), :],
            cs(0, r, size),
            cs(1, r, size),
        )
        for k in range(3):
            v_buf[k, v_at, pl.ds(r, size), :] = new[k]
        return new

    def load(s_buf, v_buf, s_at, v_at, r, size, wanted):
        g = strain(memo(lambda k, dx, dz: v_buf[k, v_at + dx, pl.ds(r + dz, size), :]))
        terms = stress_terms(g, cs(2, r, size), cs(3, r, size), wanted)
        for c in wanted:
            s_buf[c, s_at, pl.ds(r, size), :] = s_buf[c, s_at, pl.ds(r, size), :] + terms[c]

    copies[2].wait()
    copies[3].wait()
    for c, f in enumerate(front):
        for r, size in tiles:
            msg[right, pl.ds(c * m + r - PAD, size), :] = sr[f, 1, pl.ds(r, size), :]
        msg[right, pl.ds(tail + c, 1), :] = sr[f, 1, pl.ds(lowest, 1), :]
        msg[right, pl.ds(tail + 3 + c, 1), :] = sr[f, 1, pl.ds(first, 1), :]
        msg[right, pl.ds(tail + 6 + c, 1), :] = above[pl.ds(base + 5 + c, 1), :]
    for r, size in tiles + [(first, 1)]:
        move(sr, vr, 1, 0, r, size)
    for r, size in tiles + [(first, 1)]:
        load(sr, vr, 1, 0, r, size, front)

    x_at, z_at = horiz * n, vert * m
    src = (sx, sz, sy, amp)
    scale = courant * wavelet[0]

    def add_right(z, row):
        at = pl.ds(PAD + z, 1)
        sr[0, 1, at, :] = sr[0, 1, at, :] + row

    add_sources(add_right, n - 1, 0, m + 1, scale, x_at, z_at, src)
    for c, f in enumerate(front):
        for r, size in tiles:
            msg[right, pl.ds((3 + c) * m + r - PAD, size), :] = sr[f, 1, pl.ds(r, size), :]
        msg[right, pl.ds(tail + 9 + c, 1), :] = sr[f, 1, pl.ds(first, 1), :]

    copies[0].wait()
    copies[1].wait()
    for r, size in tiles + [(first, 1)]:
        new = move(sl, vl, 1, 0, r, size)
        for k in range(3):
            at = k * m + r - PAD if r < first else tail + 3 + k
            msg[left, pl.ds(at, size), :] = new[k]
        move(sl, vl, 2, 1, r, size)
    for k in range(3):
        msg[left, pl.ds(tail + k, 1), :] = vl[k, 0, pl.ds(lowest, 1), :]
    load(sl, vl, 1, 0, lowest, 1, top)
    for r, size in tiles:
        load(sl, vl, 1, 0, r, size, range(6))

    def add_left(z, row):
        at = pl.ds(PAD + z, 1)
        for c in range(3):
            sl[c, 1, at, :] = sl[c, 1, at, :] + row

    add_sources(add_left, 0, -1, m, scale, x_at, z_at, src)
    for r, size in tiles:
        new = move(sl, vl, 1, 0, r, size)
        for k in range(3):
            msg[left, pl.ds((3 + k) * m + r - PAD, size), :] = new[k]
    done = [
        pltpu.make_async_copy(msg.at[0], out_a, sems.at[0]),
        pltpu.make_async_copy(msg.at[1], out_b, sems.at[1]),
    ]
    for copy in done:
        copy.start()
    for copy in done:
        copy.wait()


def main_kernel(
    n, m, y, v_ref, s_ref, a_ref, b_ref, coef, sx, sz, sy, amp,
    out_v, out_s, below, above, sb, vb, count, in_v, in_s, off_v, off_s,
):
    horiz, vert = lax.axis_index("horiz"), lax.axis_index("vert")
    body = pl.ds(PAD, m)
    x_at, z_at = horiz * n, vert * m

    def v_in(x):
        return pltpu.make_async_copy(v_ref.at[:, x], vb.at[:, x, body], in_v.at[x])

    def s_in(x):
        return pltpu.make_async_copy(s_ref.at[:, x], sb.at[:, x + 1, body], in_s.at[x])

    def v_off(x):
        return pltpu.make_async_copy(vb.at[:, x, body], out_v.at[:, x], off_v.at[x])

    def s_off(x):
        return pltpu.make_async_copy(sb.at[:, x + 1, body], out_s.at[:, x], off_s.at[x])

    def begin(x, carry):
        s_in(x).start()
        v_in(x).start()
        count[x] = 0
        return carry

    lax.fori_loop(0, n, begin, 0)

    def tally(i, carry):
        x, z = sx[i] - x_at, sz[i] - z_at

        @pl.when((x >= 0) & (x < n) & (z >= -1) & (z <= m))
        def _():
            count[x] = count[x] + 1

        return carry

    lax.fori_loop(0, sx.shape[0], tally, 0)
    sort_levels(a_ref, b_ref, below, above)
    lowest, first, second = PAD - 1, PAD + m, PAD + m + 1
    for f in front:
        sb[f, 0] = jnp.zeros((m + 16, y), jnp.float32)
    for k in range(3):
        vb[k, n] = jnp.zeros((m + 16, y), jnp.float32)
    high = m + 16
    s2 = sb.reshape(6 * (n + 1) * high, y)
    v2 = vb.reshape(3 * (n + 1) * high, y)
    for f in range(6):
        start = (f * (n + 1) + 1) * high
        s2[pl.Slice(start + lowest, n, high), :] = below[pl.ds(f * n, n), :]
        s2[pl.Slice(start + first, n, high), :] = above[pl.ds(f * n, n), :]
    for k in range(3):
        start = k * (n + 1) * high
        v2[pl.Slice(start + lowest, n, high), :] = below[pl.ds((6 + k) * n, n), :]
        v2[pl.Slice(start + first, n, high), :] = above[pl.ds((6 + k) * n, n), :]
        v2[pl.Slice(start + second, n, high), :] = above[pl.ds((9 + k) * n, n), :]

    tiles = [(PAD + 8 * t, 8) for t in range(m // 8)]

    def cs(c, r, size):
        return coef[c, pl.ds(r, size), :]

    def move(x):
        for r, size in tiles + [(first, 1)]:
            new = velocity_tile(
                memo(lambda f, dx, dz: sb[f, x + 1 + dx, pl.ds(r + dz, size), :]),
                lambda k: vb[k, x, pl.ds(r, size), :],
                cs(0, r, size),
                cs(1, r, size),
            )
            for k in range(3):
                vb[k, x, pl.ds(r, size), :] = new[k]

    def load(x, step):
        parts = [(r, size, range(6)) for r, size in tiles]
        if step == 0:
            parts += [(lowest, 1, top), (first, 1, range(6))]
        for r, size, wanted in parts:
            g = strain(memo(lambda k, dx, dz: vb[k, x + dx, pl.ds(r + dz, size), :]))
            terms = stress_terms(g, cs(2, r, size), cs(3, r, size), wanted)
            for c in wanted:
                sb[c, x + 1, pl.ds(r, size), :] = sb[c, x + 1, pl.ds(r, size), :] + terms[c]

        def add(z, row):
            at = pl.ds(PAD + z, 1)
            for c in range(3):
                sb[c, x + 1, at, :] = sb[c, x + 1, at, :] + row

        @pl.when(count[x] > 0)
        def _():
            span = (-1, m + 1) if step == 0 else (0, m)
            add_sources(add, x, *span, courant * wavelet[step], x_at, z_at, (sx, sz, sy, amp))

    def advance(i, carry):
        @pl.when(i < n)
        def _():
            s_in(i).wait()
            v_in(i).wait()
            move(i)

        @pl.when((i >= 1) & (i <= n))
        def _():
            load(i - 1, 0)
            move(i - 1)
            v_off(i - 1).start()

        @pl.when(i >= 2)
        def _():
            load(i - 2, 1)
            s_off(i - 2).start()

        return carry

    lax.fori_loop(0, n + 2, advance, 0)

    def finish(x, carry):
        v_off(x).wait()
        s_off(x).wait()
        return carry

    lax.fori_loop(0, n, finish, 0)


def join_kernel(
    n, m, y, ra, rb_, ma, mb, coef, v_in, s_in, v_out, s_out,
    held, ea, wa, da, ds, dv, dw, qb, db, es, ev, vn, v0, v1, s0, s1, sems,
):
    horiz = lax.axis_index("horiz")
    copies = [pltpu.make_async_copy(src, held.at[i], sems.at[i]) for i, src in enumerate((ra, rb_, ma, mb))]
    planes = [
        (v_in.at[:, pl.ds(0, 2)], v_out.at[:, pl.ds(0, 2)], v0),
        (v_in.at[:, pl.ds(n - 1, 1)], v_out.at[:, pl.ds(n - 1, 1)], v1),
        (s_in.at[:, pl.ds(0, 2)], s_out.at[:, pl.ds(0, 2)], s0),
        (s_in.at[:, pl.ds(n - 2, 2)], s_out.at[:, pl.ds(n - 2, 2)], s1),
    ]
    fetch = [pltpu.make_async_copy(src, buf, sems.at[4 + i]) for i, (src, _, buf) in enumerate(planes)]
    store = [pltpu.make_async_copy(buf, dst, sems.at[4 + i]) for i, (_, dst, buf) in enumerate(planes)]
    for copy in copies + fetch:
        copy.start()
    right, left = horiz % 2, 1 - horiz % 2
    has_left = jnp.where(horiz > 0, 1.0, 0.0)
    has_right = jnp.where(horiz < lax.axis_size("horiz") - 1, 1.0, 0.0)
    lowest, first, second = PAD - 1, PAD + m, PAD + m + 1
    tail = 6 * m
    tiles = [(PAD + 8 * t, 8) for t in range(m // 8)]

    def cs(c, r, size):
        return coef[c, pl.ds(r, size), :]

    def msg(which, c, r, size):
        return held[which, pl.ds(c * m + r - PAD, size), :]

    def end(which, at):
        return held[which, pl.ds(tail + at, 1), :]

    for copy in copies:
        copy.wait()

    for k in range(3):
        rows = [(r, size, msg(left, k, r, size)) for r, size in tiles]
        rows += [(r, 1, end(left, at + k)) for r, at in ((lowest, 0), (first, 3), (second, 6))]
        for r, size, value in rows:
            da[k, pl.ds(r, size), :] = -(has_left * cs(0, r, size)) * value
        rows = [(r, size, msg(left, 3 + k, r, size), msg(2 + left, k, r, size)) for r, size in tiles]
        rows += [(first, 1, end(left, 9 + k), end(2 + left, 3 + k))]
        for r, size, value, own in rows:
            gain = cs(3, r, size) if k else cs(2, r, size) + 2.0 * cs(3, r, size)
            wa[k, pl.ds(r, size), :] = has_left * (value + gain * (own + da[k, pl.ds(r, size), :]))
        rows = [(r, size, msg(2 + right, k, r, size), msg(right, k, r, size)) for r, size in tiles]
        rows += [(r, 1, end(2 + right, at + k), end(right, at + k)) for r, at in ((lowest, 0), (first, 3))]
        for r, size, value, other in rows:
            change = -(has_right * cs(0, r, size)) * value
            db[k, pl.ds(r, size), :] = change
            qb[k, pl.ds(r, size), :] = has_right * other + change

    def flat(buf):
        def at(k, dx, dz, r, size):
            if dx:
                return None
            return buf[k, pl.ds(r + dz, size), :]

        return at

    def strain_of(buf, r, size, ahead=None):
        grads = []
        for i in range(3):
            here = buf[i, pl.ds(r, size), :]
            beyond = -here if ahead is None else ahead[i, pl.ds(r, size), :] - here
            grads.append([beyond, buf[i, pl.ds(r + 1, size), :] - here, fore_lane(here)])
        return grads

    for out, src, ends in ((ds, da, (lowest, first)), (es, db, (lowest,))):
        parts = [(r, size, range(6)) for r, size in tiles]
        parts += [(r, 1, top if r == lowest else range(6)) for r in ends]
        for r, size, wanted in parts:
            terms = stress_terms(strain_of(src, r, size), cs(2, r, size), cs(3, r, size), wanted)
            for c in wanted:
                out[c, pl.ds(r, size), :] = terms[c]

    for r, size in tiles + [(first, 1)]:
        rb, dq = cs(0, r, size), cs(1, r, size)
        for k in range(3):
            a, b, c = pair_table[k]
            here = ds[a, pl.ds(r, size), :]
            total = here - wa[k, pl.ds(r, size), :]
            total = total + (ds[b, pl.ds(r, size), :] - ds[b, pl.ds(r - 1, size), :])
            total = total + back_lane(ds[c, pl.ds(r, size), :])
            dv[k, pl.ds(r, size), :] = dq * da[k, pl.ds(r, size), :] + rb * total
            dw[k, pl.ds(r, size), :] = -rb * here

    def last_stress(c, r, size):
        q = qb[0 if c < 3 else c - 2, pl.ds(r, size), :]
        if c == 0:
            return (cs(2, r, size) + 2.0 * cs(3, r, size)) * q
        return (cs(2, r, size) if c < 3 else cs(3, r, size)) * q

    for r, size in tiles + [(first, 1)]:
        rb, dq = cs(0, r, size), cs(1, r, size)
        full = [last_stress(c, r, size) for c in range(5)]
        totals = [
            full[0] + (full[3] - last_stress(3, r - 1, size)) + back_lane(full[4]),
            full[3] + (full[1] - last_stress(1, r - 1, size)),
            full[4] + back_lane(full[2]),
        ]
        for k in range(3):
            ev[k, pl.ds(r, size), :] = rb * totals[k]
        if r == first:
            continue
        for k in range(3):
            a, b, c = pair_table[k]
            total = es[a, pl.ds(r, size), :] - (msg(2 + right, 3 + k, r, size) + full[a])
            total = total + (es[b, pl.ds(r, size), :] - es[b, pl.ds(r - 1, size), :])
            total = total + back_lane(es[c, pl.ds(r, size), :])
            change = dq * db[k, pl.ds(r, size), :] + rb * total
            vn[k, pl.ds(r, size), :] = has_right * (msg(right, 3 + k, r, size) + change)

    for copy in fetch:
        copy.wait()
    for r, size in tiles:
        out = pl.ds(r - PAD, size)
        at = pl.ds(r, size)
        rl, rm = cs(2, r, size), cs(3, r, size)
        for k in range(3):
            v0[k, 0, out, :] = v0[k, 0, out, :] + dv[k, at, :]
            v0[k, 1, out, :] = v0[k, 1, out, :] + dw[k, at, :]
            v1[k, 0, out, :] = v1[k, 0, out, :] + ev[k, at, :]
        terms = stress_terms(strain_of(dv, r, size, dw), rl, rm)
        for c in range(6):
            s0[c, 0, out, :] = s0[c, 0, out, :] + (ds[c, at, :] + terms[c])
        terms = stress_terms(strain_of(dw, r, size), rl, rm)
        for c in range(6):
            s0[c, 1, out, :] = s0[c, 1, out, :] + terms[c]
        terms = stress_terms(strain_of(ev, r, size, vn), rl, rm)
        for c in range(6):
            more = terms[c] if c == 5 else terms[c] + last_stress(c, r, size)
            s1[c, 1, out, :] = s1[c, 1, out, :] + more
        e = [ev[k, at, :] for k in range(3)]
        spread = rl * e[0]
        for c, more in enumerate((spread + 2.0 * rm * e[0], spread, spread, rm * e[1], rm * e[2])):
            s1[c, 0, out, :] = s1[c, 0, out, :] + more
    for copy in store:
        copy.start()
    for copy in store:
        copy.wait()


def local(velocity, stress, index, table, split, source_x, source_z, source_y, amplitude):
    _, n, m, y = velocity.shape
    f32 = jnp.float32
    high = m + 16
    dma = pltpu.SemaphoreType.DMA
    big = pltpu.CompilerParams(vmem_limit_bytes=40 * 1024 * 1024)
    sources = (source_x, source_z, source_y, amplitude)

    def shape(*dims):
        return jax.ShapeDtypeStruct(dims, f32)

    def cost(flops, moved):
        return pl.CostEstimate(flops=flops, bytes_accessed=moved, transcendentals=0)

    edge_a, edge_b = pl.pallas_call(
        functools.partial(edge_kernel, n, m, y),
        out_shape=[shape(MSG, y)] * 2,
        in_specs=[ANY, ANY, SMEM, SMEM, SMEM],
        out_specs=[VMEM, VMEM],
        scratch_shapes=[pltpu.VMEM((9, n + 1, 8, y), f32)] * 2 + [dma((4,))],
        compiler_params=big,
        name="edge_levels",
    )(velocity, stress, index, table, split)
    got_a, got_b = swap(edge_a, 1, False), swap(edge_b, 1, True)
    levels = pl.pallas_call(
        functools.partial(level_kernel, m),
        out_shape=shape(4, m, y),
        in_specs=[SMEM, SMEM, SMEM],
        out_specs=VMEM,
        compiler_params=big,
        name="level_coefficients",
    )(index, table, split)
    plane_a, plane_b, coef = pl.pallas_call(
        functools.partial(plane_kernel, n, m, y),
        out_shape=[shape(6 * m + 16, y)] * 2 + [shape(4, high, y)],
        in_specs=[ANY, ANY, VMEM, VMEM, VMEM] + [SMEM] * 4,
        out_specs=[ANY, ANY, VMEM],
        scratch_shapes=[
            pltpu.VMEM((MSG, y), f32),
            pltpu.VMEM((MSG, y), f32),
            pltpu.VMEM((6, 3, high, y), f32),
            pltpu.VMEM((3, 2, high, y), f32),
            pltpu.VMEM((6, 2, high, y), f32),
            pltpu.VMEM((3, 2, high, y), f32),
            pltpu.VMEM((2, 6 * m + 16, y), f32),
            dma((4,)),
        ],
        compiler_params=big,
        name="edge_planes",
    )(velocity, stress, got_a, got_b, levels, *sources)
    next_a, next_b = swap(plane_a, 0, False), swap(plane_b, 0, True)
    v_own, s_own = pl.pallas_call(
        functools.partial(main_kernel, n, m, y),
        out_shape=[shape(*velocity.shape), shape(*stress.shape)],
        in_specs=[ANY, ANY, VMEM, VMEM, VMEM] + [SMEM] * 4,
        out_specs=[ANY, ANY],
        scratch_shapes=[
            pltpu.VMEM((MSG, y), f32),
            pltpu.VMEM((MSG, y), f32),
            pltpu.VMEM((6, n + 1, high, y), f32),
            pltpu.VMEM((3, n + 1, high, y), f32),
            pltpu.SMEM((n,), jnp.int32),
            dma((n,)),
            dma((n,)),
            dma((n,)),
            dma((n,)),
        ],
        compiler_params=big,
        cost_estimate=cost(140 * n * m * y, 8 * 9 * n * m * y),
        name="both_steps",
    )(velocity, stress, got_a, got_b, coef, *sources)
    return pl.pallas_call(
        functools.partial(join_kernel, n, m, y),
        out_shape=[shape(*velocity.shape), shape(*stress.shape)],
        in_specs=[ANY] * 4 + [VMEM] + [ANY] * 2,
        out_specs=[ANY, ANY],
        input_output_aliases={5: 0, 6: 1},
        scratch_shapes=[
            pltpu.VMEM((4, 6 * m + 16, y), f32),
            pltpu.VMEM((3, high, y), f32),
            pltpu.VMEM((3, high, y), f32),
            pltpu.VMEM((3, high, y), f32),
            pltpu.VMEM((6, high, y), f32),
            pltpu.VMEM((3, high, y), f32),
            pltpu.VMEM((3, high, y), f32),
            pltpu.VMEM((3, high, y), f32),
            pltpu.VMEM((3, high, y), f32),
            pltpu.VMEM((6, high, y), f32),
            pltpu.VMEM((3, high, y), f32),
            pltpu.VMEM((3, high, y), f32),
            pltpu.VMEM((3, 2, m, y), f32),
            pltpu.VMEM((3, 1, m, y), f32),
            pltpu.VMEM((6, 2, m, y), f32),
            pltpu.VMEM((6, 2, m, y), f32),
            dma((8,)),
        ],
        compiler_params=big,
        name="join_neighbours",
    )(next_a, next_b, plane_a, plane_b, coef, v_own, s_own)


def solution(mesh):
    block = P("member", "horiz", "vert", None)
    return jax.shard_map(
        local,
        mesh=mesh,
        in_specs=(block, block, P("vert"), P(), P(), P(), P(), P(), P("member")),
        out_specs=(block, block),
        check_vma=False,
    )
```

time: 75.3 us -> 34.5 us (0.46)
  the two profiles are of different devices: /device:TPU:9 before, /device:TPU:0 now
where the time goes in v1:
time: 34.5 us; the launch traced here: 34.2 us
  Pallas kernels  19.9 us (58%)
  starting transfers between devices  6.13 us (18%)
  local copies, waits for them, and re-layouts  4.91 us (14%)
  waiting for transfers between devices  1.82 us (5%)
  between operations  1.44 us (4%)
    pallas_call x1, Pallas kernels, local(): pl.pallas_call(functools.partial(main_kernel, n, m, y), out_shape=[shape(...  11.8 us
    ppermute x4, starting transfers between devices, swap(): lax.ppermute(block, ('horiz', 'vert'), swap_pairs(rows, cols, along, odd))  6.13 us
    unnamed x19, local copies, waits for them, and re-layouts  4.91 us
    pallas_call x1, Pallas kernels, local(): pl.pallas_call(functools.partial(join_kernel, n, m, y), out_shape=[shape(...  3.82 us
    pallas_call x1, Pallas kernels, local(): pl.pallas_call(functools.partial(plane_kernel, n, m, y), out_shape=[shape...  2.44 us
    ppermute x4, waiting for transfers between devices, swap(): lax.ppermute(block, ('horiz', 'vert'), swap_pairs(rows, cols, along, odd))  1.82 us
    pallas_call x1, Pallas kernels, local(): pl.pallas_call(functools.partial(level_kernel, m), out_shape=shape(4, m,...  1.05 us
    pallas_call x1, Pallas kernels, local(): pl.pallas_call(functools.partial(edge_kernel, n, m, y), out_shape=[shape(...  0.84 us
  transfers between devices with their start and end apart: 4, of which 1 were waited for; matrix products, arithmetic and copies ran while one was open for 0% of the time, Pallas kernels for 37%

profile of v1, /device:TPU:0, one launch (start us, length us, event | category | flops | bytes accessed | tf_op | source)
XLA Modules:
  0.0 34.2 jit_solution(17183495487107963281)
XLA Ops:
  0.6 0.0 copy-start.4
  0.6 0.0 copy-start.8
  0.7 0.0 copy-start.7
  0.7 0.0 copy-start.6
  1.4 0.8 %copy.13.table_ref = f32[8,4]{1,0:T(8,128)S(1)} copy(f32[8,4]{0,1:T(4,128)} %param.12) | data formatting | bytes 256 | tf_op args[3]
  2.1 2.0 %copy-done = f32[6,16,72,128]{3,2,1,0:T(8,128)S(1)} copy-done((f32[6,16,72,128]{3,2,1,0:T(8,128)S(1)}, f32[6,16,72,128]{3,2,1,0:T(8,128)}, u32[]{:S(2)}) %copy-start) | copy-done | bytes 3538968
  4.1 1.5 %copy-done.1 = f32[3,16,72,128]{3,2,1,0:T(8,128)S(1)} copy-done((f32[3,16,72,128]{3,2,1,0:T(8,128)S(1)}, f32[3,16,72,128]{3,2,1,0:T(8,128)}, u32[]{:S(2)}) %copy-start.1) | copy-done | bytes 1769496
  5.6 0.7 %copy-done.3 = s32[72]{0:T(128)S(1)} copy-done((s32[72]{0:T(128)S(1)}, s32[72]{0:T(128)}, u32[]{:S(2)}) %copy-start.3) | copy-done | bytes 312
  6.3 0.8 %edge_levels.1 = (f32[200,128]{1,0:T(8,128)S(1)}, f32[200,128]{1,0:T(8,128)S(1)}) custom-call(f32[3,16,72,128]{3,2,1,0:T(8,128)S(1)} %copy-done.1, f32[6,16,72,128]{3,2,1,0:T(8,128)S(1)} %copy-done, s32[72]{0:T(128)S(1)} %copy-done.3, f32[8,4]{1,0:T(8,128)S(1)} %copy.13.table_ref, s32[1]{0:T(128)S(6)} %copy.17.split_ref), custom_call_target="tpu_custom_call" | custom-call | tf_op jit(solution)/shard_map/edge_levels/pallas_call | solution.py:613
  7.1 3.1 %collective-permute-start = (f32[200,128]{1,0:T(8,128)S(1)}, f32[200,128]{1,0:T(8,128)S(1)}, u32[]{:S(2)}, u32[]{:S(2)}) collective-permute-start(f32[200,128]{1,0:T(8,128)S(1)} %get-tuple-element.9), channel_id=1, source_target_pairs={{0,1},{1,0},{2,3},{3,2},{4,5},{5,4},{6,7},{7,6},{8,9},{9,8},{10,11... | collective-permute-start | bytes 307208 | tf_op jit(solution)/shard_map/ppermute | solution.py:42
  10.2 0.0 collective-permute-start.1
  10.2 1.1 %level_coefficients.1.level_ref = f32[4,72,128]{2,1,0:T(8,128)S(1)} custom-call(s32[72]{0:T(128)S(1)} %copy-done.4, f32[8,4]{1,0:T(8,128)S(1)} %copy.13.table_ref, s32[1]{0:T(128)S(6)} %copy.17.split_ref), custom_call_target="tpu_custom_call" | custom-call | tf_op jit(solution)/shard_map/level_coefficients/pallas_call | solution.py:623
  11.3 1.8 %collective-permute-done.a_ref = f32[200,128]{1,0:T(8,128)S(1)} collective-permute-done((f32[200,128]{1,0:T(8,128)S(1)}, f32[200,128]{1,0:T(8,128)S(1)}, u32[]{:S(2)}, u32[]{:S(2)}) %collective-permute-start) | collective-permute-done | bytes 102432 | tf_op jit(solution)/shard_map/ppermute | solution.py:42
  13.1 0.0 collective-permute-done.1.b_ref
  13.1 0.0 copy-done.6
  13.1 0.0 copy-done.5
  13.1 0.0 copy-done.2
  13.1 2.4 %edge_planes.1 = (f32[448,128]{1,0:T(8,128)S(1)}, f32[448,128]{1,0:T(8,128)S(1)}, f32[4,88,128]{2,1,0:T(8,128)S(1)}) custom-call(f32[3,16,72,128]{3,2,1,0:T(8,128)S(1)} %copy-done.2, f32[6,16,72,128]{3,2,1,0:T(8,128)S(1)} %copy-done, f32[200,128]{1,0:T(8,128)S(1)} %collective-permute-done.a_ref, f32[200,128]{1,0:T(8,128)S(1)} %collective-permute-done.1.b_ref, ...), custom_call_target="tpu_custom_call" | custom-call | tf_op jit(solution)/shard_map/edge_planes/pallas_call | solution.py:631
  15.6 0.1 collective-permute-start.2
  15.6 3.0 %collective-permute-start.3 = (f32[448,128]{1,0:T(8,128)S(1)}, f32[448,128]{1,0:T(8,128)S(1)}, u32[]{:S(2)}, u32[]{:S(2)}) collective-permute-start(f32[448,128]{1,0:T(8,128)S(1)} %get-tuple-element.12.mb), channel_id=1, source_target_pairs={{0,1},{1,0},{2,3},{3,2},{4,8},{5,9},{6,10},{7,11},{8,4},{9,5},{10,... | collective-permute-start | bytes 688136 | tf_op jit(solution)/shard_map/ppermute | solution.py:42
  18.6 11.8 %both_steps.1 = (f32[3,16,72,128]{3,2,1,0:T(8,128)}, f32[6,16,72,128]{3,2,1,0:T(8,128)}) custom-call(f32[3,16,72,128]{3,2,1,0:T(8,128)S(1)} %copy-done.2, f32[6,16,72,128]{3,2,1,0:T(8,128)S(1)} %copy-done, f32[200,128]{1,0:T(8,128)S(1)} %collective-permute-done.a_ref, f32[200,128]{1,0:T(8,128)S(1)} %collective-permute-done.1.b_ref, ...), custom_call_target="tpu_custom_call" | custom-call | flops 20643840 | bytes 10616832 | tf_op jit(solution)/shard_map/both_steps/pallas_call | solution.py:650
  30.4 0.0 collective-permute-done.2.ra
  30.4 0.0 collective-permute-done.3.rb_
  30.4 3.8 %join_neighbours.1 = (f32[3,16,72,128]{3,2,1,0:T(8,128)}, f32[6,16,72,128]{3,2,1,0:T(8,128)}) custom-call(f32[448,128]{1,0:T(8,128)S(1)} %collective-permute-done.2.ra, f32[448,128]{1,0:T(8,128)S(1)} %collective-permute-done.3.rb_, f32[448,128]{1,0:T(8,128)S(1)} %get-tuple-element.11.ma, ...), custom_call_target="tpu_custom_call", output_to_operand_aliasing={{0}: (5, {}), {1}: (6, {})} | custom-call | tf_op jit(solution)/shard_map/join_neighbours/pallas_call | solution.py:670
  (8 shorter events, 0.0 us)
Async XLA Ops:
  0.6 9.6 %copy-start.4 = (s32[72]{0:T(128)S(1)}, s32[72]{0:T(128)}, u32[]{:S(2)}) copy-start(s32[72]{0:T(128)} %index_ref.3) | copy-start | bytes 868
  0.6 12.4 %copy-start.8 = (f32[16]{0:T(128)S(1)}, f32[16]{0:T(128)}, u32[]{:S(2)}) copy-start(f32[16]{0:T(128)} %amp.3) | copy-start | bytes 196
  0.7 12.4 %copy-start.7 = (s32[16]{0:T(128)S(1)}, s32[16]{0:T(128)}, u32[]{:S(2)}) copy-start(s32[16]{0:T(128)} %sy.3) | copy-start | bytes 196
  0.7 12.4 %copy-start.6 = (s32[16]{0:T(128)S(1)}, s32[16]{0:T(128)}, u32[]{:S(2)}) copy-start(s32[16]{0:T(128)} %sz.3) | copy-start | bytes 196
  0.7 12.4 %copy-start.5 = (s32[16]{0:T(128)S(1)}, s32[16]{0:T(128)}, u32[]{:S(2)}) copy-start(s32[16]{0:T(128)} %sx.3) | copy-start | bytes 196
  2.1 2.0 %copy-start = (f32[6,16,72,128]{3,2,1,0:T(8,128)S(1)}, f32[6,16,72,128]{3,2,1,0:T(8,128)}, u32[]{:S(2)}) copy-start(f32[6,16,72,128]{3,2,1,0:T(8,128)} %s_ref.5) | copy-start | bytes 10616836
  4.1 1.5 %copy-start.1 = (f32[3,16,72,128]{3,2,1,0:T(8,128)S(1)}, f32[3,16,72,128]{3,2,1,0:T(8,128)}, u32[]{:S(2)}) copy-start(f32[3,16,72,128]{3,2,1,0:T(8,128)} %v_ref.5) | copy-start | bytes 5308420
  5.6 0.7 %copy-start.3 = (s32[72]{0:T(128)S(1)}, s32[72]{0:T(128)}, u32[]{:S(2)}) copy-start(s32[72]{0:T(128)} %index_ref.3) | copy-start | bytes 868
  6.3 6.9 %copy-start.2 = (f32[3,16,72,128]{3,2,1,0:T(8,128)S(1)}, f32[3,16,72,128]{3,2,1,0:T(8,128)}, u32[]{:S(2)}) copy-start(f32[3,16,72,128]{3,2,1,0:T(8,128)} %v_ref.5) | copy-start | bytes 5308420
  7.1 6.0 %collective-permute-start = (f32[200,128]{1,0:T(8,128)S(1)}, f32[200,128]{1,0:T(8,128)S(1)}, u32[]{:S(2)}, u32[]{:S(2)}) collective-permute-start(f32[200,128]{1,0:T(8,128)S(1)} %get-tuple-element.9), channel_id=1, source_target_pairs={{0,1},{1,0},{2,3},{3,2},{4,5},{5,4},{6,7},{7,6},{8,9},{9,8},{10,11... | collective-permute-start | bytes 307208 | tf_op jit(solution)/shard_map/ppermute | solution.py:42
  10.2 2.9 %collective-permute-start.1 = (f32[200,128]{1,0:T(8,128)S(1)}, f32[200,128]{1,0:T(8,128)S(1)}, u32[]{:S(2)}, u32[]{:S(2)}) collective-permute-start(f32[200,128]{1,0:T(8,128)S(1)} %get-tuple-element.10), channel_id=1, source_target_pairs={{0,4},{1,2},{2,1},{3,7},{4,0},{5,6},{6,5},{7,3},{8,12},{9,10},{10,... | collective-permute-start | bytes 307208 | tf_op jit(solution)/shard_map/ppermute | solution.py:42
  15.6 14.8 %collective-permute-start.2 = (f32[448,128]{1,0:T(8,128)S(1)}, f32[448,128]{1,0:T(8,128)S(1)}, u32[]{:S(2)}, u32[]{:S(2)}) collective-permute-start(f32[448,128]{1,0:T(8,128)S(1)} %get-tuple-element.11.ma), channel_id=1, source_target_pairs={{0,4},{1,5},{2,6},{3,7},{4,0},{5,1},{6,2},{7,3},{8,12},{9,13},{10,... | collective-permute-start | bytes 688136 | tf_op jit(solution)/shard_map/ppermute | solution.py:42
  15.6 14.7 %collective-permute-start.3 = (f32[448,128]{1,0:T(8,128)S(1)}, f32[448,128]{1,0:T(8,128)S(1)}, u32[]{:S(2)}, u32[]{:S(2)}) collective-permute-start(f32[448,128]{1,0:T(8,128)S(1)} %get-tuple-element.12.mb), channel_id=1, source_target_pairs={{0,1},{1,0},{2,3},{3,2},{4,8},{5,9},{6,10},{7,11},{8,4},{9,5},{10,... | collective-permute-start | bytes 688136 | tf_op jit(solution)/shard_map/ppermute | solution.py:42

commit v2 on v1

v2 whole, which is shorter than its diff:
```python
import functools

import jax
import jax.numpy as jnp
from jax import lax
from jax.experimental import pallas as pl
from jax.experimental.pallas import tpu as pltpu
from jax.sharding import PartitionSpec as P

courant = 0.2
wavelet = (1.0, -0.5)
pair_table = ((0, 3, 4), (3, 1, 5), (4, 5, 2))
front = (0, 3, 4)
top = (3, 1, 5)
PAD = 8
ANY = pl.BlockSpec(memory_space=pl.ANY)
HBM = pl.BlockSpec(memory_space=pltpu.HBM)
VMEM = pl.BlockSpec(memory_space=pltpu.VMEM)
SMEM = pl.BlockSpec(memory_space=pltpu.SMEM)


def swap_pairs(rows, cols, along, odd):
    out = []
    for i in range(rows):
        for j in range(cols):
            at, size = (i, rows) if along == 0 else (j, cols)
            if not odd:
                to = at ^ 1
            elif at in (0, size - 1):
                to = None
            else:
                to = at + 1 if at % 2 else at - 1
            if along == 0:
                target = (i, j ^ 1) if to is None else (to, j)
            else:
                target = (i ^ 1, j) if to is None else (i, to)
            out.append((i * cols + j, target[0] * cols + target[1]))
    return out


def swap(block, along, odd):
    rows, cols = lax.axis_size("horiz"), lax.axis_size("vert")
    return lax.ppermute(block, ("horiz", "vert"), swap_pairs(rows, cols, along, odd))


def lane_of(shape):
    return lax.broadcasted_iota(jnp.int32, shape, len(shape) - 1)


def back_lane(a):
    moved = pltpu.roll(a, 1, 1)
    return a - jnp.where(lane_of(a.shape) == 0, 0.0, moved)


def fore_lane(a):
    last = a.shape[-1] - 1
    moved = pltpu.roll(a, last, 1)
    return jnp.where(lane_of(a.shape) == last, 0.0, moved) - a


def velocity_tile(s_at, v_at, rb, dq):
    out = []
    for k in range(3):
        a, b, c = pair_table[k]
        total = (s_at(a, 0, 0) - s_at(a, -1, 0)) + (s_at(b, 0, 0) - s_at(b, 0, -1))
        total = total + back_lane(s_at(c, 0, 0))
        out.append(dq * v_at(k) + rb * total)
    return out


def strain(v_at):
    grads = []
    for i in range(3):
        here = v_at(i, 0, 0)
        grads.append([v_at(i, 1, 0) - here, v_at(i, 0, 1) - here, fore_lane(here)])
    return grads


def stress_terms(g, rl, rm, wanted=range(6)):
    out = {}
    if any(c < 3 for c in wanted):
        spread = rl * (g[0][0] + g[1][1] + g[2][2])
    for c in wanted:
        if c < 3:
            out[c] = spread + 2.0 * rm * g[c][c]
        else:
            i, j = ((0, 1), (0, 2), (1, 2))[c - 3]
            out[c] = rm * (g[i][j] + g[j][i])
    return out


def memo(fn):
    seen = {}

    def call(*key):
        if key not in seen:
            seen[key] = fn(*key)
        return seen[key]

    return call


MSG = 200


def level_scalars(index_ref, table_ref, z):
    kind = index_ref[z]
    return (
        courant * table_ref[0, kind],
        1.0 - courant * table_ref[3, kind],
        courant * table_ref[1, kind],
        courant * table_ref[2, kind],
    )


def edge_kernel(
    n, m, y, v_ref, s_ref, index, table, out_a, out_b, coef, low, high, index_ref, table_ref, sems
):
    vert = lax.axis_index("vert")
    odd = vert % 2 == 1
    copies = []
    for at, (buf, start) in enumerate(((low, 0), (high, m - 8))):
        copies.append(
            pltpu.make_async_copy(s_ref.at[:, :, pl.ds(start, 8), :], buf.at[pl.ds(0, 6), pl.ds(1, n)], sems.at[2 * at])
        )
        copies.append(
            pltpu.make_async_copy(
                v_ref.at[:, :, pl.ds(start, 8), :], buf.at[pl.ds(6, 3), pl.ds(1, n)], sems.at[2 * at + 1]
            )
        )
    scalars = [
        pltpu.make_async_copy(src, dst, sems.at[4 + i])
        for i, (src, dst) in enumerate(((index, index_ref), (table, table_ref)))
    ]
    for copy in scalars + copies:
        copy.start()
    for buf in (low, high):
        for f in front:
            buf[f, 0] = jnp.zeros((8, y), jnp.float32)
    for copy in scalars:
        copy.wait()
    at_first = level_scalars(index_ref, table_ref, 0)
    at_second = level_scalars(index_ref, table_ref, 1)
    at_last = level_scalars(index_ref, table_ref, m - 1)

    def level(z, carry):
        for c, value in enumerate(level_scalars(index_ref, table_ref, z)):
            coef[c, pl.ds(PAD + z, 1), :] = jnp.full((1, y), value, jnp.float32)
        return carry

    lax.fori_loop(0, m, level, 0, unroll=8)
    for copy in copies:
        copy.wait()
    low2 = low.reshape(9 * (n + 1) * 8, y)
    high2 = high.reshape(9 * (n + 1) * 8, y)

    def row(buf, f, z, dx=0):
        return buf[pl.Slice((f * (n + 1) + 1 + dx) * 8 + z, n, 8), :]

    def moved(buf, z, scal):
        return velocity_tile(
            memo(lambda f, dx, dz: row(buf, f, z + dz, dx)), lambda k: row(buf, 6 + k, z), scal[0], scal[1]
        )

    up = [row(high2, f, 7) for f in range(6)] + moved(high2, 7, at_last)
    down = [row(low2, f, 0) for f in range(9)] + moved(low2, 1, at_second)

    def put(at, rows, up_value, down_value):
        out_a[pl.ds(at, rows), :] = jnp.where(odd, down_value, up_value)
        out_b[pl.ds(at, rows), :] = jnp.where(odd, up_value, down_value)

    for f in range(12):
        put(f * n, n, up[f] if f < 9 else down[f], down[f])
    base = 12 * n
    for c in range(4):
        splat = [jnp.full((1, y), a[c], jnp.float32) for a in (at_last, at_first)]
        put(base + c, 1, *splat)
    ahead = jnp.full((1, y), at_second[0], jnp.float32)
    put(base + 4, 1, ahead, ahead)
    for c, f in enumerate(front):
        corner = low[f, n, pl.ds(1, 1), :]
        put(base + 5 + c, 1, corner, corner)


EDGE_MIB, LOAD_MIB, SMALL_MIB = 16, 16, 16
GROUP = 4


def load_kernel(n, m, y, v_ref, s_ref, coef_in, split, vb, sb, coef, sems):
    del coef_in
    body = pl.ds(PAD, m)

    def fetch(g):
        return (
            pltpu.make_async_copy(
                s_ref.at[:, pl.ds(GROUP * g, GROUP)], sb.at[:, pl.ds(GROUP * g + 1, GROUP), body], sems.at[0, g]
            ),
            pltpu.make_async_copy(
                v_ref.at[:, pl.ds(GROUP * g, GROUP)], vb.at[:, pl.ds(GROUP * g + 1, GROUP), body], sems.at[1, g]
            ),
        )

    for g in range(n // GROUP):
        for copy in fetch(g):
            copy.start()
    for f in front:
        sb[f, 0] = jnp.zeros((m + 16, y), jnp.float32)
    for k in range(3):
        vb[k, n + 1] = jnp.zeros((m + 16, y), jnp.float32)
    high = m + 16
    s2 = sb.reshape(6 * (n + 1) * high, y)
    for f in top:
        s2[pl.Slice((f * (n + 1) + 1) * high + PAD - 1, n, high), :] = jnp.zeros((n, y), jnp.float32)

    lowest, first = PAD - 1, PAD + m
    coef[3, pl.ds(lowest, 1), :] = jnp.ones((1, y), jnp.float32)
    coef[3, pl.ds(first, 1), :] = jnp.ones((1, y), jnp.float32)
    start = split[0] - lax.axis_index("vert") * m
    for r, size in [(PAD + 8 * t, 8) for t in range(m // 8)] + [(lowest, 1), (first, 1)]:
        level = r - PAD + lax.broadcasted_iota(jnp.int32, (size, y), 0)
        at = pl.ds(r, size)
        coef[3, at, :] = jnp.where(level >= start, coef[3, at, :], 0.0)

    def advance(g, carry):
        for copy in fetch(g):
            copy.wait()
        for p in range(GROUP):
            x = GROUP * g + p
            for t in range(m // 8):
                r = PAD + 8 * t
                new = velocity_tile(
                    memo(lambda f, dx, dz: sb[f, x + 1 + dx, pl.ds(r + dz, 8), :]),
                    lambda k: vb[k, x + 1, pl.ds(r, 8), :],
                    coef[0, pl.ds(r, 8), :],
                    coef[1, pl.ds(r, 8), :],
                )
                for k in range(3):
                    vb[k, x + 1, pl.ds(r, 8), :] = new[k]
        return carry

    lax.fori_loop(0, n // GROUP, advance, 0)


def fetch_sources(refs, held, sems):
    copies = [pltpu.make_async_copy(src, dst, sems.at[i]) for i, (src, dst) in enumerate(zip(refs, held))]
    for copy in copies:
        copy.start()
    return copies


def add_sources(add_row, plane_of, z_low, z_high, scale, x_at, z_at, src):
    sx, sz, sy, amp = src

    def body(i, carry):
        x, z = sx[i] - x_at, sz[i] - z_at

        @pl.when(plane_of(x) & (z >= z_low) & (z < z_high))
        def _():
            lane = lane_of((1, 128))
            add_row(x, z, jnp.where(lane == sy[i], scale * amp[i], 0.0))

        return carry

    lax.fori_loop(0, sx.shape[0], body, 0)


def plane_kernel(
    n, m, y, got_a, got_b, vb, sb, coef_in, *refs
):
    sources, (out_a, out_b, below, above, coef), scratch = refs[:4], refs[4:9], refs[9:]
    sl, vl, sr, vr, msg, sx, sz, sy, amp, sems = scratch
    del coef_in
    horiz, vert = lax.axis_index("horiz"), lax.axis_index("vert")
    fetched = fetch_sources(sources, (sx, sz, sy, amp), sems)
    odd = vert % 2 == 1
    has_below = jnp.where(vert > 0, 1.0, 0.0)
    has_above = jnp.where(vert < lax.axis_size("vert") - 1, 1.0, 0.0)
    for t in range(MSG // 8):
        at = pl.ds(8 * t, 8)
        a, b = got_a[at, :], got_b[at, :]
        below[at, :] = has_below * jnp.where(odd, a, b)
        above[at, :] = has_above * jnp.where(odd, b, a)
    lowest, first, second = PAD - 1, PAD + m, PAD + m + 1
    base = 12 * n
    for c in range(4):
        for r, side in ((lowest, below), (first, above)):
            value = side[pl.ds(base + c, 1), :]
            coef[c, pl.ds(r, 1), :] = value * coef[c, pl.ds(r, 1), :] if c == 3 else value
    coef[0, pl.ds(second, 1), :] = above[pl.ds(base + 4, 1), :]

    tiles = [(PAD + 8 * t, 8) for t in range(m // 8)]
    right, left = horiz % 2, 1 - horiz % 2
    tail = 6 * m

    def cs(c, r, size):
        return coef[c, pl.ds(r, size), :]

    def from_below(f, x):
        return below[pl.ds(f * n + x, 1), :]

    def from_above(f, x):
        return above[pl.ds(f * n + x, 1), :]

    for x, buf, at in ((0, vl, 0), (1, vl, 1), (n - 1, vr, 0)):
        for k in range(3):
            for r, size in tiles:
                buf[k, at, pl.ds(r, size), :] = vb[k, x + 1, pl.ds(r, size), :]
            line = pl.ds(PAD, 1)
            buf[k, at, line, :] = vb[k, x + 1, line, :] - cs(0, PAD, 1) * from_below(top[k], x)
            buf[k, at, pl.ds(lowest, 1), :] = from_below(6 + k, x)
            buf[k, at, pl.ds(second, 1), :] = from_above(9 + k, x)

        def beyond(f, dx, dz):
            if dz:
                return sb[f, x + 1, pl.ds(first - 1, 1), :]
            if x + dx < 0:
                return jnp.zeros((1, y), jnp.float32)
            return from_above(f, x + dx)

        new = velocity_tile(memo(beyond), lambda k: from_above(6 + k, x), cs(0, first, 1), cs(1, first, 1))
        for k in range(3):
            buf[k, at, pl.ds(first, 1), :] = new[k]

    def stress_rows(f, x, r, size):
        if r < PAD:
            return from_below(f, x)
        if r >= first:
            return from_above(f, x)
        return sb[f, x + 1, pl.ds(r, size), :]

    def load(out, v_buf, x, r, size, wanted, ahead):
        def at(k, dx, dz):
            if dx and not ahead:
                return 0.0
            return v_buf[k, dx, pl.ds(r + dz, size), :]

        terms = stress_terms(strain(memo(at)), cs(2, r, size), cs(3, r, size), wanted)
        for c in wanted:
            out[c, pl.ds(r, size), :] = stress_rows(c, x, r, size) + terms[c]

    for r, size in tiles + [(first, 1)]:
        load(sr, vr, n - 1, r, size, front, False)
    load(sl, vl, 0, lowest, 1, top, True)
    for r, size in tiles:
        load(sl, vl, 0, r, size, range(6), True)
    for c, f in enumerate(front):
        for r, size in tiles:
            msg[right, pl.ds(c * m + r - PAD, size), :] = sb[f, n, pl.ds(r, size), :]
            msg[left, pl.ds(c * m + r - PAD, size), :] = vl[c, 0, pl.ds(r, size), :]
        msg[right, pl.ds(tail + c, 1), :] = from_below(f, n - 1)
        msg[right, pl.ds(tail + 3 + c, 1), :] = from_above(f, n - 1)
        msg[right, pl.ds(tail + 6 + c, 1), :] = above[pl.ds(base + 5 + c, 1), :]
        msg[left, pl.ds(tail + c, 1), :] = vl[c, 0, pl.ds(lowest, 1), :]
        msg[left, pl.ds(tail + 3 + c, 1), :] = vl[c, 0, pl.ds(first, 1), :]

    for copy in fetched:
        copy.wait()

    def add(x, z, row):
        at = pl.ds(PAD + z, 1)

        @pl.when(x == 0)
        def _():
            for c in range(3):
                sl[c, at, :] = sl[c, at, :] + row

        @pl.when(x == n - 1)
        def _():
            sr[0, at, :] = sr[0, at, :] + row

    add_sources(
        add, lambda x: (x == 0) | (x == n - 1), -1, m + 1, courant * wavelet[0], horiz * n, vert * m, (sx, sz, sy, amp)
    )
    for c, f in enumerate(front):
        for r, size in tiles:
            msg[right, pl.ds((3 + c) * m + r - PAD, size), :] = sr[f, pl.ds(r, size), :]
        msg[right, pl.ds(tail + 9 + c, 1), :] = sr[f, pl.ds(first, 1), :]
    for r, size in tiles:
        new = velocity_tile(
            memo(lambda f, dx, dz: 0.0 if dx else sl[f, pl.ds(r + dz, size), :]),
            lambda k: vl[k, 0, pl.ds(r, size), :],
            cs(0, r, size),
            cs(1, r, size),
        )
        for k in range(3):
            msg[left, pl.ds((3 + k) * m + r - PAD, size), :] = new[k]
    for t in range((6 * m + 16) // 8):
        at = pl.ds(8 * t, 8)
        out_a[at, :] = msg[0, at, :]
        out_b[at, :] = msg[1, at, :]


def rest_kernel(n, m, y, v_in, s_in, below, above, coef, *refs):
    sources, (vb, sb, out_v, out_s), scratch = refs[:4], refs[4:8], refs[8:]
    sx, sz, sy, amp, near_x, near_z, near_y, near_amp, small, sems = scratch
    del v_in, s_in
    horiz, vert = lax.axis_index("horiz"), lax.axis_index("vert")
    fetched = fetch_sources(sources, (sx, sz, sy, amp), small)
    body = pl.ds(PAD, m)
    lowest, first, second = PAD - 1, PAD + m, PAD + m + 1
    high = m + 16
    s2 = sb.reshape(6 * (n + 1) * high, y)
    v2 = vb.reshape(3 * (n + 2) * high, y)
    tiles = [(PAD + 8 * t, 8) for t in range(m // 8)]

    def cs(c, r, size):
        return coef[c, pl.ds(r, size), :]

    def s_line(f, r):
        return pl.Slice((f * (n + 1) + 1) * high + r, n, high)

    def v_line(k, r):
        return pl.Slice((k * (n + 2) + 1) * high + r, n, high)

    def beyond(f, dx, dz):
        if dz:
            return s2[s_line(f, first - 1), :]
        here = above[pl.ds(f * n, n), :]
        if dx:
            rows = lax.broadcasted_iota(jnp.int32, (n, y), 0)
            return jnp.where(rows == 0, 0.0, pltpu.roll(here, 1, 0))
        return here

    new = velocity_tile(
        memo(beyond), lambda k: above[pl.ds((6 + k) * n, n), :], cs(0, first, 1), cs(1, first, 1)
    )
    for k in range(3):
        v2[v_line(k, first), :] = new[k]
        v2[v_line(k, lowest), :] = below[pl.ds((6 + k) * n, n), :]
        v2[v_line(k, second), :] = above[pl.ds((9 + k) * n, n), :]
        v2[v_line(k, PAD), :] = v2[v_line(k, PAD), :] - cs(0, PAD, 1) * below[pl.ds(top[k] * n, n), :]
    for f in range(6):
        s2[s_line(f, lowest), :] = below[pl.ds(f * n, n), :]
        s2[s_line(f, first), :] = above[pl.ds(f * n, n), :]

    def move(x):
        for r, size in tiles + [(first, 1)]:
            new = velocity_tile(
                memo(lambda f, dx, dz: sb[f, x + 1 + dx, pl.ds(r + dz, size), :]),
                lambda k: vb[k, x + 1, pl.ds(r, size), :],
                cs(0, r, size),
                cs(1, r, size),
            )
            for k in range(3):
                vb[k, x + 1, pl.ds(r, size), :] = new[k]

    def load(x, step):
        parts = [(r, size, range(6)) for r, size in tiles]
        if step == 0:
            parts += [(lowest, 1, top), (first, 1, range(6))]
        for r, size, wanted in parts:
            g = strain(memo(lambda k, dx, dz: vb[k, x + 1 + dx, pl.ds(r + dz, size), :]))
            terms = stress_terms(g, cs(2, r, size), cs(3, r, size), wanted)
            for c in wanted:
                sb[c, x + 1, pl.ds(r, size), :] = sb[c, x + 1, pl.ds(r, size), :] + terms[c]

    for copy in fetched:
        copy.wait()
    found = jnp.int32(0)
    for i in range(sx.shape[0]):
        x, z = sx[i] - horiz * n, sz[i] - vert * m
        near_x[found], near_z[found], near_y[found], near_amp[found] = x, z, sy[i], amp[i]
        found = found + ((x >= 0) & (x < n) & (z >= -1) & (z <= m)).astype(jnp.int32)

    def add_near(step, x_low, x_high, z_low, z_high):
        def add(j, carry):
            x, z = near_x[j], near_z[j]

            @pl.when((x >= x_low) & (x < x_high) & (z >= z_low) & (z < z_high))
            def _():
                row = jnp.where(lane_of((1, y)) == near_y[j], courant * wavelet[step] * near_amp[j], 0.0)
                at = pl.ds(PAD + z, 1)
                for c in range(3):
                    sb[c, x + 1, at, :] = sb[c, x + 1, at, :] + row

            return carry

        lax.fori_loop(0, found, add, 0)

    def v_off(x):
        return pltpu.make_async_copy(vb.at[:, x + 1, body], out_v.at[:, x], sems.at[0, x])

    def s_off(x):
        return pltpu.make_async_copy(sb.at[:, x + 1, body], out_s.at[:, x], sems.at[1, x])

    def send(off, x, end):
        @pl.when((x >= 2) & (x < end))
        def _():
            off(x).start()

    add_near(0, 0, n, -1, m + 1)

    def advance(g, carry):
        x = GROUP * g
        for p in range(GROUP):
            load(x + p, 0)
        for p in range(GROUP):
            move(x + p)
        for p in range(GROUP):
            send(v_off, x + p, n - 2)
        for p in range(-1, GROUP - 1):
            load(x + p, 1)
        add_near(1, x - 1, x + GROUP - 1, 0, m)
        for p in range(-1, GROUP - 1):
            send(s_off, x + p, n - 1 - GROUP)
        return carry

    lax.fori_loop(0, n // GROUP, advance, 0)
    load(n - 1, 1)
    add_near(1, n - 1, n, 0, m)

    def finish(x, carry):
        v_off(x).wait()

        @pl.when(x < n - 1 - GROUP)
        def _():
            s_off(x).wait()

        return carry

    lax.fori_loop(2, n - 2, finish, 0)


def join_kernel(n, m, y, next_a, next_b, own_a, own_b, coef, vb, sb, v_in, s_in, v_out, s_out, *scratch):
    wa, da, ds, dv, dw, qb, db, es, ev, vn, v0, v1, s0, s1, sems = scratch
    del v_in, s_in
    horiz = lax.axis_index("horiz")
    even = horiz % 2 == 0
    has_left = jnp.where(horiz > 0, 1.0, 0.0)
    has_right = jnp.where(horiz < lax.axis_size("horiz") - 1, 1.0, 0.0)
    lowest, first, second = PAD - 1, PAD + m, PAD + m + 1
    tail = 6 * m
    tiles = [(PAD + 8 * t, 8) for t in range(m // 8)]

    def cs(c, r, size):
        return coef[c, pl.ds(r, size), :]

    pick = {"right": (next_a, next_b), "left": (next_b, next_a), "own right": (own_a, own_b), "own left": (own_b, own_a)}

    def rows_of(which, at, size):
        a, b = pick[which]
        return jnp.where(even, a[pl.ds(at, size), :], b[pl.ds(at, size), :])

    def msg(which, c, r, size):
        return rows_of(which, c * m + r - PAD, size)

    def end(which, at):
        return rows_of(which, tail + at, 1)

    for k in range(3):
        rows = [(r, size, msg("left", k, r, size)) for r, size in tiles]
        rows += [(r, 1, end("left", at + k)) for r, at in ((lowest, 0), (first, 3), (second, 6))]
        for r, size, value in rows:
            da[k, pl.ds(r, size), :] = -(has_left * cs(0, r, size)) * value
        rows = [(r, size, msg("left", 3 + k, r, size), msg("own left", k, r, size)) for r, size in tiles]
        rows += [(first, 1, end("left", 9 + k), end("own left", 3 + k))]
        for r, size, value, own in rows:
            gain = cs(3, r, size) if k else cs(2, r, size) + 2.0 * cs(3, r, size)
            wa[k, pl.ds(r, size), :] = has_left * (value + gain * (own + da[k, pl.ds(r, size), :]))
        rows = [(r, size, msg("own right", k, r, size), msg("right", k, r, size)) for r, size in tiles]
        rows += [(r, 1, end("own right", at + k), end("right", at + k)) for r, at in ((lowest, 0), (first, 3))]
        for r, size, value, other in rows:
            change = -(has_right * cs(0, r, size)) * value
            db[k, pl.ds(r, size), :] = change
            qb[k, pl.ds(r, size), :] = has_right * other + change

    def strain_of(buf, r, size, ahead=None):
        grads = []
        for i in range(3):
            here = buf[i, pl.ds(r, size), :]
            beyond = -here if ahead is None else ahead[i, pl.ds(r, size), :] - here
            grads.append([beyond, buf[i, pl.ds(r + 1, size), :] - here, fore_lane(here)])
        return grads

    for out, src, ends in ((ds, da, (lowest, first)), (es, db, (lowest,))):
        parts = [(r, size, range(6)) for r, size in tiles]
        parts += [(r, 1, top if r == lowest else range(6)) for r in ends]
        for r, size, wanted in parts:
            terms = stress_terms(strain_of(src, r, size), cs(2, r, size), cs(3, r, size), wanted)
            for c in wanted:
                out[c, pl.ds(r, size), :] = terms[c]

    for r, size in tiles + [(first, 1)]:
        rb, dq = cs(0, r, size), cs(1, r, size)
        for k in range(3):
            a, b, c = pair_table[k]
            here = ds[a, pl.ds(r, size), :]
            total = here - wa[k, pl.ds(r, size), :]
            total = total + (ds[b, pl.ds(r, size), :] - ds[b, pl.ds(r - 1, size), :])
            total = total + back_lane(ds[c, pl.ds(r, size), :])
            dv[k, pl.ds(r, size), :] = dq * da[k, pl.ds(r, size), :] + rb * total
            dw[k, pl.ds(r, size), :] = -rb * here

    def last_stress(c, r, size):
        q = qb[0 if c < 3 else c - 2, pl.ds(r, size), :]
        if c == 0:
            return (cs(2, r, size) + 2.0 * cs(3, r, size)) * q
        return (cs(2, r, size) if c < 3 else cs(3, r, size)) * q

    for r, size in tiles + [(first, 1)]:
        rb, dq = cs(0, r, size), cs(1, r, size)
        full = [last_stress(c, r, size) for c in range(5)]
        totals = [
            full[0] + (full[3] - last_stress(3, r - 1, size)) + back_lane(full[4]),
            full[3] + (full[1] - last_stress(1, r - 1, size)),
            full[4] + back_lane(full[2]),
        ]
        for k in range(3):
            ev[k, pl.ds(r, size), :] = rb * totals[k]
        if r == first:
            continue
        for k in range(3):
            a, b, c = pair_table[k]
            total = es[a, pl.ds(r, size), :] - (msg("own right", 3 + k, r, size) + full[a])
            total = total + (es[b, pl.ds(r, size), :] - es[b, pl.ds(r - 1, size), :])
            total = total + back_lane(es[c, pl.ds(r, size), :])
            change = dq * db[k, pl.ds(r, size), :] + rb * total
            vn[k, pl.ds(r, size), :] = has_right * (msg("right", 3 + k, r, size) + change)

    def put(buf, dst, x, i):
        copy = pltpu.make_async_copy(buf, dst.at[:, x], sems.at[i])
        copy.start()
        return copy

    rest = pltpu.make_async_copy(
        sb.at[:, pl.ds(n - GROUP, GROUP - 1), pl.ds(PAD, m)], s_out.at[:, pl.ds(n - 1 - GROUP, GROUP - 1)], sems.at[8]
    )
    rest.start()
    copies = [rest]
    for buf, x, change in ((v0.at[:, 0], 0, dv), (v0.at[:, 1], 1, dw), (v1.at[:, 0], n - 1, ev), (v1.at[:, 1], n - 2, None)):
        for r, size in tiles:
            out, at = pl.ds(r - PAD, size), pl.ds(r, size)
            for k in range(3):
                old = vb[k, x + 1, at, :]
                buf[k, out, :] = old if change is None else old + change[k, at, :]
        copies.append(put(buf, v_out, x, len(copies) - 1))
    for buf, x, src, ahead, more in (
        (s0.at[:, 0], 0, dv, dw, lambda c, r: ds[c, pl.ds(r, 8), :]),
        (s0.at[:, 1], 1, dw, None, None),
        (s1.at[:, 0], n - 1, ev, vn, lambda c, r: None if c == 5 else last_stress(c, r, 8)),
    ):
        for r, size in tiles:
            out, at = pl.ds(r - PAD, size), pl.ds(r, size)
            terms = stress_terms(strain_of(src, r, size, ahead), cs(2, r, size), cs(3, r, size))
            for c in range(6):
                extra = None if more is None else more(c, r)
                term = terms[c] if extra is None else terms[c] + extra
                buf[c, out, :] = sb[c, x + 1, at, :] + term
        copies.append(put(buf, s_out, x, len(copies) - 1))
    for r, size in tiles:
        out, at = pl.ds(r - PAD, size), pl.ds(r, size)
        rl, rm = cs(2, r, size), cs(3, r, size)
        e = [ev[k, at, :] for k in range(3)]
        spread = rl * e[0]
        for c, term in enumerate((spread + 2.0 * rm * e[0], spread, spread, rm * e[1], rm * e[2], None)):
            old = sb[c, n - 1, at, :]
            s1[c, 1, out, :] = old if term is None else old + term
    copies.append(put(s1.at[:, 1], s_out, n - 2, len(copies) - 1))
    for copy in copies:
        copy.wait()


def local(velocity, stress, index, table, split, source_x, source_z, source_y, amplitude):
    _, n, m, y = velocity.shape
    f32, i32 = jnp.float32, jnp.int32
    high = m + 16
    dma = pltpu.SemaphoreType.DMA
    sources = (source_x, source_z, source_y, amplitude)
    held = [pltpu.SMEM(a.shape, a.dtype) for a in sources]
    near = [pltpu.SMEM((a.shape[0] + 1,), a.dtype) for a in sources]
    table = table.T
    materials = [pltpu.SMEM((m,), i32), pltpu.SMEM(table.shape, f32)]

    def shape(*dims):
        return jax.ShapeDtypeStruct(dims, f32)

    def kept(*dims):
        return pltpu.VMEM(dims, f32)

    def outside(*dims):
        return pltpu.HBM(dims, f32)

    def room(mib):
        return pltpu.CompilerParams(vmem_limit_bytes=mib * 1024 * 1024)

    def cost(flops, moved):
        return pl.CostEstimate(flops=flops, bytes_accessed=moved, transcendentals=0)

    padded_v, padded_s = kept(3, n + 2, high, y), kept(6, n + 1, high, y)
    edge_a, edge_b, coef = pl.pallas_call(
        functools.partial(edge_kernel, n, m, y),
        out_shape=[kept(MSG, y)] * 2 + [kept(4, high, y)],
        in_specs=[HBM] * 4,
        out_specs=[VMEM] * 3,
        scratch_shapes=[pltpu.VMEM((9, n + 1, 8, y), f32)] * 2 + materials + [dma((6,))],
        compiler_params=room(EDGE_MIB),
        name="edge_levels",
    )(*[pltpu.with_memory_space_constraint(a, pltpu.HBM) for a in (velocity, stress, index, table)])
    got_a, got_b = swap(edge_a, 1, False), swap(edge_b, 1, True)
    split, edge_a = lax.optimization_barrier((split, edge_a))
    vb, sb, coef = pl.pallas_call(
        functools.partial(load_kernel, n, m, y),
        out_shape=[padded_v, padded_s, kept(4, high, y)],
        in_specs=[ANY, ANY, VMEM, SMEM],
        out_specs=[VMEM] * 3,
        input_output_aliases={2: 2},
        scratch_shapes=[dma((2, n // GROUP))],
        compiler_params=room(LOAD_MIB),
        cost_estimate=cost(30 * n * m * y, 4 * 9 * n * m * y),
        name="load_block",
    )(velocity, stress, coef, split)
    plane_a, plane_b, below, above, coef = pl.pallas_call(
        functools.partial(plane_kernel, n, m, y),
        out_shape=[kept(6 * m + 16, y)] * 2 + [kept(MSG, y)] * 2 + [kept(4, high, y)],
        in_specs=[VMEM] * 5 + [ANY] * 4,
        out_specs=[VMEM] * 5,
        input_output_aliases={4: 4},
        scratch_shapes=[
            pltpu.VMEM((6, high, y), f32),
            pltpu.VMEM((3, 2, high, y), f32),
            pltpu.VMEM((6, high, y), f32),
            pltpu.VMEM((3, 1, high, y), f32),
            pltpu.VMEM((2, 6 * m + 16, y), f32),
            *held,
            dma((4,)),
        ],
        compiler_params=room(SMALL_MIB),
        name="edge_planes",
    )(got_a, got_b, vb, sb, coef, *sources)
    next_a, next_b = swap(plane_a, 0, False), swap(plane_b, 0, True)
    vb, sb, v_own, s_own = pl.pallas_call(
        functools.partial(rest_kernel, n, m, y),
        out_shape=[padded_v, padded_s, outside(*velocity.shape), outside(*stress.shape)],
        in_specs=[VMEM] * 5 + [ANY] * 4,
        out_specs=[VMEM, VMEM, HBM, HBM],
        input_output_aliases={0: 0, 1: 1},
        scratch_shapes=[*held, *near, dma((4,)), dma((2, n))],
        compiler_params=room(SMALL_MIB),
        cost_estimate=cost(110 * n * m * y, 4 * 9 * n * m * y),
        name="both_steps",
    )(vb, sb, below, above, coef, *sources)
    plane = pltpu.VMEM((3, high, y), f32)
    plane6 = pltpu.VMEM((6, high, y), f32)
    return pl.pallas_call(
        functools.partial(join_kernel, n, m, y),
        out_shape=[outside(*velocity.shape), outside(*stress.shape)],
        in_specs=[VMEM] * 7 + [HBM] * 2,
        out_specs=[HBM, HBM],
        input_output_aliases={7: 0, 8: 1},
        scratch_shapes=[plane, plane, plane6, plane, plane, plane, plane, plane6, plane, plane]
        + [pltpu.VMEM((3, 2, m, y), f32)] * 2
        + [pltpu.VMEM((6, 2, m, y), f32)] * 2
        + [dma((9,))],
        compiler_params=room(SMALL_MIB),
        name="join_neighbours",
    )(next_a, next_b, plane_a, plane_b, coef, vb, sb, v_own, s_own)


def solution(mesh):
    block = P("member", "horiz", "vert", None)
    return jax.shard_map(
        local,
        mesh=mesh,
        in_specs=(block, block, P("vert"), P(), P(), P(), P(), P(), P("member")),
        out_specs=(block, block),
        check_vma=False,
    )
```

time: 34.5 us -> 19.3 us (0.56)
  Pallas kernels: 19.9 us -> 10.7 us
  local copies, waits for them, and re-layouts: 4.91 us -> 0.03 us
  waiting for transfers between devices: 1.82 us -> 0.8 us
    pallas_call x5, Pallas kernels: 19.9 us -> 10.7 us  [the longest x1 4.87 us: local(): pl.pallas_call(functools.partial(rest_kernel, n, m, y), out_shape=[padded...]
    unnamed x19 -> x12, local copies, waits for them, and re-layouts: 4.91 us -> 0.03 us
    ppermute x4, waiting for transfers between devices: 1.82 us -> 0.8 us  [swap(): lax.ppermute(block, ('horiz', 'vert'), swap_pairs(rows, cols, along, odd))]
  transfers between devices with their start and end apart: 4 -> 4, of which waited for: 1 -> 1; matrix products, arithmetic and copies ran while one was open for 0% -> 0% of each run, Pallas kernels for 37% -> 33%
where the time goes in v2:
time: 19.3 us; the launch traced here: 19.1 us
  Pallas kernels  10.7 us (55%)
  starting transfers between devices  6.12 us (32%)
  between operations  1.42 us (7%)
  waiting for transfers between devices  0.8 us (4%)
    ppermute x4, starting transfers between devices, swap(): lax.ppermute(block, ('horiz', 'vert'), swap_pairs(rows, cols, along, odd))  6.12 us
    pallas_call x1, Pallas kernels, local(): pl.pallas_call(functools.partial(rest_kernel, n, m, y), out_shape=[padded...  4.87 us
    pallas_call x1, Pallas kernels, local(): pl.pallas_call(functools.partial(join_kernel, n, m, y), out_shape=[outsid...  1.72 us
    pallas_call x1, Pallas kernels, local(): pl.pallas_call(functools.partial(edge_kernel, n, m, y), out_shape=[kept(M...  1.59 us
    pallas_call x1, Pallas kernels, local(): pl.pallas_call(functools.partial(load_kernel, n, m, y), out_shape=[padded...  1.41 us
    pallas_call x1, Pallas kernels, local(): pl.pallas_call(functools.partial(plane_kernel, n, m, y), out_shape=[kept(...  1.16 us
    ppermute x4, waiting for transfers between devices, swap(): lax.ppermute(block, ('horiz', 'vert'), swap_pairs(rows, cols, along, odd))  0.8 us
  transfers between devices with their start and end apart: 4, of which 1 were waited for; matrix products, arithmetic and copies ran while one was open for 0% of the time, Pallas kernels for 33%

profile of v2, /device:TPU:0, one launch (start us, length us, event | category | flops | bytes accessed | tf_op | source)
XLA Modules:
  0.0 19.1 jit_solution(12672670934668502009)
XLA Ops:
  0.6 0.0 copy-start
  0.6 0.0 copy-start.1
  0.7 1.6 %edge_levels.1 = (f32[200,128]{1,0:T(8,128)S(1)}, f32[200,128]{1,0:T(8,128)S(1)}, f32[4,88,128]{2,1,0:T(8,128)S(1)}) custom-call(f32[3,16,72,128]{3,2,1,0:T(8,128)} %v_ref.3, f32[6,16,72,128]{3,2,1,0:T(8,128)} %s_ref.3, s32[72]{0:T(128)} %index.1, f32[4,8]{1,0:T(4,128)} %bitcast.1), custom_call_target="tpu_custom_call" | custom-call | tf_op jit(solution)/shard_map/edge_levels/pallas_call | solution.py:690
  2.2 0.0 copy-start.2
  2.3 0.0 copy-start.3
  2.3 0.0 copy-start.4
  2.3 0.0 copy-start.5
  2.3 3.1 %collective-permute-start = (f32[200,128]{1,0:T(8,128)S(1)}, f32[200,128]{1,0:T(8,128)S(1)}, u32[]{:S(2)}, u32[]{:S(2)}) collective-permute-start(f32[200,128]{1,0:T(8,128)S(1)} %get-tuple-element.18), channel_id=1, source_target_pairs={{0,1},{1,0},{2,3},{3,2},{4,5},{5,4},{6,7},{7,6},{8,9},{9,8},{10,11... | collective-permute-start | bytes 307208 | tf_op jit(solution)/shard_map/ppermute | solution.py:43
  5.4 0.0 collective-permute-start.1
  6.0 0.0 copy-done
  6.0 0.0 copy-done.1
  6.1 1.4 %load_block.1 = (f32[3,18,88,128]{3,2,1,0:T(8,128)S(1)}, f32[6,17,88,128]{3,2,1,0:T(8,128)S(1)}, f32[4,88,128]{2,1,0:T(8,128)S(1)}) custom-call(f32[3,16,72,128]{3,2,1,0:T(8,128)S(1)} %copy-done.1, f32[6,16,72,128]{3,2,1,0:T(8,128)S(1)} %copy-done, f32[4,88,128]{2,1,0:T(8,128)S(1)} %get-tuple-element.20.coef_in, ...), custom_call_target="tpu_custom_call", output_to_operand_aliasing={{2}: (2, {})} | custom-call | flops 4423680 | bytes 5308416 | tf_op jit(solution)/shard_map/load_block/pallas_call | solution.py:701
  7.5 0.8 %collective-permute-done.got_a = f32[200,128]{1,0:T(8,128)S(1)} collective-permute-done((f32[200,128]{1,0:T(8,128)S(1)}, f32[200,128]{1,0:T(8,128)S(1)}, u32[]{:S(2)}, u32[]{:S(2)}) %collective-permute-start) | collective-permute-done | bytes 102432 | tf_op jit(solution)/shard_map/ppermute | solution.py:43
  8.3 0.0 collective-permute-done.1.got_b
  8.3 0.0 copy-done.2
  8.3 0.0 copy-done.3
  8.3 0.0 copy-done.4
  8.3 1.2 %edge_planes.1 = (f32[448,128]{1,0:T(8,128)S(1)}, f32[448,128]{1,0:T(8,128)S(1)}, f32[200,128]{1,0:T(8,128)S(1)}, f32[200,128]{1,0:T(8,128)S(1)}, f32[4,88,128]{2,1,0:T(8,128)S(1)}) custom-call(f32[200,128]{1,0:T(8,128)S(1)} %collective-permute-done.got_a, f32[200,128]{1,0:T(8,128)S(1)} %collective-permute-done.1.got_b, ...), custom_call_target="tpu_custom_call", output_to_operand_aliasing={{4}: (4, {})} | custom-call | tf_op jit(solution)/shard_map/edge_planes/pallas_call | solution.py:712
  9.5 0.1 collective-permute-start.2
  9.5 3.0 %collective-permute-start.3 = (f32[448,128]{1,0:T(8,128)S(1)}, f32[448,128]{1,0:T(8,128)S(1)}, u32[]{:S(2)}, u32[]{:S(2)}) collective-permute-start(f32[448,128]{1,0:T(8,128)S(1)} %get-tuple-element.26.own_b), channel_id=1, source_target_pairs={{0,1},{1,0},{2,3},{3,2},{4,8},{5,9},{6,10},{7,11},{8,4},{9,5},{10,... | collective-permute-start | bytes 688136 | tf_op jit(solution)/shard_map/ppermute | solution.py:43
  12.5 4.9 %both_steps.1 = (f32[3,18,88,128]{3,2,1,0:T(8,128)S(1)}, f32[6,17,88,128]{3,2,1,0:T(8,128)S(1)}, f32[3,16,72,128]{3,2,1,0:T(8,128)}, f32[6,16,72,128]{3,2,1,0:T(8,128)}) custom-call(f32[3,18,88,128]{3,2,1,0:T(8,128)S(1)} %get-tuple-element.22.vb.v_in, ...), custom_call_target="tpu_custom_call", output_to_operand_aliasing={{0}: (0, {}), {1}: (1, {})} | custom-call | flops 16220160 | bytes 5308416 | tf_op jit(solution)/shard_map/both_steps/pallas_call | solution.py:731
  17.4 0.0 collective-permute-done.2.next_a
  17.4 0.0 collective-permute-done.3.next_b
  17.4 1.7 %join_neighbours.1 = (f32[3,16,72,128]{3,2,1,0:T(8,128)}, f32[6,16,72,128]{3,2,1,0:T(8,128)}) custom-call(f32[448,128]{1,0:T(8,128)S(1)} %collective-permute-done.2.next_a, f32[448,128]{1,0:T(8,128)S(1)} %collective-permute-done.3.next_b, f32[448,128]{1,0:T(8,128)S(1)} %get-tuple-element.25.own_a, ...), custom_call_target="tpu_custom_call", output_to_operand_aliasing={{0}: (7, {}), {1}: (8, {})} | custom-call | tf_op jit(solution)/shard_map/join_neighbours/pallas_call | solution.py:744
  (1 shorter events, 0.0 us)
Async XLA Ops:
  0.6 5.4 %copy-start = (f32[6,16,72,128]{3,2,1,0:T(8,128)S(1)}, f32[6,16,72,128]{3,2,1,0:T(8,128)}, u32[]{:S(2)}) copy-start(f32[6,16,72,128]{3,2,1,0:T(8,128)} %s_ref.3) | copy-start | bytes 10616836
  0.6 5.4 %copy-start.1 = (f32[3,16,72,128]{3,2,1,0:T(8,128)S(1)}, f32[3,16,72,128]{3,2,1,0:T(8,128)}, u32[]{:S(2)}) copy-start(f32[3,16,72,128]{3,2,1,0:T(8,128)} %v_ref.3) | copy-start | bytes 5308420
  2.2 6.0 %copy-start.2 = (s32[16]{0:T(128)S(1)}, s32[16]{0:T(128)}, u32[]{:S(2)}) copy-start(s32[16]{0:T(128)} %refs_0_.3) | copy-start | bytes 196
  2.3 6.0 %copy-start.3 = (s32[16]{0:T(128)S(1)}, s32[16]{0:T(128)}, u32[]{:S(2)}) copy-start(s32[16]{0:T(128)} %refs_1_.3) | copy-start | bytes 196
  2.3 6.0 %copy-start.4 = (s32[16]{0:T(128)S(1)}, s32[16]{0:T(128)}, u32[]{:S(2)}) copy-start(s32[16]{0:T(128)} %refs_2_.3) | copy-start | bytes 196
  2.3 6.0 %copy-start.5 = (f32[16]{0:T(128)S(1)}, f32[16]{0:T(128)}, u32[]{:S(2)}) copy-start(f32[16]{0:T(128)} %refs_3_.3) | copy-start | bytes 196
  2.3 6.0 %collective-permute-start = (f32[200,128]{1,0:T(8,128)S(1)}, f32[200,128]{1,0:T(8,128)S(1)}, u32[]{:S(2)}, u32[]{:S(2)}) collective-permute-start(f32[200,128]{1,0:T(8,128)S(1)} %get-tuple-element.18), channel_id=1, source_target_pairs={{0,1},{1,0},{2,3},{3,2},{4,5},{5,4},{6,7},{7,6},{8,9},{9,8},{10,11... | collective-permute-start | bytes 307208 | tf_op jit(solution)/shard_map/ppermute | solution.py:43
  5.4 2.9 %collective-permute-start.1 = (f32[200,128]{1,0:T(8,128)S(1)}, f32[200,128]{1,0:T(8,128)S(1)}, u32[]{:S(2)}, u32[]{:S(2)}) collective-permute-start(f32[200,128]{1,0:T(8,128)S(1)} %get-tuple-element.19), channel_id=1, source_target_pairs={{0,4},{1,2},{2,1},{3,7},{4,0},{5,6},{6,5},{7,3},{8,12},{9,10},{10,... | collective-permute-start | bytes 307208 | tf_op jit(solution)/shard_map/ppermute | solution.py:43
  9.5 7.9 %collective-permute-start.2 = (f32[448,128]{1,0:T(8,128)S(1)}, f32[448,128]{1,0:T(8,128)S(1)}, u32[]{:S(2)}, u32[]{:S(2)}) collective-permute-start(f32[448,128]{1,0:T(8,128)S(1)} %get-tuple-element.25.own_a), channel_id=1, source_target_pairs={{0,4},{1,5},{2,6},{3,7},{4,0},{5,1},{6,2},{7,3},{8,12},{9,13},{10,... | collective-permute-start | bytes 688136 | tf_op jit(solution)/shard_map/ppermute | solution.py:43
  9.5 7.9 %collective-permute-start.3 = (f32[448,128]{1,0:T(8,128)S(1)}, f32[448,128]{1,0:T(8,128)S(1)}, u32[]{:S(2)}, u32[]{:S(2)}) collective-permute-start(f32[448,128]{1,0:T(8,128)S(1)} %get-tuple-element.26.own_b), channel_id=1, source_target_pairs={{0,1},{1,0},{2,3},{3,2},{4,8},{5,9},{6,10},{7,11},{8,4},{9,5},{10,... | collective-permute-start | bytes 688136 | tf_op jit(solution)/shard_map/ppermute | solution.py:43

commit v3 on v2

--- a/solution.py
+++ b/solution.py
@@ -19,28 +19,27 @@
 SMEM = pl.BlockSpec(memory_space=pltpu.SMEM)
 
 
-def swap_pairs(rows, cols, along, odd):
+def swap_pairs(sizes, along, odd):
+    members, rows, cols = sizes
     out = []
-    for i in range(rows):
-        for j in range(cols):
-            at, size = (i, rows) if along == 0 else (j, cols)
-            if not odd:
-                to = at ^ 1
-            elif at in (0, size - 1):
-                to = None
-            else:
-                to = at + 1 if at % 2 else at - 1
-            if along == 0:
-                target = (i, j ^ 1) if to is None else (to, j)
-            else:
-                target = (i ^ 1, j) if to is None else (i, to)
-            out.append((i * cols + j, target[0] * cols + target[1]))
+    for a in range(members):
+        for i in range(rows):
+            for j in range(cols):
+                here = [a, i, j]
+                there = [a, i, j]
+                if not odd:
+                    there[along] ^= 1
+                elif 0 < here[along] < sizes[along] - 1:
+                    there[along] += 1 if here[along] % 2 else -1
+                else:
+                    there[1 if along == 2 else 2 if members % 2 else 0] ^= 1
+                out.append(tuple((p[0] * rows + p[1]) * cols + p[2] for p in (here, there)))
     return out
 
 
 def swap(block, along, odd):
-    rows, cols = lax.axis_size("horiz"), lax.axis_size("vert")
-    return lax.ppermute(block, ("horiz", "vert"), swap_pairs(rows, cols, along, odd))
+    axes = ("member", "horiz", "vert")
+    return lax.ppermute(block, axes, swap_pairs([lax.axis_size(a) for a in axes], along, odd))
 
 
 def lane_of(shape):
@@ -186,59 +185,110 @@
 GROUP = 4
 
 
-def load_kernel(n, m, y, v_ref, s_ref, coef_in, split, vb, sb, coef, sems):
+def load_kernel(n, m, y, v_ref, s_ref, coef_in, split, *refs):
+    sources, (vb, sb, raw, coef), scratch = refs[:4], refs[4:8], refs[8:]
+    sx, sz, sy, amp, small = scratch
     del coef_in
-    body = pl.ds(PAD, m)
-
-    def fetch(g):
-        return (
-            pltpu.make_async_copy(
-                s_ref.at[:, pl.ds(GROUP * g, GROUP)], sb.at[:, pl.ds(GROUP * g + 1, GROUP), body], sems.at[0, g]
-            ),
-            pltpu.make_async_copy(
-                v_ref.at[:, pl.ds(GROUP * g, GROUP)], vb.at[:, pl.ds(GROUP * g + 1, GROUP), body], sems.at[1, g]
-            ),
-        )
-
-    for g in range(n // GROUP):
-        for copy in fetch(g):
-            copy.start()
+    fetched = fetch_sources(sources, (sx, sz, sy, amp), small)
     for f in front:
         sb[f, 0] = jnp.zeros((m + 16, y), jnp.float32)
     for k in range(3):
         vb[k, n + 1] = jnp.zeros((m + 16, y), jnp.float32)
-    high = m + 16
-    s2 = sb.reshape(6 * (n + 1) * high, y)
-    for f in top:
-        s2[pl.Slice((f * (n + 1) + 1) * high + PAD - 1, n, high), :] = jnp.zeros((n, y), jnp.float32)
-
     lowest, first = PAD - 1, PAD + m
+    s_line, v_line, s2, v2 = lines(n, m, y, vb, sb)
+    zero = jnp.zeros((n, y), jnp.float32)
+    for f in range(6):
+        s2[s_line(f, lowest), :] = zero
+        s2[s_line(f, first), :] = zero
+    for k in range(3):
+        v2[v_line(k, first), :] = zero
     coef[3, pl.ds(lowest, 1), :] = jnp.ones((1, y), jnp.float32)
     coef[3, pl.ds(first, 1), :] = jnp.ones((1, y), jnp.float32)
     start = split[0] - lax.axis_index("vert") * m
-    for r, size in [(PAD + 8 * t, 8) for t in range(m // 8)] + [(lowest, 1), (first, 1)]:
+    tiles = [PAD + 8 * t for t in range(m // 8)]
+    for r, size in [(r, 8) for r in tiles] + [(lowest, 1), (first, 1)]:
         level = r - PAD + lax.broadcasted_iota(jnp.int32, (size, y), 0)
         at = pl.ds(r, size)
         coef[3, at, :] = jnp.where(level >= start, coef[3, at, :], 0.0)
 
-    def advance(g, carry):
-        for copy in fetch(g):
-            copy.wait()
-        for p in range(GROUP):
-            x = GROUP * g + p
-            for t in range(m // 8):
-                r = PAD + 8 * t
-                new = velocity_tile(
-                    memo(lambda f, dx, dz: sb[f, x + 1 + dx, pl.ds(r + dz, 8), :]),
-                    lambda k: vb[k, x + 1, pl.ds(r, 8), :],
-                    coef[0, pl.ds(r, 8), :],
-                    coef[1, pl.ds(r, 8), :],
-                )
-                for k in range(3):
-                    vb[k, x + 1, pl.ds(r, 8), :] = new[k]
+    def cs(c, r):
+        return coef[c, pl.ds(r, 8), :]
+
+    def move(x, has_before):
+        for r in tiles:
+
+            def stress_at(f, dx, dz):
+                if dx and not has_before:
+                    return 0.0
+                if dz and r == PAD:
+                    return plane_before(s_ref[f, x, pl.ds(0, 8), :])
+                return s_ref[f, x + dx, pl.ds(r - PAD + dz, 8), :]
+
+            new = velocity_tile(memo(stress_at), lambda k: v_ref[k, x, pl.ds(r - PAD, 8), :], cs(0, r), cs(1, r))
+            for k in range(3):
+                vb[k, x + 1, pl.ds(r, 8), :] = new[k]
+
+    def load(x):
+        for r in tiles:
+            grads = strain(memo(lambda k, dx, dz: vb[k, x + 1 + dx, pl.ds(r + dz, 8), :]))
+            terms = stress_terms(grads, cs(2, r), cs(3, r))
+            for c in range(6):
+                sb[c, x + 1, pl.ds(r, 8), :] = s_ref[c, x, pl.ds(r - PAD, 8), :] + terms[c]
+
+    def sweep(work, start):
+        def go(g, carry):
+            for p in range(GROUP):
+                work(GROUP * g + p)
+            return carry
+
+        lax.fori_loop(start, n // GROUP, go, 0)
+
+    for x in range(GROUP):
+        move(x, x > 0)
+    sweep(lambda x: move(x, True), 1)
+    sweep(load, 0)
+    for c, f in enumerate(front):
+        raw[c] = s_ref[f, n - 1]
+    for copy in fetched:
+        copy.wait()
+    x_at, z_at = lax.axis_index("horiz") * n, lax.axis_index("vert") * m
+
+    def add(i, carry):
+        x, z = sx[i] - x_at, sz[i] - z_at
+
+        @pl.when((x >= 0) & (x < n) & (z >= -1) & (z <= m))
+        def _():
+            row = jnp.where(lane_of((1, y)) == sy[i], courant * wavelet[0] * amp[i], 0.0)
+            at = pl.ds(PAD + z, 1)
+            for c in range(3):
+                sb[c, x + 1, at, :] = sb[c, x + 1, at, :] + row
+
         return carry
 
-    lax.fori_loop(0, n // GROUP, advance, 0)
+    lax.fori_loop(0, sx.shape[0], add, 0)
+
+
+def lines(n, m, y, vb, sb):
+    high = m + 16
+
+    def s_line(f, r):
+        return pl.Slice((f * (n + 1) + 1) * high + r, n, high)
+
+    def v_line(k, r):
+        return pl.Slice((k * (n + 2) + 1) * high + r, n, high)
+
+    return s_line, v_line, sb.reshape(6 * (n + 1) * high, y), vb.reshape(3 * (n + 2) * high, y)
+
+
+def plane_before(a):
+    rows = lax.broadcasted_iota(jnp.int32, a.shape, 0)
+    return jnp.where(rows == 0, 0.0, pltpu.roll(a, 1, 0))
+
+
+def plane_after(a):
+    last = a.shape[0] - 1
+    rows = lax.broadcasted_iota(jnp.int32, a.shape, 0)
+    return jnp.where(rows == last, 0.0, pltpu.roll(a, last, 0))
 
 
 def fetch_sources(refs, held, sems):
@@ -248,30 +298,9 @@
     return copies
 
 
-def add_sources(add_row, plane_of, z_low, z_high, scale, x_at, z_at, src):
-    sx, sz, sy, amp = src
-
-    def body(i, carry):
-        x, z = sx[i] - x_at, sz[i] - z_at
-
-        @pl.when(plane_of(x) & (z >= z_low) & (z < z_high))
-        def _():
-            lane = lane_of((1, 128))
-            add_row(x, z, jnp.where(lane == sy[i], scale * amp[i], 0.0))
-
-        return carry
-
-    lax.fori_loop(0, sx.shape[0], body, 0)
-
-
-def plane_kernel(
-    n, m, y, got_a, got_b, vb, sb, coef_in, *refs
-):
-    sources, (out_a, out_b, below, above, coef), scratch = refs[:4], refs[4:9], refs[9:]
-    sl, vl, sr, vr, msg, sx, sz, sy, amp, sems = scratch
-    del coef_in
+def plane_kernel(n, m, y, got_a, got_b, edge_a, edge_b, v_in, s_in, raw, coef_in, out_a, out_b, vb, sb, coef, below, above):
+    del v_in, s_in, coef_in
     horiz, vert = lax.axis_index("horiz"), lax.axis_index("vert")
-    fetched = fetch_sources(sources, (sx, sz, sy, amp), sems)
     odd = vert % 2 == 1
     has_below = jnp.where(vert > 0, 1.0, 0.0)
     has_above = jnp.where(vert < lax.axis_size("vert") - 1, 1.0, 0.0)
@@ -288,153 +317,109 @@
             coef[c, pl.ds(r, 1), :] = value * coef[c, pl.ds(r, 1), :] if c == 3 else value
     coef[0, pl.ds(second, 1), :] = above[pl.ds(base + 4, 1), :]
 
-    tiles = [(PAD + 8 * t, 8) for t in range(m // 8)]
-    right, left = horiz % 2, 1 - horiz % 2
-    tail = 6 * m
-
     def cs(c, r, size):
         return coef[c, pl.ds(r, size), :]
 
-    def from_below(f, x):
-        return below[pl.ds(f * n + x, 1), :]
-
-    def from_above(f, x):
-        return above[pl.ds(f * n + x, 1), :]
-
-    for x, buf, at in ((0, vl, 0), (1, vl, 1), (n - 1, vr, 0)):
-        for k in range(3):
-            for r, size in tiles:
-                buf[k, at, pl.ds(r, size), :] = vb[k, x + 1, pl.ds(r, size), :]
-            line = pl.ds(PAD, 1)
-            buf[k, at, line, :] = vb[k, x + 1, line, :] - cs(0, PAD, 1) * from_below(top[k], x)
-            buf[k, at, pl.ds(lowest, 1), :] = from_below(6 + k, x)
-            buf[k, at, pl.ds(second, 1), :] = from_above(9 + k, x)
-
-        def beyond(f, dx, dz):
-            if dz:
-                return sb[f, x + 1, pl.ds(first - 1, 1), :]
-            if x + dx < 0:
-                return jnp.zeros((1, y), jnp.float32)
-            return from_above(f, x + dx)
-
-        new = velocity_tile(memo(beyond), lambda k: from_above(6 + k, x), cs(0, first, 1), cs(1, first, 1))
-        for k in range(3):
-            buf[k, at, pl.ds(first, 1), :] = new[k]
-
-    def stress_rows(f, x, r, size):
-        if r < PAD:
-            return from_below(f, x)
-        if r >= first:
-            return from_above(f, x)
-        return sb[f, x + 1, pl.ds(r, size), :]
-
-    def load(out, v_buf, x, r, size, wanted, ahead):
-        def at(k, dx, dz):
-            if dx and not ahead:
-                return 0.0
-            return v_buf[k, dx, pl.ds(r + dz, size), :]
-
-        terms = stress_terms(strain(memo(at)), cs(2, r, size), cs(3, r, size), wanted)
+    s_line, v_line, s2, v2 = lines(n, m, y, vb, sb)
+    low = [below[pl.ds(f * n, n), :] for f in range(9)]
+    high = [above[pl.ds(f * n, n), :] for f in range(12)]
+    own = [None] * 6
+    for f in top:
+        at = pl.ds(f * n, n)
+        own[f] = jnp.where(odd, edge_b[at, :], edge_a[at, :])
+
+    def beyond(f, dx, dz):
+        if dz:
+            return own[f]
+        return plane_before(high[f]) if dx else high[f]
+
+    v_high = velocity_tile(memo(beyond), lambda k: high[6 + k], cs(0, first, 1), cs(1, first, 1))
+    change = [-cs(0, PAD, 1) * low[top[k]] for k in range(3)]
+    v_low = [v2[v_line(k, PAD), :] + change[k] for k in range(3)]
+    for k in range(3):
+        v2[v_line(k, first), :] = v_high[k]
+        v2[v_line(k, PAD), :] = v_low[k]
+
+    def add_terms(r, grads, wanted, start=None):
+        terms = stress_terms(grads, cs(2, r, 1), cs(3, r, 1), wanted)
         for c in wanted:
-            out[c, pl.ds(r, size), :] = stress_rows(c, x, r, size) + terms[c]
-
-    for r, size in tiles + [(first, 1)]:
-        load(sr, vr, n - 1, r, size, front, False)
-    load(sl, vl, 0, lowest, 1, top, True)
-    for r, size in tiles:
-        load(sl, vl, 0, r, size, range(6), True)
-    for c, f in enumerate(front):
-        for r, size in tiles:
-            msg[right, pl.ds(c * m + r - PAD, size), :] = sb[f, n, pl.ds(r, size), :]
-            msg[left, pl.ds(c * m + r - PAD, size), :] = vl[c, 0, pl.ds(r, size), :]
-        msg[right, pl.ds(tail + c, 1), :] = from_below(f, n - 1)
-        msg[right, pl.ds(tail + 3 + c, 1), :] = from_above(f, n - 1)
-        msg[right, pl.ds(tail + 6 + c, 1), :] = above[pl.ds(base + 5 + c, 1), :]
-        msg[left, pl.ds(tail + c, 1), :] = vl[c, 0, pl.ds(lowest, 1), :]
-        msg[left, pl.ds(tail + 3 + c, 1), :] = vl[c, 0, pl.ds(first, 1), :]
-
-    for copy in fetched:
-        copy.wait()
-
-    def add(x, z, row):
-        at = pl.ds(PAD + z, 1)
-
-        @pl.when(x == 0)
-        def _():
-            for c in range(3):
-                sl[c, at, :] = sl[c, at, :] + row
-
-        @pl.when(x == n - 1)
-        def _():
-            sr[0, at, :] = sr[0, at, :] + row
-
-    add_sources(
-        add, lambda x: (x == 0) | (x == n - 1), -1, m + 1, courant * wavelet[0], horiz * n, vert * m, (sx, sz, sy, amp)
-    )
-    for c, f in enumerate(front):
-        for r, size in tiles:
-            msg[right, pl.ds((3 + c) * m + r - PAD, size), :] = sr[f, pl.ds(r, size), :]
-        msg[right, pl.ds(tail + 9 + c, 1), :] = sr[f, pl.ds(first, 1), :]
+            line = s_line(c, r)
+            old = s2[line, :]
+            s2[line, :] = old + terms[c] if start is None else old + (start[c] + terms[c])
+
+    def across(v):
+        return [plane_after(v) - v, None, fore_lane(v)]
+
+    def grads_of(values, next_values):
+        out = []
+        for v, after in zip(values, next_values):
+            grad = across(v)
+            grad[1] = -v if after is None else after - v
+            out.append(grad)
+        return out
+
+    add_terms(lowest, grads_of(low[6:9], v_low), top, low)
+    add_terms(PAD, grads_of(change, [None] * 3), range(6))
+    add_terms(first, grads_of(v_high, high[9:12]), range(6), high)
+    rl, rm = cs(2, first - 1, 1), cs(3, first - 1, 1)
+    spread = rl * v_high[1]
+    for c, term in ((0, spread), (1, spread + 2.0 * rm * v_high[1]), (2, spread), (3, rm * v_high[0]), (5, rm * v_high[2])):
+        line = s_line(c, first - 1)
+        s2[line, :] = s2[line, :] + term
+
+    even = horiz % 2 == 0
+    tiles = [(PAD + 8 * t, 8) for t in range(m // 8)]
+    tail = 6 * m
+
+    def put(at, size, to_right, to_left):
+        out_a[pl.ds(at, size), :] = jnp.where(even, to_right, to_left)
+        out_b[pl.ds(at, size), :] = jnp.where(even, to_left, to_right)
+
     for r, size in tiles:
         new = velocity_tile(
-            memo(lambda f, dx, dz: 0.0 if dx else sl[f, pl.ds(r + dz, size), :]),
-            lambda k: vl[k, 0, pl.ds(r, size), :],
+            memo(lambda f, dx, dz: 0.0 if dx else sb[f, 1, pl.ds(r + dz, size), :]),
+            lambda k: vb[k, 1, pl.ds(r, size), :],
             cs(0, r, size),
             cs(1, r, size),
         )
-        for k in range(3):
-            msg[left, pl.ds((3 + k) * m + r - PAD, size), :] = new[k]
-    for t in range((6 * m + 16) // 8):
-        at = pl.ds(8 * t, 8)
-        out_a[at, :] = msg[0, at, :]
-        out_b[at, :] = msg[1, at, :]
-
-
-def rest_kernel(n, m, y, v_in, s_in, below, above, coef, *refs):
+        for c, f in enumerate(front):
+            put(c * m + r - PAD, size, raw[c, pl.ds(r - PAD, size), :], vb[c, 1, pl.ds(r, size), :])
+            put((3 + c) * m + r - PAD, size, sb[f, n, pl.ds(r, size), :], new[c])
+    for c, f in enumerate(front):
+        last = f * n + n - 1
+        before_low, before_first = below[pl.ds(last, 1), :], above[pl.ds(last, 1), :]
+        put(tail + c, 1, before_low, below[pl.ds((6 + c) * n, 1), :])
+        put(tail + 3 + c, 1, before_first, vb[c, 1, pl.ds(first, 1), :])
+        before_second, after_first = above[pl.ds(base + 5 + c, 1), :], sb[f, n, pl.ds(first, 1), :]
+        put(tail + 6 + c, 1, before_second, before_second)
+        put(tail + 9 + c, 1, after_first, after_first)
+
+
+def rest_kernel(n, m, y, v_in, s_in, coef, *refs):
     sources, (vb, sb, out_v, out_s), scratch = refs[:4], refs[4:8], refs[8:]
     sx, sz, sy, amp, near_x, near_z, near_y, near_amp, small, sems = scratch
     del v_in, s_in
     horiz, vert = lax.axis_index("horiz"), lax.axis_index("vert")
     fetched = fetch_sources(sources, (sx, sz, sy, amp), small)
     body = pl.ds(PAD, m)
-    lowest, first, second = PAD - 1, PAD + m, PAD + m + 1
-    high = m + 16
-    s2 = sb.reshape(6 * (n + 1) * high, y)
-    v2 = vb.reshape(3 * (n + 2) * high, y)
+    first = PAD + m
     tiles = [(PAD + 8 * t, 8) for t in range(m // 8)]
 
     def cs(c, r, size):
         return coef[c, pl.ds(r, size), :]
 
-    def s_line(f, r):
-        return pl.Slice((f * (n + 1) + 1) * high + r, n, high)
-
-    def v_line(k, r):
-        return pl.Slice((k * (n + 2) + 1) * high + r, n, high)
+    s_line, v_line, s2, v2 = lines(n, m, y, vb, sb)
 
     def beyond(f, dx, dz):
-        if dz:
-            return s2[s_line(f, first - 1), :]
-        here = above[pl.ds(f * n, n), :]
-        if dx:
-            rows = lax.broadcasted_iota(jnp.int32, (n, y), 0)
-            return jnp.where(rows == 0, 0.0, pltpu.roll(here, 1, 0))
-        return here
-
-    new = velocity_tile(
-        memo(beyond), lambda k: above[pl.ds((6 + k) * n, n), :], cs(0, first, 1), cs(1, first, 1)
-    )
+        here = s2[s_line(f, first + dz), :]
+        return plane_before(here) if dx else here
+
+    new = velocity_tile(memo(beyond), lambda k: v2[v_line(k, first), :], cs(0, first, 1), cs(1, first, 1))
     for k in range(3):
         v2[v_line(k, first), :] = new[k]
-        v2[v_line(k, lowest), :] = below[pl.ds((6 + k) * n, n), :]
-        v2[v_line(k, second), :] = above[pl.ds((9 + k) * n, n), :]
-        v2[v_line(k, PAD), :] = v2[v_line(k, PAD), :] - cs(0, PAD, 1) * below[pl.ds(top[k] * n, n), :]
-    for f in range(6):
-        s2[s_line(f, lowest), :] = below[pl.ds(f * n, n), :]
-        s2[s_line(f, first), :] = above[pl.ds(f * n, n), :]
 
     def move(x):
-        for r, size in tiles + [(first, 1)]:
+        for r, size in tiles:
             new = velocity_tile(
                 memo(lambda f, dx, dz: sb[f, x + 1 + dx, pl.ds(r + dz, size), :]),
                 lambda k: vb[k, x + 1, pl.ds(r, size), :],
@@ -444,14 +429,11 @@
             for k in range(3):
                 vb[k, x + 1, pl.ds(r, size), :] = new[k]
 
-    def load(x, step):
-        parts = [(r, size, range(6)) for r, size in tiles]
-        if step == 0:
-            parts += [(lowest, 1, top), (first, 1, range(6))]
-        for r, size, wanted in parts:
+    def load(x):
+        for r, size in tiles:
             g = strain(memo(lambda k, dx, dz: vb[k, x + 1 + dx, pl.ds(r + dz, size), :]))
-            terms = stress_terms(g, cs(2, r, size), cs(3, r, size), wanted)
-            for c in wanted:
+            terms = stress_terms(g, cs(2, r, size), cs(3, r, size))
+            for c in range(6):
                 sb[c, x + 1, pl.ds(r, size), :] = sb[c, x + 1, pl.ds(r, size), :] + terms[c]
 
     for copy in fetched:
@@ -460,15 +442,15 @@
     for i in range(sx.shape[0]):
         x, z = sx[i] - horiz * n, sz[i] - vert * m
         near_x[found], near_z[found], near_y[found], near_amp[found] = x, z, sy[i], amp[i]
-        found = found + ((x >= 0) & (x < n) & (z >= -1) & (z <= m)).astype(jnp.int32)
-
-    def add_near(step, x_low, x_high, z_low, z_high):
+        found = found + ((x >= 0) & (x < n) & (z >= 0) & (z < m)).astype(jnp.int32)
+
+    def add_near(x_low, x_high):
         def add(j, carry):
             x, z = near_x[j], near_z[j]
 
-            @pl.when((x >= x_low) & (x < x_high) & (z >= z_low) & (z < z_high))
+            @pl.when((x >= x_low) & (x < x_high))
             def _():
-                row = jnp.where(lane_of((1, y)) == near_y[j], courant * wavelet[step] * near_amp[j], 0.0)
+                row = jnp.where(lane_of((1, y)) == near_y[j], courant * wavelet[1] * near_amp[j], 0.0)
                 at = pl.ds(PAD + z, 1)
                 for c in range(3):
                     sb[c, x + 1, at, :] = sb[c, x + 1, at, :] + row
@@ -488,26 +470,22 @@
         def _():
             off(x).start()
 
-    add_near(0, 0, n, -1, m + 1)
-
     def advance(g, carry):
         x = GROUP * g
-        for p in range(GROUP):
-            load(x + p, 0)
         for p in range(GROUP):
             move(x + p)
         for p in range(GROUP):
             send(v_off, x + p, n - 2)
         for p in range(-1, GROUP - 1):
-            load(x + p, 1)
-        add_near(1, x - 1, x + GROUP - 1, 0, m)
+            load(x + p)
+        add_near(x - 1, x + GROUP - 1)
         for p in range(-1, GROUP - 1):
             send(s_off, x + p, n - 1 - GROUP)
         return carry
 
     lax.fori_loop(0, n // GROUP, advance, 0)
-    load(n - 1, 1)
-    add_near(1, n - 1, n, 0, m)
+    load(n - 1)
+    add_near(n - 1, n)
 
     def finish(x, carry):
         v_off(x).wait()
@@ -521,7 +499,7 @@
     lax.fori_loop(2, n - 2, finish, 0)
 
 
-def join_kernel(n, m, y, next_a, next_b, own_a, own_b, coef, vb, sb, v_in, s_in, v_out, s_out, *scratch):
+def join_kernel(n, m, y, next_b, next_a, own_a, own_b, coef, vb, sb, v_in, s_in, v_out, s_out, *scratch):
     wa, da, ds, dv, dw, qb, db, es, ev, vn, v0, v1, s0, s1, sems = scratch
     del v_in, s_in
     horiz = lax.axis_index("horiz")
@@ -696,49 +674,42 @@
         compiler_params=room(EDGE_MIB),
         name="edge_levels",
     )(*[pltpu.with_memory_space_constraint(a, pltpu.HBM) for a in (velocity, stress, index, table)])
-    got_a, got_b = swap(edge_a, 1, False), swap(edge_b, 1, True)
+    got_a, got_b = swap(edge_a, 2, False), swap(edge_b, 2, True)
     split, edge_a = lax.optimization_barrier((split, edge_a))
-    vb, sb, coef = pl.pallas_call(
+    vb, sb, raw, coef = pl.pallas_call(
         functools.partial(load_kernel, n, m, y),
-        out_shape=[padded_v, padded_s, kept(4, high, y)],
-        in_specs=[ANY, ANY, VMEM, SMEM],
-        out_specs=[VMEM] * 3,
-        input_output_aliases={2: 2},
-        scratch_shapes=[dma((2, n // GROUP))],
+        out_shape=[padded_v, padded_s, kept(3, m, y), kept(4, high, y)],
+        in_specs=[VMEM, VMEM, VMEM, SMEM] + [ANY] * 4,
+        out_specs=[VMEM] * 4,
+        input_output_aliases={2: 3},
+        scratch_shapes=[*held, dma((4,))],
         compiler_params=room(LOAD_MIB),
-        cost_estimate=cost(30 * n * m * y, 4 * 9 * n * m * y),
+        cost_estimate=cost(60 * n * m * y, 4 * 9 * n * m * y),
         name="load_block",
-    )(velocity, stress, coef, split)
-    plane_a, plane_b, below, above, coef = pl.pallas_call(
+    )(*[pltpu.with_memory_space_constraint(a, pltpu.VMEM) for a in (velocity, stress)], coef, split, *sources)
+    plane_a, plane_b, vb, sb, coef = pl.pallas_call(
         functools.partial(plane_kernel, n, m, y),
-        out_shape=[kept(6 * m + 16, y)] * 2 + [kept(MSG, y)] * 2 + [kept(4, high, y)],
-        in_specs=[VMEM] * 5 + [ANY] * 4,
+        out_shape=[kept(6 * m + 16, y)] * 2 + [padded_v, padded_s, kept(4, high, y)],
+        in_specs=[VMEM] * 8,
         out_specs=[VMEM] * 5,
-        input_output_aliases={4: 4},
-        scratch_shapes=[
-            pltpu.VMEM((6, high, y), f32),
-            pltpu.VMEM((3, 2, high, y), f32),
-            pltpu.VMEM((6, high, y), f32),
-            pltpu.VMEM((3, 1, high, y), f32),
-            pltpu.VMEM((2, 6 * m + 16, y), f32),
-            *held,
-            dma((4,)),
-        ],
+        input_output_aliases={4: 2, 5: 3, 7: 4},
+        scratch_shapes=[pltpu.VMEM((MSG, y), f32)] * 2,
         compiler_params=room(SMALL_MIB),
         name="edge_planes",
-    )(got_a, got_b, vb, sb, coef, *sources)
-    next_a, next_b = swap(plane_a, 0, False), swap(plane_b, 0, True)
+    )(got_a, got_b, edge_a, edge_b, vb, sb, raw, coef)
+    next_b = swap(plane_b, 1, True)
+    next_a = swap(plane_a, 1, False)
     vb, sb, v_own, s_own = pl.pallas_call(
         functools.partial(rest_kernel, n, m, y),
         out_shape=[padded_v, padded_s, outside(*velocity.shape), outside(*stress.shape)],
-        in_specs=[VMEM] * 5 + [ANY] * 4,
+        in_specs=[VMEM] * 3 + [ANY] * 4,
         out_specs=[VMEM, VMEM, HBM, HBM],
         input_output_aliases={0: 0, 1: 1},
         scratch_shapes=[*held, *near, dma((4,)), dma((2, n))],
         compiler_params=room(SMALL_MIB),
-        cost_estimate=cost(110 * n * m * y, 4 * 9 * n * m * y),
+        cost_estimate=cost(60 * n * m * y, 4 * 9 * n * m * y),
         name="both_steps",
-    )(vb, sb, below, above, coef, *sources)
+    )(vb, sb, coef, *sources)
     plane = pltpu.VMEM((3, high, y), f32)
     plane6 = pltpu.VMEM((6, high, y), f32)
     return pl.pallas_call(
@@ -753,7 +724,7 @@
         + [dma((9,))],
         compiler_params=room(SMALL_MIB),
         name="join_neighbours",
-    )(next_a, next_b, plane_a, plane_b, coef, vb, sb, v_own, s_own)
+    )(next_b, next_a, plane_a, plane_b, coef, vb, sb, v_own, s_own)
 
 
 def solution(mesh):

time: 19.3 us -> 16.9 us (0.88)
  the two profiles are of different devices: /device:TPU:0 before, /device:TPU:16 now
where the time goes in v3:
time: 16.9 us; the launch traced here: 16.6 us
  Pallas kernels  9.59 us (57%)
  starting transfers between devices  3.34 us (20%)
  waiting for transfers between devices  2.21 us (13%)
  between operations  1.42 us (8%)
    pallas_call x1, Pallas kernels, local(): pl.pallas_call(functools.partial(rest_kernel, n, m, y), out_shape=[padded...  3.61 us
    ppermute x4, starting transfers between devices, swap(): lax.ppermute(block, axes, swap_pairs([lax.axis_size(a) for a in axes], al...  3.34 us
    pallas_call x1, Pallas kernels, local(): pl.pallas_call(functools.partial(load_kernel, n, m, y), out_shape=[padded...  2.49 us
    ppermute x4, waiting for transfers between devices, swap(): lax.ppermute(block, axes, swap_pairs([lax.axis_size(a) for a in axes], al...  2.21 us
    pallas_call x1, Pallas kernels, local(): pl.pallas_call(functools.partial(join_kernel, n, m, y), out_shape=[outsid...  1.67 us
    pallas_call x1, Pallas kernels, local(): pl.pallas_call(functools.partial(edge_kernel, n, m, y), out_shape=[kept(M...  1.59 us
  transfers between devices with their start and end apart: 4, of which 2 were waited for; matrix products, arithmetic and copies ran while one was open for 0% of the time, Pallas kernels for 37%

profile of v3, /device:TPU:16, one launch (start us, length us, event | category | flops | bytes accessed | tf_op | source)
XLA Modules:
  0.0 16.6 jit_solution(3681196350174203693)
XLA Ops:
  0.6 0.0 copy-start
  0.6 0.0 copy-start.1
  0.7 0.0 copy-start.2
  0.7 0.0 copy-start.3
  0.7 0.0 copy-start.4
  0.7 0.0 copy-start.5
  0.7 1.6 %edge_levels.1 = (f32[200,128]{1,0:T(8,128)S(1)}, f32[200,128]{1,0:T(8,128)S(1)}, f32[4,88,128]{2,1,0:T(8,128)S(1)}) custom-call(f32[3,16,72,128]{3,2,1,0:T(8,128)} %v_ref.3, f32[6,16,72,128]{3,2,1,0:T(8,128)} %s_ref.3, s32[72]{0:T(128)} %index.1, f32[4,8]{1,0:T(4,128)} %bitcast.1), custom_call_target="tpu_custom_call" | custom-call | tf_op jit(solution)/shard_map/edge_levels/pallas_call | solution.py:668
  2.3 1.6 %collective-permute-start = (f32[200,128]{1,0:T(8,128)S(1)}, f32[200,128]{1,0:T(8,128)S(1)}, u32[]{:S(2)}, u32[]{:S(2)}) collective-permute-start(f32[200,128]{1,0:T(8,128)S(1)} %get-tuple-element.22.edge_a), channel_id=1, source_target_pairs={{0,1},{1,0},{2,3},{3,2},{4,5},{5,4},{6,7},{7,6},{8,9},{9,8},{10,11... | collective-permute-start | bytes 307208 | tf_op jit(solution)/shard_map/ppermute | solution.py:42
  3.9 0.0 collective-permute-start.1
  4.6 0.0 copy-done
  4.6 0.0 copy-done.1
  4.6 0.0 copy-done.2
  4.6 0.0 copy-done.3
  4.6 0.0 copy-done.4
  4.6 2.5 %load_block.1 = (f32[3,18,88,128]{3,2,1,0:T(8,128)S(1)}, f32[6,17,88,128]{3,2,1,0:T(8,128)S(1)}, f32[3,72,128]{2,1,0:T(8,128)S(1)}, f32[4,88,128]{2,1,0:T(8,128)S(1)}) custom-call(f32[3,16,72,128]{3,2,1,0:T(8,128)S(1)} %copy-done.1, f32[6,16,72,128]{3,2,1,0:T(8,128)S(1)} %copy-done, ...), custom_call_target="tpu_custom_call", output_to_operand_aliasing={{3}: (2, {})} | custom-call | flops 8847360 | bytes 5308416 | tf_op jit(solution)/shard_map/load_block/pallas_call | solution.py:679
  7.1 0.0 collective-permute-done.got_a
  7.2 1.4 %collective-permute-done.1.got_b = f32[200,128]{1,0:T(8,128)S(1)} collective-permute-done((f32[200,128]{1,0:T(8,128)S(1)}, f32[200,128]{1,0:T(8,128)S(1)}, u32[]{:S(2)}, u32[]{:S(2)}) %collective-permute-start.1) | collective-permute-done | bytes 102432 | tf_op jit(solution)/shard_map/ppermute | solution.py:42
  8.6 0.2 %edge_planes.1 = (f32[448,128]{1,0:T(8,128)S(1)}, f32[448,128]{1,0:T(8,128)S(1)}, f32[3,18,88,128]{3,2,1,0:T(8,128)S(1)}, f32[6,17,88,128]{3,2,1,0:T(8,128)S(1)}, f32[4,88,128]{2,1,0:T(8,128)S(1)}) custom-call(f32[200,128]{1,0:T(8,128)S(1)} %collective-permute-done.got_a, ...), custom_call_target="tpu_custom_call", output_to_operand_aliasing={{2}: (4, {}), {3}: (5, {}), {4}: (7, {})} | custom-call | tf_op jit(solution)/shard_map/edge_planes/pallas_call | solution.py:690
  8.8 1.6 %collective-permute-start.2 = (f32[448,128]{1,0:T(8,128)S(1)}, f32[448,128]{1,0:T(8,128)S(1)}, u32[]{:S(2)}, u32[]{:S(2)}) collective-permute-start(f32[448,128]{1,0:T(8,128)S(1)} %get-tuple-element.29.own_b), channel_id=1, source_target_pairs={{0,16},{1,17},{2,18},{3,19},{4,8},{5,9},{6,10},{7,11},{8,4},{9,5},... | collective-permute-start | bytes 688136 | tf_op jit(solution)/shard_map/ppermute | solution.py:42
  10.4 0.1 collective-permute-start.3
  10.5 3.6 %both_steps.1 = (f32[3,18,88,128]{3,2,1,0:T(8,128)S(1)}, f32[6,17,88,128]{3,2,1,0:T(8,128)S(1)}, f32[3,16,72,128]{3,2,1,0:T(8,128)}, f32[6,16,72,128]{3,2,1,0:T(8,128)}) custom-call(f32[3,18,88,128]{3,2,1,0:T(8,128)S(1)} %get-tuple-element.32.v_in, f32[6,17,88,128]{3,2,1,0:T(8,128)S(1)} %get-tuple-element.33.s_in, ...), custom_call_target="tpu_custom_call", output_to_operand_aliasing={{0}: (0, {}), {1}: (1, {})} | custom-call | flops 8847360 | bytes 5308416 | tf_op jit(solution)/shard_map/both_steps/pallas_call | solution.py:702
  14.2 0.8 %collective-permute-done.2.next_b = f32[448,128]{1,0:T(8,128)S(1)} collective-permute-done((f32[448,128]{1,0:T(8,128)S(1)}, f32[448,128]{1,0:T(8,128)S(1)}, u32[]{:S(2)}, u32[]{:S(2)}) %collective-permute-start.2) | collective-permute-done | bytes 229408 | tf_op jit(solution)/shard_map/ppermute | solution.py:42
  14.9 0.0 collective-permute-done.3.next_a
  14.9 1.7 %join_neighbours.1 = (f32[3,16,72,128]{3,2,1,0:T(8,128)}, f32[6,16,72,128]{3,2,1,0:T(8,128)}) custom-call(f32[448,128]{1,0:T(8,128)S(1)} %collective-permute-done.2.next_b, f32[448,128]{1,0:T(8,128)S(1)} %collective-permute-done.3.next_a, f32[448,128]{1,0:T(8,128)S(1)} %get-tuple-element.30.own_a, ...), custom_call_target="tpu_custom_call", output_to_operand_aliasing={{0}: (7, {}), {1}: (8, {})} | custom-call | tf_op jit(solution)/shard_map/join_neighbours/pallas_call | solution.py:715
  (1 shorter events, 0.0 us)
Async XLA Ops:
  0.6 4.0 %copy-start = (f32[6,16,72,128]{3,2,1,0:T(8,128)S(1)}, f32[6,16,72,128]{3,2,1,0:T(8,128)}, u32[]{:S(2)}) copy-start(f32[6,16,72,128]{3,2,1,0:T(8,128)} %s_ref.3) | copy-start | bytes 10616836
  0.6 4.0 %copy-start.1 = (f32[3,16,72,128]{3,2,1,0:T(8,128)S(1)}, f32[3,16,72,128]{3,2,1,0:T(8,128)}, u32[]{:S(2)}) copy-start(f32[3,16,72,128]{3,2,1,0:T(8,128)} %v_ref.3) | copy-start | bytes 5308420
  0.7 4.0 %copy-start.2 = (s32[16]{0:T(128)S(1)}, s32[16]{0:T(128)}, u32[]{:S(2)}) copy-start(s32[16]{0:T(128)} %refs_0_.3) | copy-start | bytes 196
  0.7 4.0 %copy-start.3 = (s32[16]{0:T(128)S(1)}, s32[16]{0:T(128)}, u32[]{:S(2)}) copy-start(s32[16]{0:T(128)} %refs_1_.3) | copy-start | bytes 196
  0.7 4.0 %copy-start.4 = (s32[16]{0:T(128)S(1)}, s32[16]{0:T(128)}, u32[]{:S(2)}) copy-start(s32[16]{0:T(128)} %refs_2_.3) | copy-start | bytes 196
  0.7 4.0 %copy-start.5 = (f32[16]{0:T(128)S(1)}, f32[16]{0:T(128)}, u32[]{:S(2)}) copy-start(f32[16]{0:T(128)} %refs_3_.3) | copy-start | bytes 196
  2.3 4.9 %collective-permute-start = (f32[200,128]{1,0:T(8,128)S(1)}, f32[200,128]{1,0:T(8,128)S(1)}, u32[]{:S(2)}, u32[]{:S(2)}) collective-permute-start(f32[200,128]{1,0:T(8,128)S(1)} %get-tuple-element.22.edge_a), channel_id=1, source_target_pairs={{0,1},{1,0},{2,3},{3,2},{4,5},{5,4},{6,7},{7,6},{8,9},{9,8},{10,11... | collective-permute-start | bytes 307208 | tf_op jit(solution)/shard_map/ppermute | solution.py:42
  3.9 4.7 %collective-permute-start.1 = (f32[200,128]{1,0:T(8,128)S(1)}, f32[200,128]{1,0:T(8,128)S(1)}, u32[]{:S(2)}, u32[]{:S(2)}) collective-permute-start(f32[200,128]{1,0:T(8,128)S(1)} %get-tuple-element.21.edge_b), channel_id=1, source_target_pairs={{0,4},{1,2},{2,1},{3,7},{4,0},{5,6},{6,5},{7,3},{8,12},{9,10},{10,... | collective-permute-start | bytes 307208 | tf_op jit(solution)/shard_map/ppermute | solution.py:42
  8.8 6.1 %collective-permute-start.2 = (f32[448,128]{1,0:T(8,128)S(1)}, f32[448,128]{1,0:T(8,128)S(1)}, u32[]{:S(2)}, u32[]{:S(2)}) collective-permute-start(f32[448,128]{1,0:T(8,128)S(1)} %get-tuple-element.29.own_b), channel_id=1, source_target_pairs={{0,16},{1,17},{2,18},{3,19},{4,8},{5,9},{6,10},{7,11},{8,4},{9,5},... | collective-permute-start | bytes 688136 | tf_op jit(solution)/shard_map/ppermute | solution.py:42
  10.4 4.5 %collective-permute-start.3 = (f32[448,128]{1,0:T(8,128)S(1)}, f32[448,128]{1,0:T(8,128)S(1)}, u32[]{:S(2)}, u32[]{:S(2)}) collective-permute-start(f32[448,128]{1,0:T(8,128)S(1)} %get-tuple-element.30.own_a), channel_id=1, source_target_pairs={{0,4},{1,5},{2,6},{3,7},{4,0},{5,1},{6,2},{7,3},{8,12},{9,13},{10,... | collective-permute-start | bytes 688136 | tf_op jit(solution)/shard_map/ppermute | solution.py:42

commit v4 on v3

--- a/solution.py
+++ b/solution.py
@@ -150,11 +150,11 @@
     lax.fori_loop(0, m, level, 0, unroll=8)
     for copy in copies:
         copy.wait()
-    low2 = low.reshape(9 * (n + 1) * 8, y)
-    high2 = high.reshape(9 * (n + 1) * 8, y)
+    low2 = low.reshape(9 * (n + 2) * 8, y)
+    high2 = high.reshape(9 * (n + 2) * 8, y)
 
     def row(buf, f, z, dx=0):
-        return buf[pl.Slice((f * (n + 1) + 1 + dx) * 8 + z, n, 8), :]
+        return buf[pl.Slice((f * (n + 2) + 1 + dx) * 8 + z, n, 8), :]
 
     def moved(buf, z, scal):
         return velocity_tile(
@@ -182,7 +182,7 @@
 
 
 EDGE_MIB, LOAD_MIB, SMALL_MIB = 16, 16, 16
-GROUP = 4
+GROUP = 8
 
 
 def load_kernel(n, m, y, v_ref, s_ref, coef_in, split, *refs):
@@ -214,39 +214,39 @@
     def cs(c, r):
         return coef[c, pl.ds(r, 8), :]
 
-    def move(x, has_before):
+    def move(x, first_group=False):
         for r in tiles:
-
-            def stress_at(f, dx, dz):
-                if dx and not has_before:
+            rb, dq = cs(0, r), cs(1, r)
+
+            def stress_of(f, p, dz):
+                if p < 0 and first_group:
                     return 0.0
                 if dz and r == PAD:
-                    return plane_before(s_ref[f, x, pl.ds(0, 8), :])
-                return s_ref[f, x + dx, pl.ds(r - PAD + dz, 8), :]
-
-            new = velocity_tile(memo(stress_at), lambda k: v_ref[k, x, pl.ds(r - PAD, 8), :], cs(0, r), cs(1, r))
-            for k in range(3):
-                vb[k, x + 1, pl.ds(r, 8), :] = new[k]
-
-    def load(x):
+                    return plane_before(s_ref[f, x + p, pl.ds(0, 8), :])
+                return s_ref[f, x + p, pl.ds(r - PAD + dz, 8), :]
+
+            stress_of = memo(stress_of)
+            for p in range(GROUP):
+                new = velocity_tile(
+                    lambda f, dx, dz: stress_of(f, p + dx, dz), lambda k: v_ref[k, x + p, pl.ds(r - PAD, 8), :], rb, dq
+                )
+                for k in range(3):
+                    vb[k, x + p + 1, pl.ds(r, 8), :] = new[k]
+
+    def load(g, carry):
+        x = GROUP * g
         for r in tiles:
-            grads = strain(memo(lambda k, dx, dz: vb[k, x + 1 + dx, pl.ds(r + dz, 8), :]))
-            terms = stress_terms(grads, cs(2, r), cs(3, r))
-            for c in range(6):
-                sb[c, x + 1, pl.ds(r, 8), :] = s_ref[c, x, pl.ds(r - PAD, 8), :] + terms[c]
-
-    def sweep(work, start):
-        def go(g, carry):
+            rl, rm = cs(2, r), cs(3, r)
+            speed_of = memo(lambda k, p, dz: vb[k, x + p + 1, pl.ds(r + dz, 8), :])
             for p in range(GROUP):
-                work(GROUP * g + p)
-            return carry
-
-        lax.fori_loop(start, n // GROUP, go, 0)
-
-    for x in range(GROUP):
-        move(x, x > 0)
-    sweep(lambda x: move(x, True), 1)
-    sweep(load, 0)
+                terms = stress_terms(strain(lambda k, dx, dz: speed_of(k, p + dx, dz)), rl, rm)
+                for c in range(6):
+                    sb[c, x + p + 1, pl.ds(r, 8), :] = s_ref[c, x + p, pl.ds(r - PAD, 8), :] + terms[c]
+        return carry
+
+    move(0, True)
+    lax.fori_loop(1, n // GROUP, lambda g, carry: (move(GROUP * g), carry)[1], 0)
+    lax.fori_loop(0, n // GROUP, load, 0)
     for c, f in enumerate(front):
         raw[c] = s_ref[f, n - 1]
     for copy in fetched:
@@ -272,12 +272,12 @@
     high = m + 16
 
     def s_line(f, r):
-        return pl.Slice((f * (n + 1) + 1) * high + r, n, high)
+        return pl.Slice((f * (n + 2) + 1) * high + r, n, high)
 
     def v_line(k, r):
         return pl.Slice((k * (n + 2) + 1) * high + r, n, high)
 
-    return s_line, v_line, sb.reshape(6 * (n + 1) * high, y), vb.reshape(3 * (n + 2) * high, y)
+    return s_line, v_line, sb.reshape(6 * (n + 2) * high, y), vb.reshape(3 * (n + 2) * high, y)
 
 
 def plane_before(a):
@@ -418,23 +418,25 @@
     for k in range(3):
         v2[v_line(k, first), :] = new[k]
 
-    def move(x):
+    def move(x, planes):
         for r, size in tiles:
-            new = velocity_tile(
-                memo(lambda f, dx, dz: sb[f, x + 1 + dx, pl.ds(r + dz, size), :]),
-                lambda k: vb[k, x + 1, pl.ds(r, size), :],
-                cs(0, r, size),
-                cs(1, r, size),
-            )
-            for k in range(3):
-                vb[k, x + 1, pl.ds(r, size), :] = new[k]
-
-    def load(x):
+            rb, dq = cs(0, r, size), cs(1, r, size)
+            stress_of = memo(lambda f, p, dz: sb[f, x + p + 1, pl.ds(r + dz, size), :])
+            for p in range(planes):
+                new = velocity_tile(
+                    lambda f, dx, dz: stress_of(f, p + dx, dz), lambda k: vb[k, x + p + 1, pl.ds(r, size), :], rb, dq
+                )
+                for k in range(3):
+                    vb[k, x + p + 1, pl.ds(r, size), :] = new[k]
+
+    def load(x, planes):
         for r, size in tiles:
-            g = strain(memo(lambda k, dx, dz: vb[k, x + 1 + dx, pl.ds(r + dz, size), :]))
-            terms = stress_terms(g, cs(2, r, size), cs(3, r, size))
-            for c in range(6):
-                sb[c, x + 1, pl.ds(r, size), :] = sb[c, x + 1, pl.ds(r, size), :] + terms[c]
+            rl, rm = cs(2, r, size), cs(3, r, size)
+            speed_of = memo(lambda k, p, dz: vb[k, x + p + 1, pl.ds(r + dz, size), :])
+            for p in range(planes):
+                terms = stress_terms(strain(lambda k, dx, dz: speed_of(k, p + dx, dz)), rl, rm)
+                for c in range(6):
+                    sb[c, x + p + 1, pl.ds(r, size), :] = sb[c, x + p + 1, pl.ds(r, size), :] + terms[c]
 
     for copy in fetched:
         copy.wait()
@@ -470,27 +472,25 @@
         def _():
             off(x).start()
 
-    def advance(g, carry):
-        x = GROUP * g
-        for p in range(GROUP):
-            move(x + p)
-        for p in range(GROUP):
+    def advance(x, planes):
+        move(x, planes)
+        for p in range(planes):
             send(v_off, x + p, n - 2)
-        for p in range(-1, GROUP - 1):
-            load(x + p)
-        add_near(x - 1, x + GROUP - 1)
-        for p in range(-1, GROUP - 1):
-            send(s_off, x + p, n - 1 - GROUP)
-        return carry
-
-    lax.fori_loop(0, n // GROUP, advance, 0)
-    load(n - 1)
+        load(x - 1, planes)
+        add_near(x - 1, x + planes - 1)
+        for p in range(-1, planes - 1):
+            send(s_off, x + p, n - 3)
+
+    lax.fori_loop(0, n // GROUP - 1, lambda g, carry: (advance(GROUP * g, GROUP), carry)[1], 0)
+    for x in range(n - GROUP, n, 2):
+        advance(x, 2)
+    load(n - 1, 1)
     add_near(n - 1, n)
 
     def finish(x, carry):
         v_off(x).wait()
 
-        @pl.when(x < n - 1 - GROUP)
+        @pl.when(x < n - 3)
         def _():
             s_off(x).wait()
 
@@ -600,18 +600,19 @@
         copy.start()
         return copy
 
-    rest = pltpu.make_async_copy(
-        sb.at[:, pl.ds(n - GROUP, GROUP - 1), pl.ds(PAD, m)], s_out.at[:, pl.ds(n - 1 - GROUP, GROUP - 1)], sems.at[8]
-    )
-    rest.start()
-    copies = [rest]
-    for buf, x, change in ((v0.at[:, 0], 0, dv), (v0.at[:, 1], 1, dw), (v1.at[:, 0], n - 1, ev), (v1.at[:, 1], n - 2, None)):
+    body = pl.ds(PAD, m)
+    copies = [
+        pltpu.make_async_copy(sb.at[:, n - 2, body], s_out.at[:, n - 3], sems.at[7]),
+        pltpu.make_async_copy(vb.at[:, n - 1, body], v_out.at[:, n - 2], sems.at[8]),
+    ]
+    for copy in copies:
+        copy.start()
+    for buf, x, change in ((v0.at[:, 0], 0, dv), (v0.at[:, 1], 1, dw), (v1.at[:, 0], n - 1, ev)):
         for r, size in tiles:
             out, at = pl.ds(r - PAD, size), pl.ds(r, size)
             for k in range(3):
-                old = vb[k, x + 1, at, :]
-                buf[k, out, :] = old if change is None else old + change[k, at, :]
-        copies.append(put(buf, v_out, x, len(copies) - 1))
+                buf[k, out, :] = vb[k, x + 1, at, :] + change[k, at, :]
+        copies.append(put(buf, v_out, x, len(copies) - 2))
     for buf, x, src, ahead, more in (
         (s0.at[:, 0], 0, dv, dw, lambda c, r: ds[c, pl.ds(r, 8), :]),
         (s0.at[:, 1], 1, dw, None, None),
@@ -624,7 +625,7 @@
                 extra = None if more is None else more(c, r)
                 term = terms[c] if extra is None else terms[c] + extra
                 buf[c, out, :] = sb[c, x + 1, at, :] + term
-        copies.append(put(buf, s_out, x, len(copies) - 1))
+        copies.append(put(buf, s_out, x, len(copies) - 2))
     for r, size in tiles:
         out, at = pl.ds(r - PAD, size), pl.ds(r, size)
         rl, rm = cs(2, r, size), cs(3, r, size)
@@ -633,7 +634,7 @@
         for c, term in enumerate((spread + 2.0 * rm * e[0], spread, spread, rm * e[1], rm * e[2], None)):
             old = sb[c, n - 1, at, :]
             s1[c, 1, out, :] = old if term is None else old + term
-    copies.append(put(s1.at[:, 1], s_out, n - 2, len(copies) - 1))
+    copies.append(put(s1.at[:, 1], s_out, n - 2, len(copies) - 2))
     for copy in copies:
         copy.wait()
 
@@ -664,13 +665,13 @@
     def cost(flops, moved):
         return pl.CostEstimate(flops=flops, bytes_accessed=moved, transcendentals=0)
 
-    padded_v, padded_s = kept(3, n + 2, high, y), kept(6, n + 1, high, y)
+    padded_v, padded_s = kept(3, n + 2, high, y), kept(6, n + 2, high, y)
     edge_a, edge_b, coef = pl.pallas_call(
         functools.partial(edge_kernel, n, m, y),
         out_shape=[kept(MSG, y)] * 2 + [kept(4, high, y)],
         in_specs=[HBM] * 4,
         out_specs=[VMEM] * 3,
-        scratch_shapes=[pltpu.VMEM((9, n + 1, 8, y), f32)] * 2 + materials + [dma((6,))],
+        scratch_shapes=[pltpu.VMEM((9, n + 2, 8, y), f32)] * 2 + materials + [dma((6,))],
         compiler_params=room(EDGE_MIB),
         name="edge_levels",
     )(*[pltpu.with_memory_space_constraint(a, pltpu.HBM) for a in (velocity, stress, index, table)])
@@ -719,7 +720,7 @@
         out_specs=[HBM, HBM],
         input_output_aliases={7: 0, 8: 1},
         scratch_shapes=[plane, plane, plane6, plane, plane, plane, plane, plane6, plane, plane]
-        + [pltpu.VMEM((3, 2, m, y), f32)] * 2
+        + [pltpu.VMEM((3, 2, m, y), f32), pltpu.VMEM((3, 1, m, y), f32)]
         + [pltpu.VMEM((6, 2, m, y), f32)] * 2
         + [dma((9,))],
         compiler_params=room(SMALL_MIB),

time: 16.9 us -> 16.6 us (0.982)
  Pallas kernels: 9.59 us -> 8.77 us
  waiting for transfers between devices: 2.21 us -> 2.87 us
    ppermute x4, waiting for transfers between devices: 2.21 us -> 2.87 us  [swap(): lax.ppermute(block, axes, swap_pairs([lax.axis_size(a) for a in axes], al...]
    pallas_call x1, Pallas kernels: 2.49 us -> 2.12 us  [local(): pl.pallas_call(functools.partial(load_kernel, n, m, y), out_shape=[padded...]
    pallas_call x1, Pallas kernels: 3.61 us -> 3.33 us  [local(): pl.pallas_call(functools.partial(rest_kernel, n, m, y), out_shape=[padded...]
    pallas_call x1, Pallas kernels: 1.67 us -> 1.5 us  [local(): pl.pallas_call(functools.partial(join_kernel, n, m, y), out_shape=[outsid...]
  transfers between devices with their start and end apart: 4 -> 4, of which waited for: 2 -> 3; matrix products, arithmetic and copies ran while one was open for 0% -> 0% of each run, Pallas kernels for 37% -> 33%
where the time goes in v4:
time: 16.6 us; the launch traced here: 16.4 us
  Pallas kernels  8.77 us (53%)
  starting transfers between devices  3.34 us (20%)
  waiting for transfers between devices  2.87 us (17%)
  between operations  1.41 us (8%)
    ppermute x4, starting transfers between devices, swap(): lax.ppermute(block, axes, swap_pairs([lax.axis_size(a) for a in axes], al...  3.34 us
    pallas_call x1, Pallas kernels, local(): pl.pallas_call(functools.partial(rest_kernel, n, m, y), out_shape=[padded...  3.33 us
    ppermute x4, waiting for transfers between devices, swap(): lax.ppermute(block, axes, swap_pairs([lax.axis_size(a) for a in axes], al...  2.87 us
    pallas_call x1, Pallas kernels, local(): pl.pallas_call(functools.partial(load_kernel, n, m, y), out_shape=[padded...  2.12 us
    pallas_call x1, Pallas kernels, local(): pl.pallas_call(functools.partial(edge_kernel, n, m, y), out_shape=[kept(M...  1.59 us
    pallas_call x1, Pallas kernels, local(): pl.pallas_call(functools.partial(join_kernel, n, m, y), out_shape=[outsid...  1.5 us
  transfers between devices with their start and end apart: 4, of which 3 were waited for; matrix products, arithmetic and copies ran while one was open for 0% of the time, Pallas kernels for 33%

profile of v4, /device:TPU:16, one launch (start us, length us, event | category | flops | bytes accessed | tf_op | source)
XLA Modules:
  0.0 16.4 jit_solution(11528908546315993619)
XLA Ops:
  0.6 0.0 copy-start
  0.6 0.0 copy-start.1
  0.7 0.0 copy-start.2
  0.7 0.0 copy-start.3
  0.7 0.0 copy-start.4
  0.7 0.0 copy-start.5
  0.7 1.6 %edge_levels.1 = (f32[200,128]{1,0:T(8,128)S(1)}, f32[200,128]{1,0:T(8,128)S(1)}, f32[4,88,128]{2,1,0:T(8,128)S(1)}) custom-call(f32[3,16,72,128]{3,2,1,0:T(8,128)} %v_ref.3, f32[6,16,72,128]{3,2,1,0:T(8,128)} %s_ref.3, s32[72]{0:T(128)} %index.1, f32[4,8]{1,0:T(4,128)} %bitcast.1), custom_call_target="tpu_custom_call" | custom-call | tf_op jit(solution)/shard_map/edge_levels/pallas_call | solution.py:669
  2.3 1.6 %collective-permute-start = (f32[200,128]{1,0:T(8,128)S(1)}, f32[200,128]{1,0:T(8,128)S(1)}, u32[]{:S(2)}, u32[]{:S(2)}) collective-permute-start(f32[200,128]{1,0:T(8,128)S(1)} %get-tuple-element.22.edge_a), channel_id=1, source_target_pairs={{0,1},{1,0},{2,3},{3,2},{4,5},{5,4},{6,7},{7,6},{8,9},{9,8},{10,11... | collective-permute-start | bytes 307208 | tf_op jit(solution)/shard_map/ppermute | solution.py:42
  3.9 0.0 collective-permute-start.1
  4.6 0.0 copy-done
  4.6 0.0 copy-done.1
  4.6 0.0 copy-done.2
  4.6 0.0 copy-done.3
  4.6 0.0 copy-done.4
  4.6 2.1 %load_block.1 = (f32[3,18,88,128]{3,2,1,0:T(8,128)S(1)}, f32[6,18,88,128]{3,2,1,0:T(8,128)S(1)}, f32[3,72,128]{2,1,0:T(8,128)S(1)}, f32[4,88,128]{2,1,0:T(8,128)S(1)}) custom-call(f32[3,16,72,128]{3,2,1,0:T(8,128)S(1)} %copy-done.1, f32[6,16,72,128]{3,2,1,0:T(8,128)S(1)} %copy-done, ...), custom_call_target="tpu_custom_call", output_to_operand_aliasing={{3}: (2, {})} | custom-call | flops 8847360 | bytes 5308416 | tf_op jit(solution)/shard_map/load_block/pallas_call | solution.py:680
  6.8 0.2 %collective-permute-done.got_a = f32[200,128]{1,0:T(8,128)S(1)} collective-permute-done((f32[200,128]{1,0:T(8,128)S(1)}, f32[200,128]{1,0:T(8,128)S(1)}, u32[]{:S(2)}, u32[]{:S(2)}) %collective-permute-start) | collective-permute-done | bytes 102432 | tf_op jit(solution)/shard_map/ppermute | solution.py:42
  7.0 1.6 %collective-permute-done.1.got_b = f32[200,128]{1,0:T(8,128)S(1)} collective-permute-done((f32[200,128]{1,0:T(8,128)S(1)}, f32[200,128]{1,0:T(8,128)S(1)}, u32[]{:S(2)}, u32[]{:S(2)}) %collective-permute-start.1) | collective-permute-done | bytes 102432 | tf_op jit(solution)/shard_map/ppermute | solution.py:42
  8.6 0.2 %edge_planes.1 = (f32[448,128]{1,0:T(8,128)S(1)}, f32[448,128]{1,0:T(8,128)S(1)}, f32[3,18,88,128]{3,2,1,0:T(8,128)S(1)}, f32[6,18,88,128]{3,2,1,0:T(8,128)S(1)}, f32[4,88,128]{2,1,0:T(8,128)S(1)}) custom-call(f32[200,128]{1,0:T(8,128)S(1)} %collective-permute-done.got_a, ...), custom_call_target="tpu_custom_call", output_to_operand_aliasing={{2}: (4, {}), {3}: (5, {}), {4}: (7, {})} | custom-call | tf_op jit(solution)/shard_map/edge_planes/pallas_call | solution.py:691
  8.8 1.6 %collective-permute-start.2 = (f32[448,128]{1,0:T(8,128)S(1)}, f32[448,128]{1,0:T(8,128)S(1)}, u32[]{:S(2)}, u32[]{:S(2)}) collective-permute-start(f32[448,128]{1,0:T(8,128)S(1)} %get-tuple-element.29.own_b), channel_id=1, source_target_pairs={{0,16},{1,17},{2,18},{3,19},{4,8},{5,9},{6,10},{7,11},{8,4},{9,5},... | collective-permute-start | bytes 688136 | tf_op jit(solution)/shard_map/ppermute | solution.py:42
  10.4 0.1 collective-permute-start.3
  10.5 3.3 %both_steps.1 = (f32[3,18,88,128]{3,2,1,0:T(8,128)S(1)}, f32[6,18,88,128]{3,2,1,0:T(8,128)S(1)}, f32[3,16,72,128]{3,2,1,0:T(8,128)}, f32[6,16,72,128]{3,2,1,0:T(8,128)}) custom-call(f32[3,18,88,128]{3,2,1,0:T(8,128)S(1)} %get-tuple-element.32.v_in, f32[6,18,88,128]{3,2,1,0:T(8,128)S(1)} %get-tuple-element.33.s_in, ...), custom_call_target="tpu_custom_call", output_to_operand_aliasing={{0}: (0, {}), {1}: (1, {})} | custom-call | flops 8847360 | bytes 5308416 | tf_op jit(solution)/shard_map/both_steps/pallas_call | solution.py:703
  13.9 1.0 %collective-permute-done.2.next_b = f32[448,128]{1,0:T(8,128)S(1)} collective-permute-done((f32[448,128]{1,0:T(8,128)S(1)}, f32[448,128]{1,0:T(8,128)S(1)}, u32[]{:S(2)}, u32[]{:S(2)}) %collective-permute-start.2) | collective-permute-done | bytes 229408 | tf_op jit(solution)/shard_map/ppermute | solution.py:42
  14.9 0.0 collective-permute-done.3.next_a
  14.9 1.5 %join_neighbours.1 = (f32[3,16,72,128]{3,2,1,0:T(8,128)}, f32[6,16,72,128]{3,2,1,0:T(8,128)}) custom-call(f32[448,128]{1,0:T(8,128)S(1)} %collective-permute-done.2.next_b, f32[448,128]{1,0:T(8,128)S(1)} %collective-permute-done.3.next_a, f32[448,128]{1,0:T(8,128)S(1)} %get-tuple-element.30.own_a, ...), custom_call_target="tpu_custom_call", output_to_operand_aliasing={{0}: (7, {}), {1}: (8, {})} | custom-call | tf_op jit(solution)/shard_map/join_neighbours/pallas_call | solution.py:716
  (1 shorter events, 0.0 us)
Async XLA Ops:
  0.6 4.0 %copy-start = (f32[6,16,72,128]{3,2,1,0:T(8,128)S(1)}, f32[6,16,72,128]{3,2,1,0:T(8,128)}, u32[]{:S(2)}) copy-start(f32[6,16,72,128]{3,2,1,0:T(8,128)} %s_ref.3) | copy-start | bytes 10616836
  0.6 4.0 %copy-start.1 = (f32[3,16,72,128]{3,2,1,0:T(8,128)S(1)}, f32[3,16,72,128]{3,2,1,0:T(8,128)}, u32[]{:S(2)}) copy-start(f32[3,16,72,128]{3,2,1,0:T(8,128)} %v_ref.3) | copy-start | bytes 5308420
  0.7 4.0 %copy-start.2 = (s32[16]{0:T(128)S(1)}, s32[16]{0:T(128)}, u32[]{:S(2)}) copy-start(s32[16]{0:T(128)} %refs_0_.3) | copy-start | bytes 196
  0.7 4.0 %copy-start.3 = (s32[16]{0:T(128)S(1)}, s32[16]{0:T(128)}, u32[]{:S(2)}) copy-start(s32[16]{0:T(128)} %refs_1_.3) | copy-start | bytes 196
  0.7 4.0 %copy-start.4 = (s32[16]{0:T(128)S(1)}, s32[16]{0:T(128)}, u32[]{:S(2)}) copy-start(s32[16]{0:T(128)} %refs_2_.3) | copy-start | bytes 196
  0.7 4.0 %copy-start.5 = (f32[16]{0:T(128)S(1)}, f32[16]{0:T(128)}, u32[]{:S(2)}) copy-start(f32[16]{0:T(128)} %refs_3_.3) | copy-start | bytes 196
  2.3 4.7 %collective-permute-start = (f32[200,128]{1,0:T(8,128)S(1)}, f32[200,128]{1,0:T(8,128)S(1)}, u32[]{:S(2)}, u32[]{:S(2)}) collective-permute-start(f32[200,128]{1,0:T(8,128)S(1)} %get-tuple-element.22.edge_a), channel_id=1, source_target_pairs={{0,1},{1,0},{2,3},{3,2},{4,5},{5,4},{6,7},{7,6},{8,9},{9,8},{10,11... | collective-permute-start | bytes 307208 | tf_op jit(solution)/shard_map/ppermute | solution.py:42
  3.9 4.7 %collective-permute-start.1 = (f32[200,128]{1,0:T(8,128)S(1)}, f32[200,128]{1,0:T(8,128)S(1)}, u32[]{:S(2)}, u32[]{:S(2)}) collective-permute-start(f32[200,128]{1,0:T(8,128)S(1)} %get-tuple-element.21.edge_b), channel_id=1, source_target_pairs={{0,4},{1,2},{2,1},{3,7},{4,0},{5,6},{6,5},{7,3},{8,12},{9,10},{10,... | collective-permute-start | bytes 307208 | tf_op jit(solution)/shard_map/ppermute | solution.py:42
  8.8 6.1 %collective-permute-start.2 = (f32[448,128]{1,0:T(8,128)S(1)}, f32[448,128]{1,0:T(8,128)S(1)}, u32[]{:S(2)}, u32[]{:S(2)}) collective-permute-start(f32[448,128]{1,0:T(8,128)S(1)} %get-tuple-element.29.own_b), channel_id=1, source_target_pairs={{0,16},{1,17},{2,18},{3,19},{4,8},{5,9},{6,10},{7,11},{8,4},{9,5},... | collective-permute-start | bytes 688136 | tf_op jit(solution)/shard_map/ppermute | solution.py:42
  10.4 4.5 %collective-permute-start.3 = (f32[448,128]{1,0:T(8,128)S(1)}, f32[448,128]{1,0:T(8,128)S(1)}, u32[]{:S(2)}, u32[]{:S(2)}) collective-permute-start(f32[448,128]{1,0:T(8,128)S(1)} %get-tuple-element.30.own_a), channel_id=1, source_target_pairs={{0,4},{1,5},{2,6},{3,7},{4,0},{5,1},{6,2},{7,3},{8,12},{9,13},{10,... | collective-permute-start | bytes 688136 | tf_op jit(solution)/shard_map/ppermute | solution.py:42

commit v5 on v4

--- a/solution.py
+++ b/solution.py
@@ -475,28 +475,25 @@
     def advance(x, planes):
         move(x, planes)
         for p in range(planes):
-            send(v_off, x + p, n - 2)
+            send(v_off, x + p, n - 1)
         load(x - 1, planes)
         add_near(x - 1, x + planes - 1)
         for p in range(-1, planes - 1):
-            send(s_off, x + p, n - 3)
+            send(s_off, x + p, n - 2)
 
     lax.fori_loop(0, n // GROUP - 1, lambda g, carry: (advance(GROUP * g, GROUP), carry)[1], 0)
-    for x in range(n - GROUP, n, 2):
-        advance(x, 2)
+    for x, planes in ((n - GROUP, GROUP - 4), (n - 4, 2), (n - 2, 2)):
+        advance(x, planes)
     load(n - 1, 1)
     add_near(n - 1, n)
 
     def finish(x, carry):
         v_off(x).wait()
-
-        @pl.when(x < n - 3)
-        def _():
-            s_off(x).wait()
-
+        s_off(x).wait()
         return carry
 
     lax.fori_loop(2, n - 2, finish, 0)
+    v_off(n - 2).wait()
 
 
 def join_kernel(n, m, y, next_b, next_a, own_a, own_b, coef, vb, sb, v_in, s_in, v_out, s_out, *scratch):
@@ -600,19 +597,13 @@
         copy.start()
         return copy
 
-    body = pl.ds(PAD, m)
-    copies = [
-        pltpu.make_async_copy(sb.at[:, n - 2, body], s_out.at[:, n - 3], sems.at[7]),
-        pltpu.make_async_copy(vb.at[:, n - 1, body], v_out.at[:, n - 2], sems.at[8]),
-    ]
-    for copy in copies:
-        copy.start()
+    copies = []
     for buf, x, change in ((v0.at[:, 0], 0, dv), (v0.at[:, 1], 1, dw), (v1.at[:, 0], n - 1, ev)):
         for r, size in tiles:
             out, at = pl.ds(r - PAD, size), pl.ds(r, size)
             for k in range(3):
                 buf[k, out, :] = vb[k, x + 1, at, :] + change[k, at, :]
-        copies.append(put(buf, v_out, x, len(copies) - 2))
+        copies.append(put(buf, v_out, x, len(copies)))
     for buf, x, src, ahead, more in (
         (s0.at[:, 0], 0, dv, dw, lambda c, r: ds[c, pl.ds(r, 8), :]),
         (s0.at[:, 1], 1, dw, None, None),
@@ -625,7 +616,7 @@
                 extra = None if more is None else more(c, r)
                 term = terms[c] if extra is None else terms[c] + extra
                 buf[c, out, :] = sb[c, x + 1, at, :] + term
-        copies.append(put(buf, s_out, x, len(copies) - 2))
+        copies.append(put(buf, s_out, x, len(copies)))
     for r, size in tiles:
         out, at = pl.ds(r - PAD, size), pl.ds(r, size)
         rl, rm = cs(2, r, size), cs(3, r, size)
@@ -634,7 +625,7 @@
         for c, term in enumerate((spread + 2.0 * rm * e[0], spread, spread, rm * e[1], rm * e[2], None)):
             old = sb[c, n - 1, at, :]
             s1[c, 1, out, :] = old if term is None else old + term
-    copies.append(put(s1.at[:, 1], s_out, n - 2, len(copies) - 2))
+    copies.append(put(s1.at[:, 1], s_out, n - 2, len(copies)))
     for copy in copies:
         copy.wait()
 
@@ -722,7 +713,7 @@
         scratch_shapes=[plane, plane, plane6, plane, plane, plane, plane, plane6, plane, plane]
         + [pltpu.VMEM((3, 2, m, y), f32), pltpu.VMEM((3, 1, m, y), f32)]
         + [pltpu.VMEM((6, 2, m, y), f32)] * 2
-        + [dma((9,))],
+        + [dma((7,))],
         compiler_params=room(SMALL_MIB),
         name="join_neighbours",
     )(next_b, next_a, plane_a, plane_b, coef, vb, sb, v_own, s_own)

time: 16.6 us -> 16.5 us (level)
  transfers between devices with their start and end apart: 4 -> 4, of which waited for: 3 -> 3; matrix products, arithmetic and copies ran while one was open for 0% -> 0% of each run, Pallas kernels for 33% -> 34%
where the time goes in v5:
time: 16.5 us; the launch traced here: 16.4 us
  Pallas kernels  8.83 us (54%)
  starting transfers between devices  3.34 us (20%)
  waiting for transfers between devices  2.77 us (17%)
  between operations  1.41 us (9%)
    pallas_call x1, Pallas kernels, local(): pl.pallas_call(functools.partial(rest_kernel, n, m, y), out_shape=[padded...  3.43 us
    ppermute x4, starting transfers between devices, swap(): lax.ppermute(block, axes, swap_pairs([lax.axis_size(a) for a in axes], al...  3.34 us
    ppermute x4, waiting for transfers between devices, swap(): lax.ppermute(block, axes, swap_pairs([lax.axis_size(a) for a in axes], al...  2.77 us
    pallas_call x1, Pallas kernels, local(): pl.pallas_call(functools.partial(load_kernel, n, m, y), out_shape=[padded...  2.12 us
    pallas_call x1, Pallas kernels, local(): pl.pallas_call(functools.partial(edge_kernel, n, m, y), out_shape=[kept(M...  1.59 us
    pallas_call x1, Pallas kernels, local(): pl.pallas_call(functools.partial(join_kernel, n, m, y), out_shape=[outsid...  1.46 us
  transfers between devices with their start and end apart: 4, of which 3 were waited for; matrix products, arithmetic and copies ran while one was open for 0% of the time, Pallas kernels for 34%

profile of v5, /device:TPU:16, one launch (start us, length us, event | category | flops | bytes accessed | tf_op | source)
XLA Modules:
  0.0 16.4 jit_solution(13616058455436132303)
XLA Ops:
  0.6 0.0 copy-start
  0.6 0.0 copy-start.1
  0.7 0.0 copy-start.2
  0.7 0.0 copy-start.3
  0.7 0.0 copy-start.4
  0.7 0.0 copy-start.5
  0.7 1.6 %edge_levels.1 = (f32[200,128]{1,0:T(8,128)S(1)}, f32[200,128]{1,0:T(8,128)S(1)}, f32[4,88,128]{2,1,0:T(8,128)S(1)}) custom-call(f32[3,16,72,128]{3,2,1,0:T(8,128)} %v_ref.3, f32[6,16,72,128]{3,2,1,0:T(8,128)} %s_ref.3, s32[72]{0:T(128)} %index.1, f32[4,8]{1,0:T(4,128)} %bitcast.1), custom_call_target="tpu_custom_call" | custom-call | tf_op jit(solution)/shard_map/edge_levels/pallas_call | solution.py:660
  2.3 1.6 %collective-permute-start = (f32[200,128]{1,0:T(8,128)S(1)}, f32[200,128]{1,0:T(8,128)S(1)}, u32[]{:S(2)}, u32[]{:S(2)}) collective-permute-start(f32[200,128]{1,0:T(8,128)S(1)} %get-tuple-element.22.edge_a), channel_id=1, source_target_pairs={{0,1},{1,0},{2,3},{3,2},{4,5},{5,4},{6,7},{7,6},{8,9},{9,8},{10,11... | collective-permute-start | bytes 307208 | tf_op jit(solution)/shard_map/ppermute | solution.py:42
  3.9 0.0 collective-permute-start.1
  4.6 0.0 copy-done
  4.6 0.0 copy-done.1
  4.6 0.0 copy-done.2
  4.6 0.0 copy-done.3
  4.6 0.0 copy-done.4
  4.6 2.1 %load_block.1 = (f32[3,18,88,128]{3,2,1,0:T(8,128)S(1)}, f32[6,18,88,128]{3,2,1,0:T(8,128)S(1)}, f32[3,72,128]{2,1,0:T(8,128)S(1)}, f32[4,88,128]{2,1,0:T(8,128)S(1)}) custom-call(f32[3,16,72,128]{3,2,1,0:T(8,128)S(1)} %copy-done.1, f32[6,16,72,128]{3,2,1,0:T(8,128)S(1)} %copy-done, ...), custom_call_target="tpu_custom_call", output_to_operand_aliasing={{3}: (2, {})} | custom-call | flops 8847360 | bytes 5308416 | tf_op jit(solution)/shard_map/load_block/pallas_call | solution.py:671
  6.8 0.2 %collective-permute-done.got_a = f32[200,128]{1,0:T(8,128)S(1)} collective-permute-done((f32[200,128]{1,0:T(8,128)S(1)}, f32[200,128]{1,0:T(8,128)S(1)}, u32[]{:S(2)}, u32[]{:S(2)}) %collective-permute-start) | collective-permute-done | bytes 102432 | tf_op jit(solution)/shard_map/ppermute | solution.py:42
  7.0 1.6 %collective-permute-done.1.got_b = f32[200,128]{1,0:T(8,128)S(1)} collective-permute-done((f32[200,128]{1,0:T(8,128)S(1)}, f32[200,128]{1,0:T(8,128)S(1)}, u32[]{:S(2)}, u32[]{:S(2)}) %collective-permute-start.1) | collective-permute-done | bytes 102432 | tf_op jit(solution)/shard_map/ppermute | solution.py:42
  8.6 0.2 %edge_planes.1 = (f32[448,128]{1,0:T(8,128)S(1)}, f32[448,128]{1,0:T(8,128)S(1)}, f32[3,18,88,128]{3,2,1,0:T(8,128)S(1)}, f32[6,18,88,128]{3,2,1,0:T(8,128)S(1)}, f32[4,88,128]{2,1,0:T(8,128)S(1)}) custom-call(f32[200,128]{1,0:T(8,128)S(1)} %collective-permute-done.got_a, ...), custom_call_target="tpu_custom_call", output_to_operand_aliasing={{2}: (4, {}), {3}: (5, {}), {4}: (7, {})} | custom-call | tf_op jit(solution)/shard_map/edge_planes/pallas_call | solution.py:682
  8.8 1.6 %collective-permute-start.2 = (f32[448,128]{1,0:T(8,128)S(1)}, f32[448,128]{1,0:T(8,128)S(1)}, u32[]{:S(2)}, u32[]{:S(2)}) collective-permute-start(f32[448,128]{1,0:T(8,128)S(1)} %get-tuple-element.29.own_b), channel_id=1, source_target_pairs={{0,16},{1,17},{2,18},{3,19},{4,8},{5,9},{6,10},{7,11},{8,4},{9,5},... | collective-permute-start | bytes 688136 | tf_op jit(solution)/shard_map/ppermute | solution.py:42
  10.4 0.1 collective-permute-start.3
  10.5 3.4 %both_steps.1 = (f32[3,18,88,128]{3,2,1,0:T(8,128)S(1)}, f32[6,18,88,128]{3,2,1,0:T(8,128)S(1)}, f32[3,16,72,128]{3,2,1,0:T(8,128)}, f32[6,16,72,128]{3,2,1,0:T(8,128)}) custom-call(f32[3,18,88,128]{3,2,1,0:T(8,128)S(1)} %get-tuple-element.32.v_in, f32[6,18,88,128]{3,2,1,0:T(8,128)S(1)} %get-tuple-element.33.s_in, ...), custom_call_target="tpu_custom_call", output_to_operand_aliasing={{0}: (0, {}), {1}: (1, {})} | custom-call | flops 8847360 | bytes 5308416 | tf_op jit(solution)/shard_map/both_steps/pallas_call | solution.py:694
  14.0 0.9 %collective-permute-done.2.next_b = f32[448,128]{1,0:T(8,128)S(1)} collective-permute-done((f32[448,128]{1,0:T(8,128)S(1)}, f32[448,128]{1,0:T(8,128)S(1)}, u32[]{:S(2)}, u32[]{:S(2)}) %collective-permute-start.2) | collective-permute-done | bytes 229408 | tf_op jit(solution)/shard_map/ppermute | solution.py:42
  14.9 0.0 collective-permute-done.3.next_a
  14.9 1.5 %join_neighbours.1 = (f32[3,16,72,128]{3,2,1,0:T(8,128)}, f32[6,16,72,128]{3,2,1,0:T(8,128)}) custom-call(f32[448,128]{1,0:T(8,128)S(1)} %collective-permute-done.2.next_b, f32[448,128]{1,0:T(8,128)S(1)} %collective-permute-done.3.next_a, f32[448,128]{1,0:T(8,128)S(1)} %get-tuple-element.30.own_a, ...), custom_call_target="tpu_custom_call", output_to_operand_aliasing={{0}: (7, {}), {1}: (8, {})} | custom-call | tf_op jit(solution)/shard_map/join_neighbours/pallas_call | solution.py:707
  (1 shorter events, 0.0 us)
Async XLA Ops:
  0.6 4.0 %copy-start = (f32[6,16,72,128]{3,2,1,0:T(8,128)S(1)}, f32[6,16,72,128]{3,2,1,0:T(8,128)}, u32[]{:S(2)}) copy-start(f32[6,16,72,128]{3,2,1,0:T(8,128)} %s_ref.3) | copy-start | bytes 10616836
  0.6 4.0 %copy-start.1 = (f32[3,16,72,128]{3,2,1,0:T(8,128)S(1)}, f32[3,16,72,128]{3,2,1,0:T(8,128)}, u32[]{:S(2)}) copy-start(f32[3,16,72,128]{3,2,1,0:T(8,128)} %v_ref.3) | copy-start | bytes 5308420
  0.7 4.0 %copy-start.2 = (s32[16]{0:T(128)S(1)}, s32[16]{0:T(128)}, u32[]{:S(2)}) copy-start(s32[16]{0:T(128)} %refs_0_.3) | copy-start | bytes 196
  0.7 4.0 %copy-start.3 = (s32[16]{0:T(128)S(1)}, s32[16]{0:T(128)}, u32[]{:S(2)}) copy-start(s32[16]{0:T(128)} %refs_1_.3) | copy-start | bytes 196
  0.7 4.0 %copy-start.4 = (s32[16]{0:T(128)S(1)}, s32[16]{0:T(128)}, u32[]{:S(2)}) copy-start(s32[16]{0:T(128)} %refs_2_.3) | copy-start | bytes 196
  0.7 4.0 %copy-start.5 = (f32[16]{0:T(128)S(1)}, f32[16]{0:T(128)}, u32[]{:S(2)}) copy-start(f32[16]{0:T(128)} %refs_3_.3) | copy-start | bytes 196
  2.3 4.7 %collective-permute-start = (f32[200,128]{1,0:T(8,128)S(1)}, f32[200,128]{1,0:T(8,128)S(1)}, u32[]{:S(2)}, u32[]{:S(2)}) collective-permute-start(f32[200,128]{1,0:T(8,128)S(1)} %get-tuple-element.22.edge_a), channel_id=1, source_target_pairs={{0,1},{1,0},{2,3},{3,2},{4,5},{5,4},{6,7},{7,6},{8,9},{9,8},{10,11... | collective-permute-start | bytes 307208 | tf_op jit(solution)/shard_map/ppermute | solution.py:42
  3.9 4.7 %collective-permute-start.1 = (f32[200,128]{1,0:T(8,128)S(1)}, f32[200,128]{1,0:T(8,128)S(1)}, u32[]{:S(2)}, u32[]{:S(2)}) collective-permute-start(f32[200,128]{1,0:T(8,128)S(1)} %get-tuple-element.21.edge_b), channel_id=1, source_target_pairs={{0,4},{1,2},{2,1},{3,7},{4,0},{5,6},{6,5},{7,3},{8,12},{9,10},{10,... | collective-permute-start | bytes 307208 | tf_op jit(solution)/shard_map/ppermute | solution.py:42
  8.8 6.1 %collective-permute-start.2 = (f32[448,128]{1,0:T(8,128)S(1)}, f32[448,128]{1,0:T(8,128)S(1)}, u32[]{:S(2)}, u32[]{:S(2)}) collective-permute-start(f32[448,128]{1,0:T(8,128)S(1)} %get-tuple-element.29.own_b), channel_id=1, source_target_pairs={{0,16},{1,17},{2,18},{3,19},{4,8},{5,9},{6,10},{7,11},{8,4},{9,5},... | collective-permute-start | bytes 688136 | tf_op jit(solution)/shard_map/ppermute | solution.py:42
  10.4 4.5 %collective-permute-start.3 = (f32[448,128]{1,0:T(8,128)S(1)}, f32[448,128]{1,0:T(8,128)S(1)}, u32[]{:S(2)}, u32[]{:S(2)}) collective-permute-start(f32[448,128]{1,0:T(8,128)S(1)} %get-tuple-element.30.own_a), channel_id=1, source_target_pairs={{0,4},{1,5},{2,6},{3,7},{4,0},{5,1},{6,2},{7,3},{8,12},{9,13},{10,... | collective-permute-start | bytes 688136 | tf_op jit(solution)/shard_map/ppermute | solution.py:42

commit v6 on v5

--- a/solution.py
+++ b/solution.py
@@ -187,7 +187,7 @@
 
 def load_kernel(n, m, y, v_ref, s_ref, coef_in, split, *refs):
     sources, (vb, sb, raw, coef), scratch = refs[:4], refs[4:8], refs[8:]
-    sx, sz, sy, amp, small = scratch
+    sx, sz, sy, amp, near_x, near_z, near_y, near_amp, small = scratch
     del coef_in
     fetched = fetch_sources(sources, (sx, sz, sy, amp), small)
     for f in front:
@@ -252,20 +252,20 @@
     for copy in fetched:
         copy.wait()
     x_at, z_at = lax.axis_index("horiz") * n, lax.axis_index("vert") * m
-
-    def add(i, carry):
+    found = jnp.int32(0)
+    for i in range(sx.shape[0]):
         x, z = sx[i] - x_at, sz[i] - z_at
-
-        @pl.when((x >= 0) & (x < n) & (z >= -1) & (z <= m))
-        def _():
-            row = jnp.where(lane_of((1, y)) == sy[i], courant * wavelet[0] * amp[i], 0.0)
-            at = pl.ds(PAD + z, 1)
-            for c in range(3):
-                sb[c, x + 1, at, :] = sb[c, x + 1, at, :] + row
-
+        near_x[found], near_z[found], near_y[found], near_amp[found] = x, z, sy[i], amp[i]
+        found = found + ((x >= 0) & (x < n) & (z >= -1) & (z <= m)).astype(jnp.int32)
+
+    def add(j, carry):
+        x, at = near_x[j], pl.ds(PAD + near_z[j], 1)
+        row = jnp.where(lane_of((1, y)) == near_y[j], courant * wavelet[0] * near_amp[j], 0.0)
+        for c in range(3):
+            sb[c, x + 1, at, :] = sb[c, x + 1, at, :] + row
         return carry
 
-    lax.fori_loop(0, sx.shape[0], add, 0)
+    lax.fori_loop(0, found, add, 0)
 
 
 def lines(n, m, y, vb, sb):
@@ -674,7 +674,7 @@
         in_specs=[VMEM, VMEM, VMEM, SMEM] + [ANY] * 4,
         out_specs=[VMEM] * 4,
         input_output_aliases={2: 3},
-        scratch_shapes=[*held, dma((4,))],
+        scratch_shapes=[*held, *near, dma((4,))],
         compiler_params=room(LOAD_MIB),
         cost_estimate=cost(60 * n * m * y, 4 * 9 * n * m * y),
         name="load_block",

time: 16.5 us -> 16.5 us (level)
  Pallas kernels: 8.83 us -> 8.66 us
  waiting for transfers between devices: 2.77 us -> 2.94 us
    ppermute x4, waiting for transfers between devices: 2.77 us -> 2.94 us  [swap(): lax.ppermute(block, axes, swap_pairs([lax.axis_size(a) for a in axes], al...]
    pallas_call x1, Pallas kernels: 2.12 us -> 1.95 us  [local(): pl.pallas_call(functools.partial(load_kernel, n, m, y), out_shape=[padded...]
  transfers between devices with their start and end apart: 4 -> 4, of which waited for: 3 -> 3; matrix products, arithmetic and copies ran while one was open for 0% -> 0% of each run, Pallas kernels for 34% -> 33%
where the time goes in v6:
time: 16.5 us; the launch traced here: 16.4 us
  Pallas kernels  8.66 us (52%)
  starting transfers between devices  3.34 us (20%)
  waiting for transfers between devices  2.94 us (18%)
  between operations  1.41 us (9%)
    pallas_call x1, Pallas kernels, local(): pl.pallas_call(functools.partial(rest_kernel, n, m, y), out_shape=[padded...  3.43 us
    ppermute x4, starting transfers between devices, swap(): lax.ppermute(block, axes, swap_pairs([lax.axis_size(a) for a in axes], al...  3.34 us
    ppermute x4, waiting for transfers between devices, swap(): lax.ppermute(block, axes, swap_pairs([lax.axis_size(a) for a in axes], al...  2.94 us
    pallas_call x1, Pallas kernels, local(): pl.pallas_call(functools.partial(load_kernel, n, m, y), out_shape=[padded...  1.95 us
    pallas_call x1, Pallas kernels, local(): pl.pallas_call(functools.partial(edge_kernel, n, m, y), out_shape=[kept(M...  1.59 us
    pallas_call x1, Pallas kernels, local(): pl.pallas_call(functools.partial(join_kernel, n, m, y), out_shape=[outsid...  1.46 us
  transfers between devices with their start and end apart: 4, of which 3 were waited for; matrix products, arithmetic and copies ran while one was open for 0% of the time, Pallas kernels for 33%

profile of v6, /device:TPU:16, one launch (start us, length us, event | category | flops | bytes accessed | tf_op | source)
XLA Modules:
  0.0 16.4 jit_solution(13940262405026877333)
XLA Ops:
  0.6 0.0 copy-start
  0.6 0.0 copy-start.1
  0.7 0.0 copy-start.2
  0.7 0.0 copy-start.3
  0.7 0.0 copy-start.4
  0.7 0.0 copy-start.5
  0.7 1.6 %edge_levels.1 = (f32[200,128]{1,0:T(8,128)S(1)}, f32[200,128]{1,0:T(8,128)S(1)}, f32[4,88,128]{2,1,0:T(8,128)S(1)}) custom-call(f32[3,16,72,128]{3,2,1,0:T(8,128)} %v_ref.3, f32[6,16,72,128]{3,2,1,0:T(8,128)} %s_ref.3, s32[72]{0:T(128)} %index.1, f32[4,8]{1,0:T(4,128)} %bitcast.1), custom_call_target="tpu_custom_call" | custom-call | tf_op jit(solution)/shard_map/edge_levels/pallas_call | solution.py:660
  2.3 1.6 %collective-permute-start = (f32[200,128]{1,0:T(8,128)S(1)}, f32[200,128]{1,0:T(8,128)S(1)}, u32[]{:S(2)}, u32[]{:S(2)}) collective-permute-start(f32[200,128]{1,0:T(8,128)S(1)} %get-tuple-element.22.edge_a), channel_id=1, source_target_pairs={{0,1},{1,0},{2,3},{3,2},{4,5},{5,4},{6,7},{7,6},{8,9},{9,8},{10,11... | collective-permute-start | bytes 307208 | tf_op jit(solution)/shard_map/ppermute | solution.py:42
  3.9 0.0 collective-permute-start.1
  4.6 0.0 copy-done
  4.6 0.0 copy-done.1
  4.6 0.0 copy-done.2
  4.6 0.0 copy-done.3
  4.6 0.0 copy-done.4
  4.6 1.9 %load_block.1 = (f32[3,18,88,128]{3,2,1,0:T(8,128)S(1)}, f32[6,18,88,128]{3,2,1,0:T(8,128)S(1)}, f32[3,72,128]{2,1,0:T(8,128)S(1)}, f32[4,88,128]{2,1,0:T(8,128)S(1)}) custom-call(f32[3,16,72,128]{3,2,1,0:T(8,128)S(1)} %copy-done.1, f32[6,16,72,128]{3,2,1,0:T(8,128)S(1)} %copy-done, ...), custom_call_target="tpu_custom_call", output_to_operand_aliasing={{3}: (2, {})} | custom-call | flops 8847360 | bytes 5308416 | tf_op jit(solution)/shard_map/load_block/pallas_call | solution.py:671
  6.6 0.4 %collective-permute-done.got_a = f32[200,128]{1,0:T(8,128)S(1)} collective-permute-done((f32[200,128]{1,0:T(8,128)S(1)}, f32[200,128]{1,0:T(8,128)S(1)}, u32[]{:S(2)}, u32[]{:S(2)}) %collective-permute-start) | collective-permute-done | bytes 102432 | tf_op jit(solution)/shard_map/ppermute | solution.py:42
  7.0 1.6 %collective-permute-done.1.got_b = f32[200,128]{1,0:T(8,128)S(1)} collective-permute-done((f32[200,128]{1,0:T(8,128)S(1)}, f32[200,128]{1,0:T(8,128)S(1)}, u32[]{:S(2)}, u32[]{:S(2)}) %collective-permute-start.1) | collective-permute-done | bytes 102432 | tf_op jit(solution)/shard_map/ppermute | solution.py:42
  8.6 0.2 %edge_planes.1 = (f32[448,128]{1,0:T(8,128)S(1)}, f32[448,128]{1,0:T(8,128)S(1)}, f32[3,18,88,128]{3,2,1,0:T(8,128)S(1)}, f32[6,18,88,128]{3,2,1,0:T(8,128)S(1)}, f32[4,88,128]{2,1,0:T(8,128)S(1)}) custom-call(f32[200,128]{1,0:T(8,128)S(1)} %collective-permute-done.got_a, ...), custom_call_target="tpu_custom_call", output_to_operand_aliasing={{2}: (4, {}), {3}: (5, {}), {4}: (7, {})} | custom-call | tf_op jit(solution)/shard_map/edge_planes/pallas_call | solution.py:682
  8.8 1.6 %collective-permute-start.2 = (f32[448,128]{1,0:T(8,128)S(1)}, f32[448,128]{1,0:T(8,128)S(1)}, u32[]{:S(2)}, u32[]{:S(2)}) collective-permute-start(f32[448,128]{1,0:T(8,128)S(1)} %get-tuple-element.29.own_b), channel_id=1, source_target_pairs={{0,16},{1,17},{2,18},{3,19},{4,8},{5,9},{6,10},{7,11},{8,4},{9,5},... | collective-permute-start | bytes 688136 | tf_op jit(solution)/shard_map/ppermute | solution.py:42
  10.4 0.1 collective-permute-start.3
  10.5 3.4 %both_steps.1 = (f32[3,18,88,128]{3,2,1,0:T(8,128)S(1)}, f32[6,18,88,128]{3,2,1,0:T(8,128)S(1)}, f32[3,16,72,128]{3,2,1,0:T(8,128)}, f32[6,16,72,128]{3,2,1,0:T(8,128)}) custom-call(f32[3,18,88,128]{3,2,1,0:T(8,128)S(1)} %get-tuple-element.32.v_in, f32[6,18,88,128]{3,2,1,0:T(8,128)S(1)} %get-tuple-element.33.s_in, ...), custom_call_target="tpu_custom_call", output_to_operand_aliasing={{0}: (0, {}), {1}: (1, {})} | custom-call | flops 8847360 | bytes 5308416 | tf_op jit(solution)/shard_map/both_steps/pallas_call | solution.py:694
  14.0 0.9 %collective-permute-done.2.next_b = f32[448,128]{1,0:T(8,128)S(1)} collective-permute-done((f32[448,128]{1,0:T(8,128)S(1)}, f32[448,128]{1,0:T(8,128)S(1)}, u32[]{:S(2)}, u32[]{:S(2)}) %collective-permute-start.2) | collective-permute-done | bytes 229408 | tf_op jit(solution)/shard_map/ppermute | solution.py:42
  14.9 0.0 collective-permute-done.3.next_a
  14.9 1.5 %join_neighbours.1 = (f32[3,16,72,128]{3,2,1,0:T(8,128)}, f32[6,16,72,128]{3,2,1,0:T(8,128)}) custom-call(f32[448,128]{1,0:T(8,128)S(1)} %collective-permute-done.2.next_b, f32[448,128]{1,0:T(8,128)S(1)} %collective-permute-done.3.next_a, f32[448,128]{1,0:T(8,128)S(1)} %get-tuple-element.30.own_a, ...), custom_call_target="tpu_custom_call", output_to_operand_aliasing={{0}: (7, {}), {1}: (8, {})} | custom-call | tf_op jit(solution)/shard_map/join_neighbours/pallas_call | solution.py:707
  (1 shorter events, 0.0 us)
Async XLA Ops:
  0.6 4.0 %copy-start = (f32[6,16,72,128]{3,2,1,0:T(8,128)S(1)}, f32[6,16,72,128]{3,2,1,0:T(8,128)}, u32[]{:S(2)}) copy-start(f32[6,16,72,128]{3,2,1,0:T(8,128)} %s_ref.3) | copy-start | bytes 10616836
  0.6 4.0 %copy-start.1 = (f32[3,16,72,128]{3,2,1,0:T(8,128)S(1)}, f32[3,16,72,128]{3,2,1,0:T(8,128)}, u32[]{:S(2)}) copy-start(f32[3,16,72,128]{3,2,1,0:T(8,128)} %v_ref.3) | copy-start | bytes 5308420
  0.7 4.0 %copy-start.2 = (s32[16]{0:T(128)S(1)}, s32[16]{0:T(128)}, u32[]{:S(2)}) copy-start(s32[16]{0:T(128)} %refs_0_.3) | copy-start | bytes 196
  0.7 4.0 %copy-start.3 = (s32[16]{0:T(128)S(1)}, s32[16]{0:T(128)}, u32[]{:S(2)}) copy-start(s32[16]{0:T(128)} %refs_1_.3) | copy-start | bytes 196
  0.7 4.0 %copy-start.4 = (s32[16]{0:T(128)S(1)}, s32[16]{0:T(128)}, u32[]{:S(2)}) copy-start(s32[16]{0:T(128)} %refs_2_.3) | copy-start | bytes 196
  0.7 4.0 %copy-start.5 = (f32[16]{0:T(128)S(1)}, f32[16]{0:T(128)}, u32[]{:S(2)}) copy-start(f32[16]{0:T(128)} %refs_3_.3) | copy-start | bytes 196
  2.3 4.7 %collective-permute-start = (f32[200,128]{1,0:T(8,128)S(1)}, f32[200,128]{1,0:T(8,128)S(1)}, u32[]{:S(2)}, u32[]{:S(2)}) collective-permute-start(f32[200,128]{1,0:T(8,128)S(1)} %get-tuple-element.22.edge_a), channel_id=1, source_target_pairs={{0,1},{1,0},{2,3},{3,2},{4,5},{5,4},{6,7},{7,6},{8,9},{9,8},{10,11... | collective-permute-start | bytes 307208 | tf_op jit(solution)/shard_map/ppermute | solution.py:42
  3.9 4.7 %collective-permute-start.1 = (f32[200,128]{1,0:T(8,128)S(1)}, f32[200,128]{1,0:T(8,128)S(1)}, u32[]{:S(2)}, u32[]{:S(2)}) collective-permute-start(f32[200,128]{1,0:T(8,128)S(1)} %get-tuple-element.21.edge_b), channel_id=1, source_target_pairs={{0,4},{1,2},{2,1},{3,7},{4,0},{5,6},{6,5},{7,3},{8,12},{9,10},{10,... | collective-permute-start | bytes 307208 | tf_op jit(solution)/shard_map/ppermute | solution.py:42
  8.8 6.1 %collective-permute-start.2 = (f32[448,128]{1,0:T(8,128)S(1)}, f32[448,128]{1,0:T(8,128)S(1)}, u32[]{:S(2)}, u32[]{:S(2)}) collective-permute-start(f32[448,128]{1,0:T(8,128)S(1)} %get-tuple-element.29.own_b), channel_id=1, source_target_pairs={{0,16},{1,17},{2,18},{3,19},{4,8},{5,9},{6,10},{7,11},{8,4},{9,5},... | collective-permute-start | bytes 688136 | tf_op jit(solution)/shard_map/ppermute | solution.py:42
  10.4 4.5 %collective-permute-start.3 = (f32[448,128]{1,0:T(8,128)S(1)}, f32[448,128]{1,0:T(8,128)S(1)}, u32[]{:S(2)}, u32[]{:S(2)}) collective-permute-start(f32[448,128]{1,0:T(8,128)S(1)} %get-tuple-element.30.own_a), channel_id=1, source_target_pairs={{0,4},{1,5},{2,6},{3,7},{4,0},{5,1},{6,2},{7,3},{8,12},{9,13},{10,... | collective-permute-start | bytes 688136 | tf_op jit(solution)/shard_map/ppermute | solution.py:42
